TPU v7x, 32 devices: a whole 2x2x4 slice. The times are simulated.
32 devices in a mesh: dp: 8 (over z, y), mp: 4 (over x, core).
Axes of the slice: x: 2, y: 2, z: 4, core: 2. Of those that a mesh axis runs over, the one named last changes fastest.
Arguments:
- tokens: bfloat16 [16384, 1024], P(('dp', 'mp')), may hold values from -6 to 6
- lengths: int32 [8, 8], P('dp'), may hold values from 0 to 2048, as said below
- norm1_gain: float32 [1024], replicated, may hold values from 0.5 to 1.5
- norm1_shift: float32 [1024], replicated, may hold values from -1.8 to 1.8
- query_weight: bfloat16 [1024, 1024], P(None, 'mp'), may hold values from -0.1875 to 0.1875
- query_bias: float32 [1024], P('mp'), may hold values from -1.8 to 1.8
- key_weight: bfloat16 [1024, 1024], P(None, 'mp'), may hold values from -0.1875 to 0.1875
- value_weight: bfloat16 [1024, 1024], P(None, 'mp'), may hold values from -0.1875 to 0.1875
- value_bias: float32 [1024], P('mp'), may hold values from -1.8 to 1.8
- head_scale: float32 [16], P('mp'), may hold values from 0.1 to 1.9
- output_weight: bfloat16 [1024, 1024], P('mp'), may hold values from -0.75 to 0.75
- output_bias: float32 [1024], replicated, may hold values from -1.8 to 1.8
- norm2_gain: float32 [1024], replicated, may hold values from 0.5 to 1.5
- norm2_shift: float32 [1024], replicated, may hold values from -1.8 to 1.8
- norm3_gain: float32 [1024], replicated, may hold values from 0.5 to 1.5
- norm3_shift: float32 [1024], replicated, may hold values from -1.8 to 1.8
- fc1_weight: bfloat16 [1024, 4096], P(None, 'mp'), may hold values from -0.1875 to 0.1875
- fc1_bias: float32 [4096], P('mp'), may hold values from -1.8 to 1.8
- mid_gain: float32 [4096], P('mp'), may hold values from 0.5 to 1.5
- mid_shift: float32 [4096], P('mp'), may hold values from -1.8 to 1.8
- fc2_weight: bfloat16 [4096, 1024], P('mp'), may hold values from -0.09375 to 0.09375
- fc2_bias: float32 [1024], replicated, may hold values from -1.8 to 1.8
- out_grad: bfloat16 [16384, 1024], P(('dp', 'mp')), may hold values from -6 to 6
Outputs:
- output: bfloat16 [16384, 1024], P(('dp', 'mp'))
- token_grad: float32 [16384, 1024], P(('dp', 'mp'))
- grad_norm1_gain: float32 [1024], replicated
- grad_norm1_shift: float32 [1024], replicated
- grad_query_weight: float32 [1024, 1024], P(None, 'mp')
- grad_query_bias: float32 [1024], P('mp')
- grad_key_weight: float32 [1024, 1024], P(None, 'mp')
- grad_value_weight: float32 [1024, 1024], P(None, 'mp')
- grad_value_bias: float32 [1024], P('mp')
- grad_head_scale: float32 [16], P('mp')
- grad_output_weight: float32 [1024, 1024], P('mp')
- grad_output_bias: float32 [1024], replicated
- grad_norm2_gain: float32 [1024], replicated
- grad_norm2_shift: float32 [1024], replicated
- grad_norm3_gain: float32 [1024], replicated
- grad_norm3_shift: float32 [1024], replicated
- grad_fc1_weight: float32 [1024, 4096], P(None, 'mp')
- grad_fc1_bias: float32 [4096], P('mp')
- grad_mid_gain: float32 [4096], P('mp')
- grad_mid_shift: float32 [4096], P('mp')
- grad_fc2_weight: float32 [4096, 1024], P('mp')
- grad_fc2_bias: float32 [1024], replicated
Inputs may be any that keep to these rules, and one draw needn't show every extreme that they name: Each row's 8 lengths sum to at most 2048; the rest of the row is padding. Some rows hold a single sequence of exactly 2048 tokens in every draw.
All inputs are finite; a program needn't handle non-finite values.
Results may differ from a plain program's by a relative error of at most 0.023.
Values may be sent and summed in bfloat16 or wider, within the bound.
No kernel may reach another device: no remote copies, remote signals or barrier semaphores. Data moves between devices by JAX's collectives and lax.ppermute only.
A program may use at most 192 MiB of HBM per device.

v0:
```python
import functools
import math

import jax
import jax.numpy as jnp
from jax import lax
from jax.experimental import pallas as pl
from jax.experimental.pallas import tpu as pltpu
from jax.sharding import PartitionSpec as P

HEAD_DIM = 64
FF = 4096
ROW = 2048
PAIR = 2 * HEAD_DIM
EPSILON = 1e-05
MASKED = -1000000000.0
LOG2E = math.log2(math.e)
SCORE_SCALE = LOG2E * HEAD_DIM**-0.5
SMEM_SPEC = pl.BlockSpec(memory_space=pltpu.SMEM)
VMEM_SPEC = pl.BlockSpec(memory_space=pltpu.VMEM)
BF16 = jnp.bfloat16
F32 = jnp.float32
PARAMS = pltpu.CompilerParams(vmem_limit_bytes=56 * 2**20)


def shape(dims, dtype):
    return jax.ShapeDtypeStruct(dims, dtype)


def cost(us):
    return pl.CostEstimate(flops=0, bytes_accessed=int(us * 1000), transcendentals=0)


def dot(a, b, ca=1, cb=0, precision=None):
    return lax.dot_general(
        a, b, (((ca,), (cb,)), ((), ())), preferred_element_type=F32, precision=precision
    )


def spread_heads(block, heads):
    lane = lax.broadcasted_iota(jnp.int32, (1, block.shape[1]), 1) // HEAD_DIM
    zero = jnp.zeros_like(block)
    return jnp.concatenate([jnp.where(lane == h, block, zero) for h in range(heads)], axis=0)


def seq_ends(len_ref):
    ends = []
    total = jnp.int32(0)
    for j in range(len_ref.shape[-1]):
        total = total + len_ref[0, j]
        ends.append(total)
    return ends


def start_of(ends, pos):
    first = jnp.zeros_like(pos)
    for e in ends:
        first = jnp.maximum(first, jnp.where(e <= pos, e, 0))
    return first


def query_positions(q0, tok, heads):
    lane = lax.broadcasted_iota(jnp.int32, (1, tok), 1) + q0
    return jnp.concatenate([lane] * heads, axis=1)


def hide(scores, k0, pos, first):
    key = lax.broadcasted_iota(jnp.int32, scores.shape, 0) + k0
    return jnp.where((key >= first) & (key <= pos), scores, MASKED)


def slot_rows(place, me, tok):
    return pl.ds(pl.multiple_of((place ^ me) * tok, tok), tok)


def fold_heads(side, heads, tok):
    return jnp.concatenate([side[:, h * tok : (h + 1) * tok] for h in range(heads)], axis=0).T


def key_range(ends, place, tok):
    begin = start_of(ends, place * tok) // tok
    whole = (start_of(ends, place * tok + tok - 1) + tok - 1) // tok
    return begin, jnp.minimum(whole, place)


def forward_kernel(tok, me_ref, len_ref, q_ref, k_ref, v_ref, scale_ref, *refs):
    nslot = ROW // tok
    width = q_ref.shape[1]
    heads = width // HEAD_DIM
    att_ref, lse_ref = refs[:2]
    mix_refs = refs[2 : 2 + nslot]
    vt_ref, mix_ref = refs[2 + nslot :]
    me = me_ref[0]
    ends = seq_ends(len_ref)

    @pl.loop(0, nslot)
    def _(b):
        rows = pl.ds(pl.multiple_of(b * tok, tok), tok)
        vt_ref[b] = v_ref[rows, :].astype(F32).T.astype(BF16)

    @pl.loop(0, nslot)
    def _(place):
        slot = place ^ me
        rows = slot_rows(place, me, tok)
        q4 = spread_heads(q_ref[rows, :], heads)
        pos = query_positions(place * tok, tok, heads)
        first = start_of(ends, pos)

        def tile(ki, state, masked):
            s = dot(k_ref[slot_rows(ki, me, tok), :], q4, 1, 1) * SCORE_SCALE
            if masked:
                s = hide(s, ki * tok, pos, first)
            top = jnp.max(s, 0, keepdims=True)
            vt = vt_ref[ki ^ me]
            if state is not None:
                m, l, acc = state
                top = jnp.maximum(top, m)
            p = jnp.exp2(s - top)
            add = jnp.sum(p, 0, keepdims=True)
            pb = p.astype(BF16)
            out = jnp.concatenate(
                [
                    dot(vt[h * HEAD_DIM : (h + 1) * HEAD_DIM], pb[:, h * tok : (h + 1) * tok])
                    for h in range(heads)
                ],
                axis=1,
            )
            if state is not None:
                fade = jnp.exp2(m - top)
                add = add + l * fade
                out = out + acc * fade
            return top, add, out

        begin, whole = key_range(ends, place, tok)
        state = tile(place, None, True)
        state = lax.fori_loop(begin, whole, lambda ki, st: tile(ki, st, True), state)
        m, l, acc = lax.fori_loop(
            jnp.maximum(whole, begin), place, lambda ki, st: tile(ki, st, False), state
        )
        o = fold_heads(acc / l, heads, tok)
        att_ref[rows, :] = o
        mix_ref[slot] = (o * scale_ref[...]).astype(BF16)
        lse_ref[slot] = m + jnp.log2(l)

    for s in range(nslot):
        mix_refs[s][...] = mix_ref[s]


def pair_blocks(qkv, pair):
    pairs = qkv.shape[1] // (3 * PAIR)
    return [pl.BlockSpec((ROW, PAIR), lambda t, c=j * pairs + pair: (0, c)) for j in range(3)]


def whole_spec(dims):
    return pl.BlockSpec(dims, lambda t: (0,) * len(dims))


def attend_forward(me, lengths, qkv, scale_lanes, tok, pair):
    nslot = ROW // tok
    lanes = PAIR // HEAD_DIM * tok
    made = [((ROW, PAIR), F32), ((nslot, 1, lanes), F32)] + [((tok, PAIR), BF16)] * nslot
    out = pl.pallas_call(
        functools.partial(forward_kernel, tok),
        grid=(1,),
        out_shape=[shape(*m) for m in made],
        in_specs=[SMEM_SPEC, SMEM_SPEC]
        + pair_blocks(qkv, pair)
        + [pl.BlockSpec((1, PAIR), lambda t: (0, pair))],
        out_specs=[whole_spec(m[0]) for m in made],
        scratch_shapes=[
            pltpu.VMEM((nslot, PAIR, tok), BF16),
            pltpu.VMEM((nslot, tok, PAIR), BF16),
        ],
        compiler_params=PARAMS,
        cost_estimate=cost(8),
        name="attend_forward",
    )(me, lengths, qkv, qkv, qkv, scale_lanes)
    return out[0], out[1], list(out[2:])


def end_of(ends, pos):
    last = jnp.full_like(pos, ROW)
    for e in ends:
        last = jnp.where(e > pos, jnp.minimum(last, e), last)
    return last


def backward_kernel(tok, turn, me_ref, len_ref, q_ref, k_ref, v_ref, att_ref, lse_ref, *refs):
    nslot = ROW // tok
    width = q_ref.shape[1]
    heads = width // HEAD_DIM
    do_refs = refs[:nslot]
    if turn == 0:
        dqkv_ref, sum_ref, dqt_ref = refs[nslot : nslot + 3]
    else:
        dqkv_in, sum_in, dqt_in, dqkv_ref, sum_ref, dqt_ref = refs[nslot : nslot + 6]
    do_ref, q4_ref, do4_ref, delta_ref = refs[-4:]
    me = me_ref[0]
    ends = seq_ends(len_ref)
    for s in range(nslot):
        do_ref[s] = do_refs[s][...]
    if turn == 0:
        sum_ref[...] = jnp.zeros_like(sum_ref)
        dqt_ref[...] = jnp.zeros_like(dqt_ref)
    else:
        sum_ref[...] = sum_in[...]
        dqt_ref[...] = dqt_in[...]
    pick = lax.broadcasted_iota(jnp.int32, (8, width), 1) // HEAD_DIM
    pick = (pick == lax.broadcasted_iota(jnp.int32, (8, width), 0)).astype(F32)

    @pl.loop(0, nslot)
    def _(place):
        rows = slot_rows(place, me, tok)
        q4_ref[place] = spread_heads(q_ref[rows, :], heads)
        do = do_ref[place ^ me]
        do4_ref[place] = spread_heads(do, heads)
        both = do.astype(F32) * att_ref[rows, :]
        if turn == 0:
            sum_ref[:, 3 * width :] += jnp.sum(both, 0, keepdims=True)
        d = dot(pick, both, 1, 1, lax.Precision.HIGHEST)
        delta_ref[place] = jnp.concatenate([d[h : h + 1] for h in range(heads)], axis=1)

    @pl.loop(0, nslot // 2)
    def _(j):
        ki = 4 * (j // 2) + (3 * (j % 2) if turn == 0 else 1 + j % 2)
        rows = slot_rows(ki, me, tok)
        k = k_ref[rows, :]
        v = v_ref[rows, :]
        kt = k.astype(F32).T.astype(BF16)

        def tile(qi, state, masked):
            q4 = q4_ref[qi]
            do4 = do4_ref[qi]
            s = dot(k, q4, 1, 1) * SCORE_SCALE
            if masked:
                pos = query_positions(qi * tok, tok, heads)
                s = hide(s, ki * tok, pos, start_of(ends, pos))
            p = jnp.exp2(s - lse_ref[qi ^ me])
            dp = dot(v, do4, 1, 1)
            ds = (p * (dp - delta_ref[qi])).astype(BF16)
            dv = dot(p.astype(BF16), do4)
            dk = dot(ds, q4)
            dqt_ref[qi] += jnp.concatenate(
                [
                    dot(kt[h * HEAD_DIM : (h + 1) * HEAD_DIM], ds[:, h * tok : (h + 1) * tok])
                    for h in range(heads)
                ],
                axis=1,
            )
            if state is None:
                return dk, dv
            return state[0] + dk, state[1] + dv

        state = tile(ki, None, True)
        k0 = ki * tok
        upto = (end_of(ends, k0 + tok - 1) + tok - 1) // tok
        whole = jnp.clip(end_of(ends, k0) // tok, ki + 1, jnp.maximum(upto, ki + 1))
        state = lax.fori_loop(ki + 1, whole, lambda qi, st: tile(qi, st, False), state)
        dk, dv = lax.fori_loop(whole, upto, lambda qi, st: tile(qi, st, True), state)
        dk = (dk * HEAD_DIM**-0.5).astype(BF16)
        dv = dv.astype(BF16)
        dqkv_ref[rows, width : 2 * width] = dk
        dqkv_ref[rows, 2 * width :] = dv
        sum_ref[:, width : 2 * width] += jnp.sum(dk.astype(F32), 0, keepdims=True)
        sum_ref[:, 2 * width : 3 * width] += jnp.sum(dv.astype(F32), 0, keepdims=True)

    if turn == 0:
        return

    @pl.loop(0, nslot // 2)
    def _(j):
        rows = slot_rows(4 * (j // 2) + 3 * (j % 2), me, tok)
        dqkv_ref[rows, width:] = dqkv_in[rows, width:]

    @pl.loop(0, nslot)
    def _(place):
        dq = (fold_heads(dqt_ref[place], heads, tok) * HEAD_DIM**-0.5).astype(BF16)
        dqkv_ref[slot_rows(place, me, tok), :width] = dq
        sum_ref[:, :width] += jnp.sum(dq.astype(F32), 0, keepdims=True)


def attend_backward(me, lengths, qkv, att, lse, grads, tok, pair, turn, held=()):
    nslot = ROW // tok
    lanes = PAIR // HEAD_DIM * tok
    made = [((ROW, 3 * PAIR), BF16), ((1, 4 * PAIR), F32), ((nslot, HEAD_DIM, lanes), F32)]
    return pl.pallas_call(
        functools.partial(backward_kernel, tok, turn),
        grid=(1,),
        out_shape=[shape(*m) for m in made],
        in_specs=[SMEM_SPEC, SMEM_SPEC]
        + pair_blocks(qkv, pair)
        + [whole_spec(att.shape), whole_spec(lse.shape)]
        + [pl.BlockSpec((tok, PAIR), lambda t: (0, pair))] * nslot
        + [whole_spec(v.shape) for v in held],
        out_specs=[whole_spec(m[0]) for m in made],
        scratch_shapes=[
            pltpu.VMEM((nslot, tok, PAIR), BF16),
            pltpu.VMEM((nslot, lanes, PAIR), BF16),
            pltpu.VMEM((nslot, lanes, PAIR), BF16),
            pltpu.VMEM((nslot, 1, lanes), F32),
        ],
        compiler_params=PARAMS,
        cost_estimate=cost(8),
        name="attend_backward",
    )(me, lengths, qkv, qkv, qkv, att, lse, *grads, *held)


def centred(v):
    center = v - jnp.mean(v, -1, keepdims=True)
    inv = lax.rsqrt(jnp.mean(center * center, -1, keepdims=True) + EPSILON)
    return center * inv, inv


def norm_back(unit, inv, e):
    return inv * (e - jnp.mean(e, -1, keepdims=True) - unit * jnp.mean(e * unit, -1, keepdims=True))


def first_norm_kernel(x_ref, gain_ref, shift_ref, out_ref):
    unit, _ = centred(x_ref[...].astype(F32))
    out_ref[...] = (unit * gain_ref[...] + shift_ref[...]).astype(BF16)


def first_norm(x, gain, shift):
    return pl.pallas_call(
        first_norm_kernel,
        out_shape=shape(x.shape, BF16),
        in_specs=[VMEM_SPEC] * 3,
        out_specs=VMEM_SPEC,
        compiler_params=PARAMS,
        cost_estimate=cost(2),
        name="first_norm",
    )(x, gain, shift)


def qkv_kernel(n, *refs):
    slots = refs[:n]
    weights = refs[n : n + 3]
    bias_ref = refs[n + 3]
    out_ref = refs[-1]
    tok = slots[0].shape[0]
    width = weights[0].shape[1]
    for s in range(n):
        for j in range(3):
            cols = slice(j * width, (j + 1) * width)
            made = dot(slots[s][...], weights[j][...]) + bias_ref[:, cols]
            out_ref[s * tok : (s + 1) * tok, cols] = made.astype(BF16)


def qkv_part(slots, weights, bias, part, earlier=None):
    n = len(slots)
    tok = slots[0].shape[0]
    width = weights[0].shape[1]
    args = [*slots, *weights, bias]
    specs = [VMEM_SPEC] * len(args)
    aliases = {}
    if earlier is not None:
        aliases = {len(args): 0}
        args.append(earlier)
        specs.append(pl.BlockSpec(memory_space=pl.ANY))
    return pl.pallas_call(
        functools.partial(qkv_kernel, n),
        grid=(1,),
        out_shape=shape((ROW, 3 * width), BF16),
        in_specs=specs,
        out_specs=pl.BlockSpec((n * tok, 3 * width), lambda t: (part, 0)),
        input_output_aliases=aliases,
        compiler_params=PARAMS,
        cost_estimate=cost(3),
        name="qkv_part",
    )(*args)


def join_lanes(refs):
    return jnp.concatenate([r[...] for r in refs], axis=1) if len(refs) > 1 else refs[0][...]


def after_attention_kernel(n, pairs, *refs):
    mixed = refs[: n * pairs]
    weights = refs[n * pairs : n * pairs + n]
    vectors = refs[n * pairs + n :]
    tok_ref, bias_ref, gain2_ref, shift2_ref, gain3_ref, shift3_ref = vectors[:6]
    branch_ref, residual_ref, ffn_ref = vectors[6:]
    branch = bias_ref[...]
    for s in range(n):
        branch = branch + dot(join_lanes(mixed[s * pairs : (s + 1) * pairs]), weights[s][...])
    branch_ref[...] = branch
    unit, _ = centred(branch)
    residual = tok_ref[...].astype(F32) + (unit * gain2_ref[...] + shift2_ref[...])
    residual_ref[...] = residual
    unit, _ = centred(residual)
    ffn_ref[...] = (unit * gain3_ref[...] + shift3_ref[...]).astype(BF16)


class Window:
    def __init__(self, array, first, rows):
        self.array, self.first, self.shape = array, first, (rows, array.shape[1])
        self.ndim = 2


def array_of(v):
    return v.array if isinstance(v, Window) else v


def row_tiles(rows, cols, tile):
    return pl.BlockSpec((tile, cols), lambda t: (t, 0))


def fixed(array):
    if isinstance(array, Window):
        at = array.first // array.shape[0]
        return pl.BlockSpec(array.shape, lambda *_: (at, 0))
    return pl.BlockSpec(array.shape, lambda *_: (0,) * array.ndim)


def after_attention(mixed, weights, tokens, *vectors, tile=128):
    rows, d = tokens.shape
    tile = min(tile, rows)
    n, pairs = len(mixed), len(mixed[0])
    mixed = [v for slot in mixed for v in slot]
    wide = row_tiles(rows, d, tile)
    return pl.pallas_call(
        functools.partial(after_attention_kernel, n, pairs),
        grid=(rows // tile,),
        in_specs=[row_tiles(rows, PAIR, tile)] * (n * pairs)
        + [fixed(w) for w in weights]
        + [wide]
        + [fixed(v) for v in vectors],
        out_specs=(wide, wide, wide),
        out_shape=(shape((rows, d), F32), shape((rows, d), F32), shape((rows, d), BF16)),
        compiler_params=PARAMS,
        cost_estimate=cost(3),
        name="after_attention",
    )(*mixed, *map(array_of, weights), tokens, *vectors)


def before_attention_kernel(n, adds, *refs):
    came = refs[:adds]
    residual_ref, branch_ref, cot_ref, gain3_ref, gain2_ref, scale_ref = refs[adds : adds + 6]
    weights = refs[adds + 6 : adds + 6 + n]
    outs = refs[adds + 6 + n :]
    grad_ref, low_ref, sum_ref = outs[:3]
    pieces = outs[3:]
    c = came[0][...].astype(F32)
    for r in came[1:]:
        c = c + r[...].astype(F32)
    unit3, inv3 = centred(residual_ref[...])
    cot = cot_ref[...].astype(F32)
    grad = cot + norm_back(unit3, inv3, c * gain3_ref[...])
    grad_ref[...] = grad
    unit2, inv2 = centred(branch_ref[...])
    low = norm_back(unit2, inv2, grad * gain2_ref[...]).astype(BF16)
    low_ref[...] = low

    @pl.when(pl.program_id(0) == 0)
    def _():
        sum_ref[...] = jnp.zeros_like(sum_ref)

    tops = [grad * unit2, grad, c * unit3, c, low.astype(F32), cot]
    sums = [jnp.sum(v, 0, keepdims=True) for v in tops]
    sum_ref[...] += jnp.concatenate(sums + [jnp.zeros_like(sums[0])] * 2, axis=0)
    width = pieces[0].shape[1]
    for s in range(n):
        made = dot(low, weights[s][...], 1, 1) * scale_ref[:, s * width : (s + 1) * width]
        pieces[s][...] = made.astype(BF16)


def before_attention(came, residual, branch, cot, gain3, gain2, scale_slots, weights, tile=128):
    rows, d = residual.shape
    width = weights[0].shape[0]
    tile = min(tile, rows)
    n = len(weights)
    wide = row_tiles(rows, d, tile)
    vectors = [gain3, gain2, scale_slots]
    out = pl.pallas_call(
        functools.partial(before_attention_kernel, n, len(came)),
        grid=(rows // tile,),
        in_specs=[wide] * (len(came) + 3)
        + [fixed(v) for v in vectors]
        + [fixed(w) for w in weights],
        out_specs=(wide, wide, pl.BlockSpec((8, d), lambda t: (0, 0)))
        + (row_tiles(rows, width, tile),) * n,
        out_shape=(shape((rows, d), F32), shape((rows, d), BF16), shape((8, d), F32))
        + (shape((rows, width), BF16),) * n,
        compiler_params=PARAMS,
        cost_estimate=cost(3),
        name="before_attention",
    )(*came, residual, branch, cot, *vectors, *map(array_of, weights))
    return out[0], out[1], out[2], list(out[3:])


def last_norm_kernel(adds, *refs):
    came = refs[:adds]
    x_ref, grad_ref, gain_ref, out_ref = refs[adds:]
    c = came[0][...].astype(F32)
    for r in came[1:]:
        c = c + r[...].astype(F32)
    unit, inv = centred(x_ref[...].astype(F32))
    out_ref[...] = grad_ref[...] + norm_back(unit, inv, c * gain_ref[...])


def last_norm(came, x, grad, gain, tile=128):
    rows, d = x.shape
    tile = min(tile, rows)
    wide = row_tiles(rows, d, tile)
    return pl.pallas_call(
        functools.partial(last_norm_kernel, len(came)),
        grid=(rows // tile,),
        in_specs=[wide] * (len(came) + 2) + [fixed(gain)],
        out_specs=wide,
        out_shape=shape((rows, d), F32),
        compiler_params=PARAMS,
        cost_estimate=cost(2),
        name="last_norm",
    )(*came, x, grad, gain)


def gelu_parts(u):
    k = math.sqrt(2 / math.pi)
    square = u * u
    t = jnp.tanh(u * (k + (k * 0.044715) * square))
    return 0.5 + 0.5 * t, t, square


def pick_piece(refs, places):
    step = pl.program_id(0)
    out = refs[0][...]
    for ref, (first, _, _) in zip(refs[1:], places[1:]):
        out = jnp.where(step >= first, ref[...], out)
    return out


def places_of(pieces, tile):
    places, at = [], 0
    for v in pieces:
        first = v.first // tile if isinstance(v, Window) else 0
        places.append((at, v.shape[0] // tile, first))
        at += v.shape[0] // tile
    return tuple(places)


def piece_tiles(places, tile, cols):
    return [
        pl.BlockSpec((tile, cols), lambda t, f=f, c=c, a=a: (jnp.clip(t - f, 0, c - 1) + a, 0))
        for f, c, a in places
    ]


def ffn_first_kernel(xp, cp, *refs):
    n = len(xp) + len(cp)
    w1_ref, b1_ref, gain_ref, w2_ref = refs[n : n + 4]
    u_ref, hg_ref, stat_ref = refs[n + 4 :]
    units = u_ref.shape[1]
    u = dot(pick_piece(refs[: len(xp)], xp), w1_ref[...]) + b1_ref[...]
    u_ref[...] = u
    half, _, _ = gelu_parts(u)
    a = u * half
    total = jnp.sum(a, 1, keepdims=True)
    d = a - total * (1.0 / units)
    hg = dot(pick_piece(refs[len(xp) : n], cp), w2_ref[...], 1, 1)
    hg_ref[...] = hg
    sg = hg * gain_ref[...]
    cols = [
        total,
        jnp.sum(d * d, 1, keepdims=True),
        jnp.sum(sg, 1, keepdims=True),
        jnp.sum(sg * d, 1, keepdims=True),
    ]
    lane = lax.broadcasted_iota(jnp.int32, (u.shape[0], 128), 1)
    wide = jnp.zeros(lane.shape, F32)
    for j, col in enumerate(cols):
        wide = jnp.where(lane == j, col, wide)
    stat_ref[...] = wide.T[:8]


def ffn_first(xs, cots, w1, b1, gain, w2, tile=256):
    d, units = w1.shape
    tile = min(tile, *(v.shape[0] for v in (*xs, *cots)))
    xp, cp = places_of(xs, tile), places_of(cots, tile)
    rows = sum(v.shape[0] for v in xs)
    return pl.pallas_call(
        functools.partial(ffn_first_kernel, xp, cp),
        grid=(rows // tile,),
        in_specs=piece_tiles(xp, tile, d)
        + piece_tiles(cp, tile, d)
        + [fixed(v) for v in (w1, b1, gain, w2)],
        out_specs=(
            row_tiles(rows, units, tile),
            row_tiles(rows, units, tile),
            pl.BlockSpec((8, tile), lambda t: (0, t)),
        ),
        out_shape=(shape((rows, units), F32), shape((rows, units), F32), shape((8, rows), F32)),
        compiler_params=PARAMS,
        cost_estimate=cost(5),
        name="ffn_first",
    )(*xs, *map(array_of, cots), w1, b1, gain, w2)


def ffn_second_kernel(ndev, n, per, *refs):
    u_ref, hg_ref, gain_ref, shift_ref, w1_ref = refs[:5]
    stats = [r[...] for r in refs[5 : 5 + ndev]]
    hid_ref, fg_ref, sum_ref = refs[-3 - n : -n]
    backs = refs[-n:]
    units = u_ref.shape[1]
    mean = sum(s[0:1] for s in stats) * (1.0 / FF)
    spread = jnp.zeros_like(mean)
    total = jnp.zeros_like(mean)
    cross = jnp.zeros_like(mean)
    for s in stats:
        gap = s[0:1] * (1.0 / units) - mean
        spread += s[1:2] + units * (gap * gap)
        total += s[2:3]
        cross += s[3:4] + gap * s[2:3]
    inv = lax.rsqrt(spread * (1.0 / FF) + EPSILON)
    packed = [mean, inv, total * (1.0 / FF), cross * inv * (1.0 / FF)]
    packed = jnp.concatenate(packed + [jnp.zeros_like(mean)] * 4, axis=0).T
    mean, inv, total, cross = (packed[:, j : j + 1] for j in range(4))
    u = u_ref[...]
    hg = hg_ref[...]
    half, t, square = gelu_parts(u)
    unit = (u * half - mean) * inv
    gain = gain_ref[...]
    hid_ref[...] = (unit * gain + shift_ref[...]).astype(BF16)
    k = math.sqrt(2 / math.pi)
    slope = half + (0.5 * u) * ((1.0 - t * t) * (k + (3 * k * 0.044715) * square))
    fg = (inv * (hg * gain - total - unit * cross) * slope).astype(BF16)
    fg_ref[...] = fg
    back = dot(fg, w1_ref[...], 1, 1).astype(BF16)
    step = pl.program_id(0) // per
    for s in range(n):

        @pl.when(step == s)
        def _(s=s):
            backs[s][...] = back

    @pl.when(pl.program_id(0) == 0)
    def _():
        sum_ref[...] = jnp.zeros_like(sum_ref)

    sums = [jnp.sum(v, 0, keepdims=True) for v in (hg * unit, hg, fg.astype(F32))]
    sum_ref[...] += jnp.concatenate(sums + [jnp.zeros((5, units), F32)], axis=0)


def ffn_second(u, hg, gain, shift, w1, stats, tok, part, earlier=None, tile=256):
    rows, units = u.shape
    d = w1.shape[0]
    tile = min(tile, tok)
    per = tok // tile
    ndev = len(stats)
    n = rows // tok
    skip = part * n * per

    def stat_place(s):
        return lambda t: (0, (((t + skip) // per) ^ s) * per + t % per)

    in_specs = [row_tiles(rows, units, tile)] * 2 + [fixed(v) for v in (gain, shift, w1)]
    in_specs += [pl.BlockSpec((8, tile), stat_place(s)) for s in range(ndev)]
    args = [u, hg, gain, shift, w1, *stats]
    aliases = {}
    if earlier is not None:
        in_specs += [pl.BlockSpec(memory_space=pl.ANY)] * 2
        aliases = {len(args): 0, len(args) + 1: 1}
        args += list(earlier)
    moved = pl.BlockSpec((tile, units), lambda t: (t + skip, 0))
    out = pl.pallas_call(
        functools.partial(ffn_second_kernel, ndev, n, per),
        grid=(rows // tile,),
        in_specs=in_specs,
        out_specs=(moved, moved, pl.BlockSpec((8, units), lambda t: (0, 0)))
        + tuple(piece_tiles([(s * per, per, 0) for s in range(n)], tile, d)),
        out_shape=(shape((ROW, units), BF16), shape((ROW, units), BF16), shape((8, units), F32))
        + (shape((tok, d), BF16),) * n,
        input_output_aliases=aliases,
        compiler_params=PARAMS,
        cost_estimate=cost(5),
        name="ffn_second",
    )(*args)
    return out[0], out[1], out[2], list(out[3:])


def products_kernel(nx, nw, flip, groups, *refs):
    xs, ws, outs = refs[:nx], refs[nx : nx + nw], refs[nx + nw :]
    cols = xs[0].shape[1] // nw
    tok = xs[0].shape[0] // sum(len(g) for g in groups)
    for group, out in zip(groups, outs):
        for at, s in enumerate(group):
            total = None
            for j, w in enumerate(ws):
                left = [x[s * tok : (s + 1) * tok, j * cols : (j + 1) * cols] for x in xs]
                left = jnp.concatenate(left, axis=1) if nx > 1 else left[0]
                made = dot(left, w[...], 1, 1 if flip else 0)
                total = made if total is None else total + made
            out[at * tok : (at + 1) * tok, :] = total.astype(BF16)


def products(xs, weights, flip, tok, first, groups):
    n = sum(len(g) for g in groups)
    d = weights[0].shape[0 if flip else 1]
    out = pl.pallas_call(
        functools.partial(products_kernel, len(xs), len(weights), flip, groups),
        grid=(1,),
        in_specs=[pl.BlockSpec((n * tok, x.shape[1]), lambda t: (first // n, 0)) for x in xs]
        + [fixed(w) for w in weights],
        out_specs=[whole_spec((len(g) * tok, d)) for g in groups],
        out_shape=[shape((len(g) * tok, d), BF16) for g in groups],
        compiler_params=PARAMS,
        cost_estimate=cost(2),
        name="products",
    )(*xs, *weights)
    return list(out)


def head_gradient_kernel(n, pairs, groups, *refs):
    left = refs[n * pairs][...]
    d = left.shape[1]
    for group, out in zip(groups, refs[n * pairs + 1 :]):
        for at, s in enumerate(group):
            made = dot(left, join_lanes(refs[s * pairs : (s + 1) * pairs]), 0, 0)
            out[at * d : (at + 1) * d, :] = made.astype(BF16)


def head_gradient(mixed, low, groups):
    n, pairs = len(mixed), len(mixed[0])
    d = low.shape[1]
    mixed = [v for slot in mixed for v in slot]
    return list(
        pl.pallas_call(
            functools.partial(head_gradient_kernel, n, pairs, groups),
            out_shape=[shape((len(g) * d, pairs * PAIR), BF16) for g in groups],
            in_specs=[VMEM_SPEC] * (n * pairs + 1),
            out_specs=[VMEM_SPEC] * len(groups),
            compiler_params=PARAMS,
            cost_estimate=cost(2),
            name="head_gradient",
        )(*mixed, low)
    )


def gradient_kernel(steps, nl, nr, nj, extra, me_ref, *refs):
    del me_ref
    joins, refs = refs[:nj], refs[nj:]
    lefts, rights = refs[:nl], refs[nl : nl + nr]
    send_ref, keep_ref = refs[nl + nr + extra : nl + nr + extra + 2]
    step = pl.program_id(0)
    pieces = rights if nr > 1 else lefts
    total = None
    at = 0
    for s, piece in enumerate(pieces):
        rows = slice(at, at + piece.shape[0])
        at += piece.shape[0]
        left = lefts[s][...] if nl > 1 else lefts[0][rows, :]
        right = rights[s][...] if nr > 1 else rights[0][rows, :]
        made = dot(left, right, 0, 0)
        total = made if total is None else total + made

    made = total.astype(BF16)
    if nj:
        more = joins[0][...].astype(F32)
        for r in joins[1:]:
            more = more + r[...].astype(F32)
        made = jnp.concatenate([made, more.astype(BF16)], axis=1)

    @pl.when(step < steps // 2)
    def _():
        send_ref[...] = made

    @pl.when(step >= steps // 2)
    def _():
        keep_ref[...] = made

    if extra:
        weights = refs[nl + nr : nl + nr + extra - 1]
        sum_ref = refs[nl + nr + extra - 1]
        width = weights[0].shape[1]
        cross = jnp.zeros((total.shape[0], width), F32)
        plain = cross
        for j, w_ref in enumerate(weights):
            cols = slice(j * width, (j + 1) * width)
            w = w_ref[...].astype(F32)
            cross += w * total[:, cols]
            plain += w * sum_ref[:, cols]
        cross = jnp.sum(cross, 1, keepdims=True)
        plain = jnp.sum(plain, 1, keepdims=True)
        lane = lax.broadcasted_iota(jnp.int32, (total.shape[0], 128), 1)
        wide = jnp.where(lane == 0, cross, jnp.where(lane == 1, plain, 0.0))
        refs[-1][...] = wide.T[:8]


def gradient(side, lefts, rights, weights=(), pair=0, sums=None, joins=(), steps=4):
    m = lefts[0].shape[1]
    steps = min(steps, m // 128)
    size = m // steps
    n = rights[0].shape[1]
    nl, nr = len(lefts), len(rights)
    n += joins[0].shape[1] if joins else 0
    extra = len(weights) + 1 if weights else 0

    def chunk_of(t, side):
        return (t + (1 - side[0]) * (steps // 2)) % steps

    def join_spec(v):
        at = v.first // size if isinstance(v, Window) else 0
        return pl.BlockSpec((size, v.shape[1]), lambda t, me: (chunk_of(t, me) + at, 0))

    in_specs = [join_spec(v) for v in joins]
    in_specs += [pl.BlockSpec((v.shape[0], size), lambda t, me: (0, chunk_of(t, me))) for v in lefts]
    in_specs += [fixed(v) for v in rights]
    in_specs += [pl.BlockSpec((size, PAIR), lambda t, me: (chunk_of(t, me), pair)) for w in weights]
    out_specs = [
        pl.BlockSpec((size, n), lambda t, me: (jnp.minimum(t, steps // 2 - 1), 0)),
        pl.BlockSpec((size, n), lambda t, me: (jnp.maximum(t - steps // 2, 0), 0)),
    ]
    out_shape = [shape((m // 2, n), BF16)] * 2
    args = [side, *map(array_of, joins), *lefts, *map(array_of, rights), *weights]
    if extra:
        args.append(sums)
        in_specs.append(pl.BlockSpec(sums.shape, lambda t, me: (0, 0)))
        out_specs.append(pl.BlockSpec((8, size), lambda t, me: (0, chunk_of(t, me))))
        out_shape.append(shape((8, m), F32))
    return pl.pallas_call(
        functools.partial(gradient_kernel, steps, nl, nr, len(joins), extra),
        grid_spec=pltpu.PrefetchScalarGridSpec(
            num_scalar_prefetch=1, grid=(steps,), in_specs=in_specs, out_specs=out_specs
        ),
        out_shape=out_shape,
        compiler_params=PARAMS,
        cost_estimate=cost(4),
        name="gradient",
    )(*args)


def assemble_kernel(nx, cols, turned, side_ref, *refs):
    mine, came, outs = refs[:nx], refs[nx : 2 * nx], refs[2 * nx :]
    size = mine[0].shape[0]
    side = side_ref[0]
    n = len(outs) - (1 if turned else 0)
    for x in range(nx):
        for ref, first in ((mine[x], side * size), (came[x], (1 - side) * size)):
            first = pl.multiple_of(first, size)
            for j in range(n):
                made = ref[:, j * cols : (j + 1) * cols].astype(F32)
                outs[j][pl.ds(first, size), x * cols : (x + 1) * cols] = made
            if x == 0 and turned:
                outs[n][:, pl.ds(first, size)] = ref[:, n * cols :].astype(F32).T


def assemble(side, mine, came, cols, turned=0):
    size = mine[0].shape[0]
    n = (mine[0].shape[1] - turned) // cols
    out = [shape((2 * size, cols * len(mine)), F32)] * n
    if turned:
        out = out + [shape((turned, 2 * size), F32)]
    return pl.pallas_call(
        functools.partial(assemble_kernel, len(mine), cols, turned),
        out_shape=out,
        in_specs=[SMEM_SPEC] + [VMEM_SPEC] * (2 * len(mine)),
        out_specs=[VMEM_SPEC] * len(out),
        compiler_params=PARAMS,
        cost_estimate=cost(2),
        name="assemble",
    )(side, *mine, *came)


def swap(value, axis, size, bit):
    return lax.ppermute(value, axis, [(i, i ^ bit) for i in range(size)])


def bits_of(size):
    return [1 << b for b in range(size.bit_length() - 1)]


def after(value, *others):
    return lax.optimization_barrier((value, *others))[0]


def spread_low(slots, axis, size, bits):
    slots = dict(slots)
    for bit in bits:
        slots.update({s | bit: swap(v, axis, size, bit) for s, v in slots.items()})
    return slots


def add_low(left, right):
    return (left.astype(F32) + right.astype(F32)).astype(BF16)


def direct_slots(value, axis, size):
    return [value] + [swap(value, axis, size, s) for s in range(1, size)]


class Scatter:
    def __init__(self, size):
        self.size = size
        self.low = bits_of(size)[:-1]
        self.top = size // 2

    def within(self, parts):
        held = {s: [v] for s, v in parts.items()}
        for bit in self.low:
            for s in sorted(held, reverse=True):
                if s & bit:
                    terms = held.pop(s)
                    total = terms[0]
                    for t in terms[1:]:
                        total = add_low(total, t)
                    held[s ^ bit].append(swap(total, "mp", self.size, bit))
        [(_, terms)] = held.items()
        return terms

    def across(self, terms):
        total = terms[0].astype(F32)
        for t in terms[1:]:
            total = total + t.astype(F32)
        total = total.astype(BF16)
        return total, swap(total, "mp", self.size, self.top)


class Stream:
    def __init__(self, dp, bits, send, keep):
        self.dp = dp
        self.index = lax.axis_index("dp")
        self.bits = bits
        self.stage = 0
        self.held = keep
        self.came = swap(send, "dp", dp, bits[0])

    def advance(self, *tie):
        n = len(self.bits)
        if self.stage == 2 * n - 1:
            return self.held
        held, came = after(self.held, *tie), after(self.came, *tie)
        self.stage += 1
        if self.stage <= n:
            cur = add_low(held, came)
            if self.stage == n:
                self.held = send = cur
                bit = self.bits[-1]
            else:
                bit = self.bits[self.stage]
                upper = (self.index & bit) != 0
                low, high = cur[: cur.shape[0] // 2], cur[cur.shape[0] // 2 :]
                send = jnp.where(upper, low, high)
                self.held = jnp.where(upper, high, low)
        else:
            upper = (self.index & self.bits[2 * n - self.stage]) != 0
            low, high = jnp.where(upper, came, held), jnp.where(upper, held, came)
            self.held = send = jnp.concatenate([low, high])
            bit = self.bits[2 * n - self.stage - 1]
        self.came = swap(send, "dp", self.dp, bit)
        return send

    def done(self, *tie):
        while self.stage < 2 * len(self.bits) - 1:
            self.advance(*tie)
        return self


class Direct:
    def __init__(self, dp, send, keep):
        self.dp = dp
        self.index = lax.axis_index("dp")
        self.held = keep
        self.came = swap(send, "dp", dp, 1)
        self.stage = 0

    def others(self, parts):
        return [parts[0]] + [swap(v, "dp", self.dp, 2 * j) for j, v in enumerate(parts) if j]

    def ordered(self, parts):
        bit = 2
        step = 1
        while step < len(parts):
            upper = (self.index & bit) != 0
            parts = [jnp.where(upper, parts[j ^ step], v) for j, v in enumerate(parts)]
            bit, step = 2 * bit, 2 * step
        return parts

    def advance(self, *tie):
        n = self.dp // 2
        self.stage += 1
        if self.stage == 1:
            total = add_low(after(self.held, *tie), after(self.came, *tie))
            size = total.shape[0] // n
            parts = self.ordered([total[j * size : (j + 1) * size] for j in range(n)])
            self.parts = self.others(parts)
            return parts[0]
        if self.stage == 2:
            total = sum(after(v, *tie).astype(F32) for v in self.parts).astype(BF16)
            self.parts = self.others([total] * n)
            return total
        if self.stage == 3:
            parts = [after(v, *tie) for v in self.parts]
            self.held = jnp.concatenate(self.ordered(parts))
            self.came = swap(self.held, "dp", self.dp, 1)
        return self.held

    def done(self, *tie):
        while self.stage < 3:
            self.advance(*tie)
        return self


def on_device(
    dp,
    mp,
    tokens,
    lengths,
    norm1_gain,
    norm1_shift,
    query_weight,
    query_bias,
    key_weight,
    value_weight,
    value_bias,
    head_scale,
    output_weight,
    output_bias,
    norm2_gain,
    norm2_shift,
    norm3_gain,
    norm3_shift,
    fc1_weight,
    fc1_bias,
    mid_gain,
    mid_shift,
    fc2_weight,
    fc2_bias,
    out_grad,
):
    tok, d = tokens.shape
    width = query_weight.shape[1]
    heads = width // HEAD_DIM
    pairs = width // PAIR
    half = mp // 2
    units = fc1_weight.shape[1]
    me = lax.axis_index("mp").astype(jnp.int32)
    me_arr = me[None]
    index = lax.axis_index("dp").astype(jnp.int32)
    plain = bits_of(dp)
    turned = [plain[1], plain[0], *plain[2:]]
    side, side_turned = (index & 1)[None], ((index >> 1) & 1)[None]
    lower = list(reversed(bits_of(mp)[:-1]))
    scatter = Scatter(mp)
    one_by_one = [[s] for s in range(half)]
    merged = [[0], [2], [1, 3]] if mp == 4 else [[s] for s in range(mp)]

    def merged_terms(outs, rows):
        if mp != 4:
            return scatter.within(dict(enumerate(outs[:half]))), scatter.within(
                {half + j: v for j, v in enumerate(outs[half:])}
            )
        came = swap(outs[2], "mp", mp, 1)
        return [outs[0], Window(came, 0, rows)], [outs[1], Window(came, rows, rows)]

    def plain_rows(v):
        return v.array[v.first : v.first + v.shape[0]] if isinstance(v, Window) else v

    def wide_swap(v):
        return swap(v, "mp", mp, half)

    def listed(near, far):
        slots = {**near, **far}
        return [slots[s] for s in range(mp)]

    def row(v):
        return v[None]

    qkv_weights = (query_weight, key_weight, value_weight)
    bias_qkv = jnp.concatenate([query_bias, jnp.zeros_like(query_bias), value_bias])[None]
    scale_lanes = jnp.repeat(head_scale, HEAD_DIM)[None]
    place = me * tok + lax.broadcasted_iota(jnp.int32, (tok, 1), 0)
    cot_low = jnp.where(place < jnp.sum(lengths), out_grad, jnp.zeros_like(out_grad))

    normed_own = first_norm(tokens, row(norm1_gain), row(norm1_shift))
    normed_far = wide_swap(normed_own)
    normed_near = spread_low({0: normed_own}, "mp", mp, lower)
    start = normed_near[half - 1]
    qkv = qkv_part([normed_near[s] for s in range(half)], qkv_weights, bias_qkv, 0)
    cot_low, output_weight = (after(v, start) for v in (cot_low, output_weight))
    cot_near = spread_low({0: cot_low}, "mp", mp, lower)
    out_near = spread_low({0: output_weight}, "mp", mp, lower)
    both = jnp.concatenate([cot_low, output_weight])
    normed_far = after(normed_far, qkv, both, cot_near[half - 1], out_near[half - 1])
    both_far = wide_swap(after(both, normed_far))
    normed_far = spread_low({half: normed_far}, "mp", mp, lower)
    qkv = qkv_part([normed_far[half + s] for s in range(half)], qkv_weights, bias_qkv, 1, qkv)
    normed = listed(normed_near, normed_far)

    far_first = [*range(half, mp), *range(1, half)]
    atts, lses, mixed = [], [], [[] for _ in range(mp)]
    mark = (qkv,)
    for p in range(pairs):
        att, lse, mix = attend_forward(me_arr, lengths, after(qkv, *mark), scale_lanes, tok, p)
        atts.append(att)
        lses.append(lse)
        if p > 0:
            mix = [after(v, *(m[-1] for m in mixed[1:])) for v in mix]
        mixed[0].append(mix[0])
        for s in far_first:
            mixed[s].append(swap(mix[s], "mp", mp, s))
        mark = (mix[0],)
    both_far = spread_low({half: after(both_far, mix[0])}, "mp", mp, lower)
    cot_far = {s: Window(v, 0, tok) for s, v in both_far.items()}
    out_far = {s: Window(v, tok, width) for s, v in both_far.items()}
    out_rows = listed(out_near, out_far)
    branch, residual, ffn_own = after_attention(
        mixed,
        out_rows,
        tokens,
        *(row(v) for v in (output_bias, norm2_gain, norm2_shift, norm3_gain, norm3_shift)),
    )

    ffn_far = wide_swap(ffn_own)
    ffn_near = spread_low({0: ffn_own}, "mp", mp, lower)
    scale_slots = direct_slots(after(scale_lanes, ffn_own), "mp", mp)
    ffn_args = (fc1_weight, row(fc1_bias), row(mid_gain), fc2_weight)
    u_near, hg_near, st_near = ffn_first(
        [ffn_near[s] for s in range(half)], [cot_near[s] for s in range(half)], *ffn_args
    )
    ffn_far = spread_low({half: after(ffn_far, st_near)}, "mp", mp, lower)
    ffn_args = (fc1_weight, after(row(fc1_bias), *scale_slots[1:]), row(mid_gain), fc2_weight)
    cots = listed(cot_near, cot_far)
    ffn_in = listed(ffn_near, ffn_far)
    u_far, hg_far, st_far = ffn_first(ffn_in[half:], cots[half:], *ffn_args)
    stats = direct_slots(jnp.concatenate([st_near, st_far], axis=1), "mp", mp)
    ffn_args = (row(mid_gain), row(mid_shift), fc1_weight, stats, tok)
    hid, fg, mid_far, back_far = ffn_second(u_far, hg_far, *ffn_args, 1)
    back_far = scatter.within({half + j: v for j, v in enumerate(back_far)})
    hid, fg, mid_near, back_near = ffn_second(u_near, hg_near, *ffn_args, 0, (hid, fg))
    scale_slots = jnp.concatenate(scale_slots, axis=1)
    back_far[1:] = [after(v, mid_near) for v in back_far[1:]]
    back_sum, back_far = scatter.across(back_far)
    back_near = scatter.within(dict(enumerate(back_near)))

    send, keep = gradient(side, [after(hid, back_sum)], cots)
    fc2 = Stream(dp, plain, send, keep)
    send, keep = gradient(side_turned, ffn_in, [after(fg, send)])
    fc1 = Stream(dp, turned, send, keep)
    hid = after(hid, send)
    out_near_terms, out_far_terms = merged_terms(
        products([hid], [fc2_weight], False, tok, 0, merged), tok
    )
    came = [after(v, *(t for t in out_far_terms if not isinstance(t, Window))) for v in (*back_near, back_far)]
    residual_grad, branch_low, sums, grads = before_attention(
        came, residual, branch, cot_low, row(norm3_gain), row(norm2_gain), scale_slots, out_rows
    )

    do = {s: swap(grads[s], "mp", mp, s) for s in far_first}
    do = [grads[0]] + [do[s] for s in range(1, mp)]
    mark = fc1.advance(branch_low)
    mark = fc2.advance(mark)
    low = after(branch_low, mark, *do[1:half])
    g_near_terms, g_far_terms = merged_terms(head_gradient(mixed, low, merged), d)
    g_out_sum, g_out_top = scatter.across([plain_rows(v) for v in g_far_terms])
    out_far_terms = [after(plain_rows(v), g_out_sum) for v in out_far_terms]
    out_sum, out_top = scatter.across(out_far_terms)
    mark = after(out_sum, *do[1:])
    mark = fc2.advance(mark)
    mark = fc1.advance(mark)

    dqkvs, sums_att, rows, streams = [], [], [], []

    def between(call):
        nonlocal mark
        if call == 0:
            mark = fc2.advance(mark)
        elif call == 1:
            mark = fc1.advance(after(mark, g_out_top))
            mark = fc2.advance(mark)
        elif call == 2:
            mark = fc1.advance(mark)
            mark = fc2.advance(mark)
            for stream in streams:
                mark = stream.advance(mark)

    call = 0
    for p in range(pairs):
        held = ()
        for turn in range(2):
            held = attend_backward(
                me_arr, lengths, after(qkv, mark), atts[p], lses[p], do, tok, p, turn, held
            )
            mark = held[0]
            between(call)
            call += 1
        dqkv, sum_att, _ = held
        dqkvs.append(dqkv)
        sums_att.append(sum_att)
        if p < pairs - 1:
            joins = [*g_near_terms, g_out_top] if p == 0 else ()
            send, keep, r = gradient(
                side, normed, [after(dqkv, mark)], qkv_weights, p, sum_att, joins
            )
            rows.append(r)
            streams.append(Stream(dp, plain, send, keep))
            mark = send

    mark = after(mark, out_top)
    mark = fc1.advance(mark)
    for stream in streams:
        mark = stream.advance(mark)
    joins = [*g_near_terms, g_out_top] if pairs == 1 else ()
    send, keep, r = gradient(
        side, normed, [after(dqkvs[-1], mark)], qkv_weights, pairs - 1, sums_att[-1], joins
    )
    rows.append(r)
    last = Direct(dp, send, keep)
    far = products(
        [after(v, send) for v in dqkvs], qkv_weights, True, tok, half, one_by_one
    )
    far_terms = scatter.within({half + j: v for j, v in enumerate(far)})
    packed = jnp.concatenate([sums[:6], sum(rows)[:2]])
    packed = jnp.broadcast_to(after(packed, far[0])[None], (mp, *packed.shape))
    packed = lax.all_to_all(packed, "mp", 0, 0)
    near = products([after(v, far[0]) for v in dqkvs], qkv_weights, True, tok, 0, one_by_one)
    far_terms[1:] = [after(v, near[0]) for v in far_terms[1:]]
    far_sum, far_top = scatter.across(far_terms)
    near_terms = scatter.within(dict(enumerate(near)))
    fc2.done(far_sum)
    [grad_fc2_weight] = assemble(side, [after(fc2.held, far_sum)], [fc2.came], fc2.held.shape[1])
    for stream in streams:
        mark = stream.advance(grad_fc2_weight)
    mark = last.advance(mark)
    packed = after(packed, mark).sum(0)
    mids = jnp.pad(mid_near + mid_far, ((0, 0), (0, d - units)))[:4]
    heads_sums = jnp.concatenate(sums_att, axis=1)
    heads_sums = jnp.pad(heads_sums, ((0, 3), (0, d - heads_sums.shape[1])))
    packed = jnp.concatenate([packed, mids, heads_sums])
    packed = jnp.broadcast_to(packed[None], (dp, *packed.shape))
    sent = packed
    packed = lax.all_to_all(packed, "dp", 0, 0)
    fc1.done(sent)
    [grad_fc1_weight] = assemble(
        side_turned, [after(fc1.held, sent)], [fc1.came], fc1.held.shape[1]
    )
    for stream in streams:
        mark = stream.advance(grad_fc1_weight)
    mark = last.advance(mark)
    for stream in streams:
        mark = stream.advance(mark)
    token_grad = last_norm(
        [*near_terms, after(far_top, mark)], tokens, residual_grad, row(norm1_gain)
    )
    mark = last.advance(token_grad)
    output = residual + row(fc2_bias)
    for t in (*out_near_terms, out_top):
        output = output + after(plain_rows(t), mark).astype(F32)
    output = output.astype(BF16)
    packed = after(packed, mark).sum(0)
    streams.append(last)
    for stream in streams:
        stream.done(mark)
    grad_query_weight, grad_key_weight, grad_value_weight, grad_output_weight = assemble(
        side, [v.held for v in streams], [v.came for v in streams], PAIR, width
    )
    shift1 = packed[7]
    gain1 = (packed[6] - norm1_shift * shift1) / norm1_gain
    per_head = packed[12, : 4 * width].reshape(pairs, 4, PAIR)
    return (
        output,
        token_grad,
        gain1,
        shift1,
        grad_query_weight,
        per_head[:, 0].reshape(width),
        grad_key_weight,
        grad_value_weight,
        per_head[:, 2].reshape(width),
        jnp.sum(per_head[:, 3].reshape(heads, HEAD_DIM), 1) / head_scale,
        grad_output_weight,
        packed[4],
        packed[0],
        packed[1],
        packed[2],
        packed[3],
        grad_fc1_weight,
        packed[10, :units],
        packed[8, :units],
        packed[9, :units],
        grad_fc2_weight,
        packed[5],
    )


def solution(mesh):
    own = P(("dp", "mp"), None)
    cols, rows, vec, same = P(None, "mp"), P("mp", None), P("mp"), P()
    ends = (cols, vec, vec, vec, rows, same)
    norms = (same,) * 5
    in_specs = (own, P("dp", None), same, same, cols, vec, cols, cols, vec, vec, rows, *norms, *ends, own)
    out_specs = (own, own, same, same, cols, vec, cols, cols, vec, vec, rows, *norms, *ends)
    return jax.shard_map(
        functools.partial(on_device, mesh.shape["dp"], mesh.shape["mp"]),
        mesh=mesh,
        in_specs=in_specs,
        out_specs=out_specs,
        check_vma=False,
    )
```

profile of v0, /device:TPU:0, one launch (start us, length us, event | category | flops | bytes accessed | tf_op | source)
XLA Modules:
  0.0 426.3 jit_solution(7976984230985633403)
XLA Ops:
  0.7 3.0 first_norm.1.refs_0_.refs_3_
  4.2 2.5 collective-permute-start
  10.6 5.0 %qkv_part.2.refs_6_ = bf16[2048,768]{1,0:T(8,128)(2,1)} custom-call(bf16[512,1024]{1,0:T(8,128)(2,1)} %first_norm.1.refs_0_.refs_3_, bf16[512,1024]{1,0:T(8,128)(2,1)} %copy-done.4, bf16[1024,256]{1,0:T(8,128)(2,1)} %refs_2_.7, bf16[1024,256]{1,0:T(8,128)(2,1)} %refs_3_.8, bf16[1024,256]{1,0:T(8,128)(2,1)} %refs_4_.15, f32[1,768]{1,0:T(1,128)} %broadcast_in_dim.82.refs_5_), custom_call_target="tpu_custom_call" | custom-call | bytes 3000 | tf_op jit(solution)/shard_map/qkv_part/pallas_call | solution.py:360
  17.4 13.3 %collective-permute-done.refs_0_.refs_5_.refs_2_ = bf16[512,1024]{1,0:T(8,128)(2,1)S(1)} collective-permute-done((bf16[512,1024]{1,0:T(8,128)(2,1)}, bf16[512,1024]{1,0:T(8,128)(2,1)S(1)}, u32[]{:S(2)}, u32[]{:S(2)}) %collective-permute-start) | collective-permute-done | bytes 1048608 | tf_op jit(solution)/shard_map/ppermute | solution.py:864
  37.1 4.9 %qkv_part.3.q_ref.k_ref.v_ref = bf16[2048,768]{1,0:T(8,128)(2,1)} custom-call(bf16[512,1024]{1,0:T(8,128)(2,1)} %copy-done.3, bf16[512,1024]{1,0:T(8,128)(2,1)} %collective-permute-done.4.refs_1_.refs_6_.refs_3_, bf16[1024,256]{1,0:T(8,128)(2,1)} %refs_2_.7, bf16[1024,256]{1,0:T(8,128)(2,1)} %refs_3_.8, ...), custom_call_target="tpu_custom_call", output_to_operand_aliasing={{}: (6, {})} | custom-call | bytes 3000 | tf_op jit(solution)/shard_map/qkv_part/pallas_call | solution.py:360
  42.1 14.2 %attend_forward.2 = (f32[2048,128]{1,0:T(8,128)}, f32[4,1,1024]{2,1,0:T(1,128)}, bf16[512,128]{1,0:T(8,128)(2,1)}, bf16[512,128]{1,0:T(8,128)(2,1)}, bf16[512,128]{1,0:T(8,128)(2,1)}, /*index=5*/bf16[512,128]{1,0:T(8,128)(2,1)}) custom-call(s32[1]{0:T(128)} %bitcast.me_ref, s32[1,8]{1,0:T(1,128)} %len_ref.11, bf16[2048,768]{1,0:T(8,128)(2,1)} %qkv_part.3.q_ref.k_ref.v_ref, ...), custom_call_target="tpu_custom_call" | custom-call | bytes 8000 | tf_op jit(solution)/shard_map/attend_forward/pallas_call | solution.py:162
  58.2 14.0 %attend_forward.3 = (f32[2048,128]{1,0:T(8,128)}, f32[4,1,1024]{2,1,0:T(1,128)}, bf16[512,128]{1,0:T(8,128)(2,1)}, bf16[512,128]{1,0:T(8,128)(2,1)}, bf16[512,128]{1,0:T(8,128)(2,1)}, /*index=5*/bf16[512,128]{1,0:T(8,128)(2,1)}) custom-call(s32[1]{0:T(128)} %bitcast.me_ref, s32[1,8]{1,0:T(1,128)} %len_ref.11, bf16[2048,768]{1,0:T(8,128)(2,1)} %qkv_part.3.q_ref.k_ref.v_ref, ...), custom_call_target="tpu_custom_call" | custom-call | bytes 8000 | tf_op jit(solution)/shard_map/attend_forward/pallas_call | solution.py:162
  76.4 3.9 collective-permute-done.10.refs_7_
  80.3 3.1 collective-permute-done.9.refs_5_
  84.6 6.5 %after_attention.1 = (f32[512,1024]{1,0:T(8,128)}, f32[512,1024]{1,0:T(8,128)}, bf16[512,1024]{1,0:T(8,128)(2,1)}) custom-call(bf16[512,128]{1,0:T(8,128)(2,1)} %get-tuple-element.185.refs_0_, bf16[512,128]{1,0:T(8,128)(2,1)} %get-tuple-element.191.refs_1_, bf16[512,128]{1,0:T(8,128)(2,1)} %copy-done.29, bf16[512,128]{1,0:T(8,128)(2,1)} %copy-done.34, ...), custom_call_target="tpu_custom_call" | custom-call | bytes 3000 | tf_op jit(solution)/shard_map/after_attention/pallas_call | solution.py:421
  95.0 10.5 %ffn_first.2 = (f32[1024,1024]{1,0:T(8,128)}, f32[1024,1024]{1,0:T(8,128)}, f32[8,1024]{1,0:T(8,128)}) custom-call(bf16[512,1024]{1,0:T(8,128)(2,1)} %get-tuple-element.201.refs_0_, bf16[512,1024]{1,0:T(8,128)(2,1)} %copy-done.8, bf16[512,1024]{1,0:T(8,128)(2,1)} %copy-done, bf16[512,1024]{1,0:T(8,128)(2,1)} %copy-done.7, bf16[1024,1024]{1,0:T(8,128)(2,1)} %refs_4_.13, ...), custom_call_target="tpu_custom_call" | custom-call | bytes 5000 | tf_op jit(solution)/shard_map/ffn_first/pallas_call | solution.py:580
  105.6 11.4 %collective-permute-done.14.refs_0_.refs_2_ = bf16[512,1024]{1,0:T(8,128)(2,1)S(1)} collective-permute-done((bf16[512,1024]{1,0:T(8,128)(2,1)}, bf16[512,1024]{1,0:T(8,128)(2,1)S(1)}, u32[]{:S(2)}, u32[]{:S(2)}) %collective-permute-start.14) | collective-permute-done | bytes 1048608 | tf_op jit(solution)/shard_map/ppermute | solution.py:864
  123.8 10.5 %ffn_first.3 = (f32[1024,1024]{1,0:T(8,128)}, f32[1024,1024]{1,0:T(8,128)}, f32[8,1024]{1,0:T(8,128)}) custom-call(bf16[512,1024]{1,0:T(8,128)(2,1)} %copy-done.14, bf16[512,1024]{1,0:T(8,128)(2,1)} %copy-done.15, bf16[768,1024]{1,0:T(8,128)(2,1)} %copy-done.1, bf16[768,1024]{1,0:T(8,128)(2,1)} %copy-done.2, bf16[1024,1024]{1,0:T(8,128)(2,1)} %refs_4_.13, ...), custom_call_target="tpu_custom_call" | custom-call | bytes 5000 | tf_op jit(solution)/shard_map/ffn_first/pallas_call | solution.py:580
  137.0 3.1 collective-permute-done.20.refs_7_
  141.2 12.2 %ffn_second.2 = (bf16[2048,1024]{1,0:T(8,128)(2,1)}, bf16[2048,1024]{1,0:T(8,128)(2,1)}, f32[8,1024]{1,0:T(8,128)}, bf16[512,1024]{1,0:T(8,128)(2,1)}, bf16[512,1024]{1,0:T(8,128)(2,1)}) custom-call(f32[1024,1024]{1,0:T(8,128)} %get-tuple-element.209.refs_0_, f32[1024,1024]{1,0:T(8,128)} %get-tuple-element.210.refs_1_, f32[1,1024]{1,0:T(1,128)} %bitcast.30, ...), custom_call_target="tpu_custom_call" | custom-call | bytes 5000 | tf_op jit(solution)/shard_map/ffn_second/pallas_call | solution.py:664
  153.7 11.8 %ffn_second.3 = (bf16[2048,1024]{1,0:T(8,128)(2,1)}, bf16[2048,1024]{1,0:T(8,128)(2,1)}, f32[8,1024]{1,0:T(8,128)}, bf16[512,1024]{1,0:T(8,128)(2,1)}, bf16[512,1024]{1,0:T(8,128)(2,1)}) custom-call(f32[1024,1024]{1,0:T(8,128)} %get-tuple-element.202.refs_0_, ...), custom_call_target="tpu_custom_call", output_to_operand_aliasing={{0}: (9, {}), {1}: (10, {})} | custom-call | bytes 5000 | tf_op jit(solution)/shard_map/ffn_second/pallas_call | solution.py:664
  168.0 9.0 %gradient.4 = (bf16[512,1024]{1,0:T(8,128)(2,1)}, bf16[512,1024]{1,0:T(8,128)(2,1)}) custom-call(s32[1]{0:T(128)} %bitcast.12.me_ref.side_ref, bf16[2048,1024]{1,0:T(8,128)(2,1)} %get-tuple-element.223.refs_0_, bf16[512,1024]{1,0:T(8,128)(2,1)} %copy-done, bf16[512,1024]{1,0:T(8,128)(2,1)} %copy-done.7, bf16[768,1024]{1,0:T(8,128)(2,1)} %copy-done.1, ...), custom_call_target="tpu_custom_call" | custom-call | bytes 4000 | tf_op jit(solution)/shard_map/gradient/pallas_call | solution.py:819
  176.9 9.2 %gradient.5 = (bf16[512,1024]{1,0:T(8,128)(2,1)}, bf16[512,1024]{1,0:T(8,128)(2,1)}) custom-call(s32[1]{0:T(128)} %bitcast.11.me_ref.side_ref, bf16[512,1024]{1,0:T(8,128)(2,1)} %get-tuple-element.201.refs_0_, bf16[512,1024]{1,0:T(8,128)(2,1)} %copy-done.8, bf16[512,1024]{1,0:T(8,128)(2,1)} %copy-done.14, bf16[512,1024]{1,0:T(8,128)(2,1)} %copy-done.15, ...), custom_call_target="tpu_custom_call" | custom-call | bytes 4000 | tf_op jit(solution)/shard_map/gradient/pallas_call | solution.py:819
  189.2 8.7 %products.3 = (bf16[512,1024]{1,0:T(8,128)(2,1)}, bf16[512,1024]{1,0:T(8,128)(2,1)}, bf16[1024,1024]{1,0:T(8,128)(2,1)}) custom-call(bf16[2048,1024]{1,0:T(8,128)(2,1)} %get-tuple-element.223.refs_0_, bf16[1024,1024]{1,0:T(8,128)(2,1)} %refs_1_.1), custom_call_target="tpu_custom_call" | custom-call | bytes 2000 | tf_op jit(solution)/shard_map/products/pallas_call | solution.py:698
  199.5 10.6 %before_attention.1 = (f32[512,1024]{1,0:T(8,128)}, bf16[512,1024]{1,0:T(8,128)(2,1)}, f32[8,1024]{1,0:T(8,128)}, bf16[512,256]{1,0:T(8,128)(2,1)}, bf16[512,256...) custom-call(bf16[512,1024]{1,0:T(8,128)(2,1)} %get-tuple-element.227.refs_0_, ...), custom_call_target="tpu_custom_call" | custom-call | bytes 3000 | tf_op jit(solution)/shard_map/before_attention/pallas_call | solution.py:474
  214.7 4.0 head_gradient.1
  227.0 4.7 %collective-permute-done.31.refs_2_ = bf16[512,256]{1,0:T(8,128)(2,1)S(1)} collective-permute-done((bf16[512,256]{1,0:T(8,128)(2,1)}, bf16[512,256]{1,0:T(8,128)(2,1)S(1)}, u32[]{:S(2)}, u32[]{:S(2)}) %collective-permute-start.31) | collective-permute-done | bytes 262176 | tf_op jit(solution)/shard_map/ppermute | solution.py:864
  231.7 4.6 %collective-permute-done.32.refs_3_ = bf16[512,256]{1,0:T(8,128)(2,1)S(1)} collective-permute-done((bf16[512,256]{1,0:T(8,128)(2,1)}, bf16[512,256]{1,0:T(8,128)(2,1)S(1)}, u32[]{:S(2)}, u32[]{:S(2)}) %collective-permute-start.32) | collective-permute-done | bytes 262176 | tf_op jit(solution)/shard_map/ppermute | solution.py:864
  236.6 2.7 collective-permute-start.35
  240.0 13.2 %attend_backward.4 = (bf16[2048,384]{1,0:T(8,128)(2,1)}, f32[1,512]{1,0:T(1,128)}, f32[4,64,1024]{2,1,0:T(8,128)}) custom-call(s32[1]{0:T(128)} %bitcast.me_ref, s32[1,8]{1,0:T(1,128)} %len_ref.11, bf16[2048,768]{1,0:T(8,128)(2,1)} %qkv_part.3.q_ref.k_ref.v_ref, bf16[2048,768]{1,0:T(8,128)(2,1)} %qkv_part.3.q_ref.k_ref.v_ref, ...), custom_call_target="tpu_custom_call" | custom-call | bytes 8000 | tf_op jit(solution)/shard_map/attend_backward/pallas_call | solution.py:286
  253.1 4.6 %collective-permute-done.35 = bf16[128,1024]{1,0:T(8,128)(2,1)S(1)} collective-permute-done((bf16[128,1024]{1,0:T(8,128)(2,1)S(1)}, bf16[128,1024]{1,0:T(8,128)(2,1)S(1)}, u32[]{:S(2)}, u32[]{:S(2)}) %collective-permute-start.35) | collective-permute-done | bytes 262176 | tf_op jit(solution)/shard_map/ppermute | solution.py:864
  257.9 15.1 %attend_backward.5 = (bf16[2048,384]{1,0:T(8,128)(2,1)}, f32[1,512]{1,0:T(1,128)}, f32[4,64,1024]{2,1,0:T(8,128)}) custom-call(s32[1]{0:T(128)} %bitcast.me_ref, s32[1,8]{1,0:T(1,128)} %len_ref.11, bf16[2048,768]{1,0:T(8,128)(2,1)} %qkv_part.3.q_ref.k_ref.v_ref, bf16[2048,768]{1,0:T(8,128)(2,1)} %qkv_part.3.q_ref.k_ref.v_ref, ...), custom_call_target="tpu_custom_call" | custom-call | bytes 8000 | tf_op jit(solution)/shard_map/attend_backward/pallas_call | solution.py:286
  275.8 7.4 %gradient.6 = (bf16[512,640]{1,0:T(8,128)(2,1)}, bf16[512,640]{1,0:T(8,128)(2,1)}, f32[8,1024]{1,0:T(8,128)}) custom-call(s32[1]{0:T(128)} %bitcast.12.me_ref.side_ref, bf16[1024,256]{1,0:T(8,128)(2,1)} %get-tuple-element.241.refs_0_, bf16[2048,256]{1,0:T(8,128)(2,1)} %copy-done.16, bf16[1024,256]{1,0:T(8,128)(2,1)} %collective-permute-done.29.refs_2_, ...), custom_call_target="tpu_custom_call" | custom-call | bytes 4000 | tf_op jit(solution)/shard_map/gradient/pallas_call | solution.py:819
  283.8 13.2 %attend_backward.6 = (bf16[2048,384]{1,0:T(8,128)(2,1)}, f32[1,512]{1,0:T(1,128)}, f32[4,64,1024]{2,1,0:T(8,128)}) custom-call(s32[1]{0:T(128)} %bitcast.me_ref, s32[1,8]{1,0:T(1,128)} %len_ref.11, bf16[2048,768]{1,0:T(8,128)(2,1)} %qkv_part.3.q_ref.k_ref.v_ref, bf16[2048,768]{1,0:T(8,128)(2,1)} %qkv_part.3.q_ref.k_ref.v_ref, ...), custom_call_target="tpu_custom_call" | custom-call | bytes 8000 | tf_op jit(solution)/shard_map/attend_backward/pallas_call | solution.py:286
  297.3 3.5 collective-permute-done.40
  301.0 2.4 collective-permute-start.43
  303.4 15.1 %attend_backward.7 = (bf16[2048,384]{1,0:T(8,128)(2,1)}, f32[1,512]{1,0:T(1,128)}, f32[4,64,1024]{2,1,0:T(8,128)}) custom-call(s32[1]{0:T(128)} %bitcast.me_ref, s32[1,8]{1,0:T(1,128)} %len_ref.11, bf16[2048,768]{1,0:T(8,128)(2,1)} %qkv_part.3.q_ref.k_ref.v_ref, bf16[2048,768]{1,0:T(8,128)(2,1)} %qkv_part.3.q_ref.k_ref.v_ref, ...), custom_call_target="tpu_custom_call" | custom-call | bytes 8000 | tf_op jit(solution)/shard_map/attend_backward/pallas_call | solution.py:286
  321.5 6.8 %gradient.7 = (bf16[512,384]{1,0:T(8,128)(2,1)}, bf16[512,384]{1,0:T(8,128)(2,1)}, f32[8,1024]{1,0:T(8,128)}) custom-call(s32[1]{0:T(128)} %bitcast.12.me_ref.side_ref, bf16[512,1024]{1,0:T(8,128)(2,1)} %first_norm.1.refs_0_.refs_3_, bf16[512,1024]{1,0:T(8,128)(2,1)} %copy-done.4, bf16[512,1024]{1,0:T(8,128)(2,1)} %copy-done.3, ...), custom_call_target="tpu_custom_call" | custom-call | bytes 4000 | tf_op jit(solution)/shard_map/gradient/pallas_call | solution.py:819
  328.3 4.7 %products.4 = (bf16[512,1024]{1,0:T(8,128)(2,1)}, bf16[512,1024]{1,0:T(8,128)(2,1)}) custom-call(bf16[2048,384]{1,0:T(8,128)(2,1)} %get-tuple-element.301.refs_7_.refs_0_, bf16[2048,384]{1,0:T(8,128)(2,1)} %get-tuple-element.302.refs_4_.refs_1_, bf16[1024,256]{1,0:T(8,128)(2,1)} %refs_2_.7, bf16[1024,256]{1,0:T(8,128)(2,1)} %refs_3_.8, ...), custom_call_target="tpu_custom_call" | custom-call | bytes 2000 | tf_op jit(solution)/shard_map/products/pallas_call | solution.py:698
  338.0 3.3 all-to-all-start
  341.3 4.7 %products.5 = (bf16[512,1024]{1,0:T(8,128)(2,1)}, bf16[512,1024]{1,0:T(8,128)(2,1)}) custom-call(bf16[2048,384]{1,0:T(8,128)(2,1)} %get-tuple-element.301.refs_7_.refs_0_, bf16[2048,384]{1,0:T(8,128)(2,1)} %get-tuple-element.302.refs_4_.refs_1_, bf16[1024,256]{1,0:T(8,128)(2,1)} %refs_2_.7, bf16[1024,256]{1,0:T(8,128)(2,1)} %refs_3_.8, ...), custom_call_target="tpu_custom_call" | custom-call | bytes 2000 | tf_op jit(solution)/shard_map/products/pallas_call | solution.py:698
  346.5 2.6 add_convert_fusion.1
  349.1 9.9 %collective-permute-done.45.refs_1_ = bf16[512,1024]{1,0:T(8,128)(2,1)} collective-permute-done((bf16[512,1024]{1,0:T(8,128)(2,1)S(1)}, bf16[512,1024]{1,0:T(8,128)(2,1)}, u32[]{:S(2)}, u32[]{:S(2)}) %collective-permute-start.45) | collective-permute-done | bytes 1048608 | tf_op jit(solution)/shard_map/ppermute | solution.py:864
  360.3 3.8 assemble.3
  369.1 3.8 assemble.4
  374.3 3.0 collective-permute-start.52
  378.6 4.4 %all-to-all-start.1 = ((f32[8,16,1024]{2,1,0:T(8,128)}), f32[8,16,1024]{2,1,0:T(8,128)}, u32[]{:S(2)}, u32[]{:S(2)}) async-start(f32[8,16,1024]{2,1,0:T(8,128)} %broadcast_in_dim.97), calls=%async_computation.1 | async-start | bytes 1048576 | tf_op jit(solution)/shard_map/all_to_all | solution.py:1230
  385.2 2.3 collective-permute-start.57
  387.6 9.4 %collective-permute-done.56 = bf16[256,640]{1,0:T(8,128)(2,1)S(1)} collective-permute-done((bf16[256,640]{1,0:T(8,128)(2,1)S(1)}, bf16[256,640]{1,0:T(8,128)(2,1)S(1)}, u32[]{:S(2)}, u32[]{:S(2)}) %collective-permute-start.56) | collective-permute-done | bytes 327712 | tf_op jit(solution)/shard_map/ppermute | solution.py:864
  399.4 5.4 %last_norm.1 = f32[512,1024]{1,0:T(8,128)} custom-call(bf16[512,1024]{1,0:T(8,128)(2,1)} %get-tuple-element.303.refs_0_, bf16[512,1024]{1,0:T(8,128)(2,1)} %collective-permute-done.54.refs_1_, bf16[512,1024]{1,0:T(8,128)(2,1)} %collective-permute-done.55.refs_2_, bf16[512,1024]{1,0:T(8,128)(2,1)} %refs_3_.9, f32[512,1024]{1,0:T(8,128)} %get-tuple-element.327.refs_4_, ...), custom_call_target="tpu_custom_call" | custom-call | bytes 2000 | tf_op jit(solution)/shard_map/last_norm/pallas_call | solution.py:505
  413.1 3.3 add_convert_fusion
  417.3 4.7 %collective-permute-done.60.refs_3_ = bf16[512,384]{1,0:T(8,128)(2,1)} collective-permute-done((bf16[512,384]{1,0:T(8,128)(2,1)S(1)}, bf16[512,384]{1,0:T(8,128)(2,1)}, u32[]{:S(2)}, u32[]{:S(2)}) %collective-permute-start.60) | collective-permute-done | bytes 393248 | tf_op jit(solution)/shard_map/ppermute | solution.py:864
  422.0 3.8 assemble.5
  (281 shorter events, 90.6 us)
Async XLA Ops:
  4.2 26.5 %collective-permute-start = (bf16[512,1024]{1,0:T(8,128)(2,1)}, bf16[512,1024]{1,0:T(8,128)(2,1)S(1)}, u32[]{:S(2)}, u32[]{:S(2)}) collective-permute-start(bf16[512,1024]{1,0:T(8,128)(2,1)} %first_norm.1.refs_0_.refs_3_), channel_id=1, source_target_pairs={{0,2},{1,3},{2,0},{3,1},{4,6},{5,7},{6,4},{7,5},{8,10},{9,11},{10,... | collective-permute-start | bytes 3145736 | tf_op jit(solution)/shard_map/ppermute | solution.py:864
  9.4 22.2 %collective-permute-start.2 = (bf16[512,1024]{1,0:T(8,128)(2,1)S(1)}, bf16[512,1024]{1,0:T(8,128)(2,1)S(1)}, u32[]{:S(2)}, u32[]{:S(2)}) collective-permute-start(bf16[512,1024]{1,0:T(8,128)(2,1)S(1)} %broadcast_select_fusion.refs_2_.refs_1_.refs_5_), channel_id=1, source_target_pairs={{0,1},{1,0},{2,3},{3,2},{4,5},{5,4},{6,7},{7,6},{8,9},{9,8},{10,11... | collective-permute-start | bytes 3145736 | tf_op jit(solution)/shard_map/ppermute | solution.py:864
  9.7 21.0 %collective-permute-start.3 = (bf16[256,1024]{1,0:T(8,128)(2,1)S(1)}, bf16[256,1024]{1,0:T(8,128)(2,1)S(1)}, u32[]{:S(2)}, u32[]{:S(2)}) collective-permute-start(bf16[256,1024]{1,0:T(8,128)(2,1)S(1)} %copy-done.6), channel_id=1, source_target_pairs={{0,1},{1,0},{2,3},{3,2},{4,5},{5,4},{6,7},{7,6},{8,9},{9,8},{10,11... | collective-permute-start | bytes 1572872 | tf_op jit(solution)/shard_map/ppermute | solution.py:864
  32.6 41.2 %collective-permute-start.11 = (bf16[768,1024]{1,0:T(8,128)(2,1)}, bf16[768,1024]{1,0:T(8,128)(2,1)S(1)}, u32[]{:S(2)}, u32[]{:S(2)}) collective-permute-start(bf16[768,1024]{1,0:T(8,128)(2,1)} %constant_dynamic-update-slice_fusion), channel_id=1, source_target_pairs={{0,2},{1,3},{2,0},{3,1},{4,6},{5,7},{6,4},{7,5},{8,10},{9,11},{10,... | collective-permute-start | bytes 4718600 | tf_op jit(solution)/shard_map/ppermute | solution.py:864
  56.3 15.9 %collective-permute-start.5 = (bf16[512,128]{1,0:T(8,128)(2,1)}, bf16[512,128]{1,0:T(8,128)(2,1)S(1)}, u32[]{:S(2)}, u32[]{:S(2)}) collective-permute-start(bf16[512,128]{1,0:T(8,128)(2,1)} %get-tuple-element.188), channel_id=1, source_target_pairs={{0,1},{1,0},{2,3},{3,2},{4,5},{5,4},{6,7},{7,6},{8,9},{9,8},{10,11... | collective-permute-start | bytes 393224 | tf_op jit(solution)/shard_map/ppermute | solution.py:864
  56.5 16.4 %collective-permute-start.6 = (bf16[512,128]{1,0:T(8,128)(2,1)}, bf16[512,128]{1,0:T(8,128)(2,1)S(1)}, u32[]{:S(2)}, u32[]{:S(2)}) collective-permute-start(bf16[512,128]{1,0:T(8,128)(2,1)} %get-tuple-element.189), channel_id=1, source_target_pairs={{0,2},{1,3},{2,0},{3,1},{4,6},{5,7},{6,4},{7,5},{8,10},{9,11},{10,... | collective-permute-start | bytes 393224 | tf_op jit(solution)/shard_map/ppermute | solution.py:864
  56.8 17.0 %collective-permute-start.7 = (bf16[512,128]{1,0:T(8,128)(2,1)}, bf16[512,128]{1,0:T(8,128)(2,1)S(1)}, u32[]{:S(2)}, u32[]{:S(2)}) collective-permute-start(bf16[512,128]{1,0:T(8,128)(2,1)} %get-tuple-element.190), channel_id=1, source_target_pairs={{0,3},{1,2},{2,1},{3,0},{4,7},{5,6},{6,5},{7,4},{8,11},{9,10},{10,... | collective-permute-start | bytes 393224 | tf_op jit(solution)/shard_map/ppermute | solution.py:864
  73.8 9.5 %collective-permute-start.12 = (bf16[768,1024]{1,0:T(8,128)(2,1)S(1)}, bf16[768,1024]{1,0:T(8,128)(2,1)S(1)}, u32[]{:S(2)}, u32[]{:S(2)}) collective-permute-start(bf16[768,1024]{1,0:T(8,128)(2,1)S(1)} %collective-permute-done.11.refs_10_.refs_2_.refs_3_.refs_11_), channel_id=1, source_target_pairs={{0,1},{1,0},{2,3},{3,2},{4,5},{5,4},{6,7},{7,6},{8,9},{9,8},{10,11... | collective-permute-start | bytes 4718600 | tf_op jit(solution)/shard_map/ppermute | solution.py:864
  75.8 7.6 %collective-permute-start.9 = (bf16[512,128]{1,0:T(8,128)(2,1)}, bf16[512,128]{1,0:T(8,128)(2,1)S(1)}, u32[]{:S(2)}, u32[]{:S(2)}) collective-permute-start(bf16[512,128]{1,0:T(8,128)(2,1)} %get-tuple-element.195), channel_id=1, source_target_pairs={{0,2},{1,3},{2,0},{3,1},{4,6},{5,7},{6,4},{7,5},{8,10},{9,11},{10,... | collective-permute-start | bytes 393224 | tf_op jit(solution)/shard_map/ppermute | solution.py:864
  91.2 25.8 %collective-permute-start.14 = (bf16[512,1024]{1,0:T(8,128)(2,1)}, bf16[512,1024]{1,0:T(8,128)(2,1)S(1)}, u32[]{:S(2)}, u32[]{:S(2)}) collective-permute-start(bf16[512,1024]{1,0:T(8,128)(2,1)} %get-tuple-element.201.refs_0_), channel_id=1, source_target_pairs={{0,2},{1,3},{2,0},{3,1},{4,6},{5,7},{6,4},{7,5},{8,10},{9,11},{10,... | collective-permute-start | bytes 3145736 | tf_op jit(solution)/shard_map/ppermute | solution.py:864
  153.3 12.5 %collective-permute-start.22 = (bf16[512,1024]{1,0:T(8,128)(2,1)}, bf16[512,1024]{1,0:T(8,128)(2,1)S(1)}, u32[]{:S(2)}, u32[]{:S(2)}) collective-permute-start(bf16[512,1024]{1,0:T(8,128)(2,1)} %get-tuple-element.216), channel_id=1, source_target_pairs={{0,1},{1,0},{2,3},{3,2},{4,5},{5,4},{6,7},{7,6},{8,9},{9,8},{10,11... | collective-permute-start | bytes 3145736 | tf_op jit(solution)/shard_map/ppermute | solution.py:864
  165.5 33.0 %collective-permute-start.23 = (bf16[512,1024]{1,0:T(8,128)(2,1)}, bf16[512,1024]{1,0:T(8,128)(2,1)S(1)}, u32[]{:S(2)}, u32[]{:S(2)}) collective-permute-start(bf16[512,1024]{1,0:T(8,128)(2,1)} %get-tuple-element.228), channel_id=1, source_target_pairs={{0,1},{1,0},{2,3},{3,2},{4,5},{5,4},{6,7},{7,6},{8,9},{9,8},{10,11... | collective-permute-start | bytes 3145736 | tf_op jit(solution)/shard_map/ppermute | solution.py:864
  167.2 31.3 %collective-permute-start.24 = (bf16[512,1024]{1,0:T(8,128)(2,1)}, bf16[512,1024]{1,0:T(8,128)(2,1)}, u32[]{:S(2)}, u32[]{:S(2)}) collective-permute-start(bf16[512,1024]{1,0:T(8,128)(2,1)} %add_convert_fusion.5), channel_id=1, source_target_pairs={{0,2},{1,3},{2,0},{3,1},{4,6},{5,7},{6,4},{7,5},{8,10},{9,11},{10,... | collective-permute-start | bytes 3145736 | tf_op jit(solution)/shard_map/ppermute | solution.py:864
  186.1 25.2 %collective-permute-start.25 = (bf16[512,1024]{1,0:T(8,128)(2,1)}, bf16[512,1024]{1,0:T(8,128)(2,1)}, u32[]{:S(2)}, u32[]{:S(2)}) collective-permute-start(bf16[512,1024]{1,0:T(8,128)(2,1)} %get-tuple-element.222), channel_id=1, source_target_pairs={{0,8},{4,12},{8,0},{12,4},{16,24},{20,28},{24,16},{28,20},{1,9},{5... | collective-permute-start | bytes 3145736 | tf_op jit(solution)/shard_map/ppermute | solution.py:864
  187.7 25.4 %collective-permute-start.26 = (bf16[512,1024]{1,0:T(8,128)(2,1)}, bf16[512,1024]{1,0:T(8,128)(2,1)S(1)}, u32[]{:S(2)}, u32[]{:S(2)}) collective-permute-start(bf16[512,1024]{1,0:T(8,128)(2,1)} %get-tuple-element.220), channel_id=1, source_target_pairs={{0,4},{4,0},{8,12},{12,8},{16,20},{20,16},{24,28},{28,24},{1,5},{5... | collective-permute-start | bytes 3145736 | tf_op jit(solution)/shard_map/ppermute | solution.py:864
  197.9 25.8 %collective-permute-start.30 = (bf16[1024,1024]{1,0:T(8,128)(2,1)}, bf16[1024,1024]{1,0:T(8,128)(2,1)}, u32[]{:S(2)}, u32[]{:S(2)}) collective-permute-start(bf16[1024,1024]{1,0:T(8,128)(2,1)} %get-tuple-element.245), channel_id=1, source_target_pairs={{0,1},{1,0},{2,3},{3,2},{4,5},{5,4},{6,7},{7,6},{8,9},{9,8},{10,11... | collective-permute-start | bytes 6291464 | tf_op jit(solution)/shard_map/ppermute | solution.py:864
  219.2 17.2 %collective-permute-start.33 = (bf16[256,1024]{1,0:T(8,128)(2,1)}, bf16[256,1024]{1,0:T(8,128)(2,1)S(1)}, u32[]{:S(2)}, u32[]{:S(2)}) collective-permute-start(bf16[256,1024]{1,0:T(8,128)(2,1)} %get-tuple-element.349), channel_id=1, source_target_pairs={{0,8},{4,12},{8,0},{12,4},{16,24},{20,28},{24,16},{28,20},{1,9},{5... | collective-permute-start | bytes 1572872 | tf_op jit(solution)/shard_map/ppermute | solution.py:864
  220.7 18.6 %collective-permute-start.34 = (bf16[256,1024]{1,0:T(8,128)(2,1)S(1)}, bf16[256,1024]{1,0:T(8,128)(2,1)S(1)}, u32[]{:S(2)}, u32[]{:S(2)}) collective-permute-start(bf16[256,1024]{1,0:T(8,128)(2,1)S(1)} %get-tuple-element.347), channel_id=1, source_target_pairs={{0,4},{4,0},{8,12},{12,8},{16,20},{20,16},{24,28},{28,24},{1,5},{5... | collective-permute-start | bytes 1572872 | tf_op jit(solution)/shard_map/ppermute | solution.py:864
  222.3 9.5 %collective-permute-start.31 = (bf16[512,256]{1,0:T(8,128)(2,1)}, bf16[512,256]{1,0:T(8,128)(2,1)S(1)}, u32[]{:S(2)}, u32[]{:S(2)}) collective-permute-start(bf16[512,256]{1,0:T(8,128)(2,1)} %get-tuple-element.247), channel_id=1, source_target_pairs={{0,2},{1,3},{2,0},{3,1},{4,6},{5,7},{6,4},{7,5},{8,10},{9,11},{10,... | collective-permute-start | bytes 786440 | tf_op jit(solution)/shard_map/ppermute | solution.py:864
  223.7 12.7 %collective-permute-start.32 = (bf16[512,256]{1,0:T(8,128)(2,1)}, bf16[512,256]{1,0:T(8,128)(2,1)S(1)}, u32[]{:S(2)}, u32[]{:S(2)}) collective-permute-start(bf16[512,256]{1,0:T(8,128)(2,1)} %get-tuple-element.248), channel_id=1, source_target_pairs={{0,3},{1,2},{2,1},{3,0},{4,7},{5,6},{6,5},{7,4},{8,11},{9,10},{10,... | collective-permute-start | bytes 786440 | tf_op jit(solution)/shard_map/ppermute | solution.py:864
  225.7 47.2 %collective-permute-start.29 = (bf16[1024,256]{1,0:T(8,128)(2,1)S(1)}, bf16[1024,256]{1,0:T(8,128)(2,1)}, u32[]{:S(2)}, u32[]{:S(2)}) collective-permute-start(bf16[1024,256]{1,0:T(8,128)(2,1)S(1)} %add_convert_fusion.9), channel_id=1, source_target_pairs={{0,2},{1,3},{2,0},{3,1},{4,6},{5,7},{6,4},{7,5},{8,10},{9,11},{10,... | collective-permute-start | bytes 1572872 | tf_op jit(solution)/shard_map/ppermute | solution.py:864
  236.6 21.1 %collective-permute-start.35 = (bf16[128,1024]{1,0:T(8,128)(2,1)S(1)}, bf16[128,1024]{1,0:T(8,128)(2,1)S(1)}, u32[]{:S(2)}, u32[]{:S(2)}) collective-permute-start(bf16[128,1024]{1,0:T(8,128)(2,1)S(1)} %get-tuple-element.361), channel_id=1, source_target_pairs={{0,16},{4,20},{8,24},{12,28},{16,0},{20,4},{24,8},{28,12},{1,17},{... | collective-permute-start | bytes 786440 | tf_op jit(solution)/shard_map/ppermute | solution.py:864
  239.6 33.4 %collective-permute-start.37 = (bf16[128,1024]{1,0:T(8,128)(2,1)S(1)}, bf16[128,1024]{1,0:T(8,128)(2,1)S(1)}, u32[]{:S(2)}, u32[]{:S(2)}) collective-permute-start(bf16[128,1024]{1,0:T(8,128)(2,1)S(1)} %get-tuple-element.359), channel_id=1, source_target_pairs={{0,16},{4,20},{8,24},{12,28},{16,0},{20,4},{24,8},{28,12},{1,17},{... | collective-permute-start | bytes 786440 | tf_op jit(solution)/shard_map/ppermute | solution.py:864
  257.8 17.0 %collective-permute-start.36 = (bf16[128,1024]{1,0:T(8,128)(2,1)S(1)}, bf16[128,1024]{1,0:T(8,128)(2,1)S(1)}, u32[]{:S(2)}, u32[]{:S(2)}) collective-permute-start(bf16[128,1024]{1,0:T(8,128)(2,1)S(1)} %add_convert_fusion.13), channel_id=1, source_target_pairs={{0,16},{4,20},{8,24},{12,28},{16,0},{20,4},{24,8},{28,12},{1,17},{... | collective-permute-start | bytes 786440 | tf_op jit(solution)/shard_map/ppermute | solution.py:864
  273.0 23.9 %collective-permute-start.39 = (bf16[128,1024]{1,0:T(8,128)(2,1)S(1)}, bf16[128,1024]{1,0:T(8,128)(2,1)S(1)}, u32[]{:S(2)}, u32[]{:S(2)}) collective-permute-start(bf16[128,1024]{1,0:T(8,128)(2,1)S(1)} %add_convert_fusion.12), channel_id=1, source_target_pairs={{0,16},{4,20},{8,24},{12,28},{16,0},{20,4},{24,8},{28,12},{1,17},{... | collective-permute-start | bytes 786440 | tf_op jit(solution)/shard_map/ppermute | solution.py:864
  274.9 22.2 %collective-permute-start.38 = (bf16[256,1024]{1,0:T(8,128)(2,1)S(1)}, bf16[256,1024]{1,0:T(8,128)(2,1)S(1)}, u32[]{:S(2)}, u32[]{:S(2)}) collective-permute-start(bf16[256,1024]{1,0:T(8,128)(2,1)S(1)} %pad_maximum_fusion.3), channel_id=1, source_target_pairs={{0,8},{4,12},{8,0},{12,4},{16,24},{20,28},{24,16},{28,20},{1,9},{5... | collective-permute-start | bytes 1572872 | tf_op jit(solution)/shard_map/ppermute | solution.py:864
  275.4 43.1 %collective-permute-start.42 = (bf16[512,1024]{1,0:T(8,128)(2,1)S(1)}, bf16[512,1024]{1,0:T(8,128)(2,1)S(1)}, u32[]{:S(2)}, u32[]{:S(2)}) collective-permute-start(bf16[512,1024]{1,0:T(8,128)(2,1)S(1)} %add_convert_fusion.2), channel_id=1, source_target_pairs={{0,2},{1,3},{2,0},{3,1},{4,6},{5,7},{6,4},{7,5},{8,10},{9,11},{10,... | collective-permute-start | bytes 3145736 | tf_op jit(solution)/shard_map/ppermute | solution.py:864
  283.2 17.6 %collective-permute-start.40 = (bf16[512,640]{1,0:T(8,128)(2,1)}, bf16[512,640]{1,0:T(8,128)(2,1)S(1)}, u32[]{:S(2)}, u32[]{:S(2)}) collective-permute-start(bf16[512,640]{1,0:T(8,128)(2,1)} %get-tuple-element.273), channel_id=1, source_target_pairs={{0,4},{4,0},{8,12},{12,8},{16,20},{20,16},{24,28},{28,24},{1,5},{5... | collective-permute-start | bytes 1966088 | tf_op jit(solution)/shard_map/ppermute | solution.py:864
  297.0 21.5 %collective-permute-start.41 = (bf16[256,1024]{1,0:T(8,128)(2,1)S(1)}, bf16[256,1024]{1,0:T(8,128)(2,1)S(1)}, u32[]{:S(2)}, u32[]{:S(2)}) collective-permute-start(bf16[256,1024]{1,0:T(8,128)(2,1)S(1)} %pad_maximum_fusion.4), channel_id=1, source_target_pairs={{0,4},{4,0},{8,12},{12,8},{16,20},{20,16},{24,28},{28,24},{1,5},{5... | collective-permute-start | bytes 1572872 | tf_op jit(solution)/shard_map/ppermute | solution.py:864
  301.0 18.4 %collective-permute-start.43 = (bf16[256,640]{1,0:T(8,128)(2,1)S(1)}, bf16[256,640]{1,0:T(8,128)(2,1)}, u32[]{:S(2)}, u32[]{:S(2)}) collective-permute-start(bf16[256,640]{1,0:T(8,128)(2,1)S(1)} %get-tuple-element.353), channel_id=1, source_target_pairs={{0,8},{4,12},{8,0},{12,4},{16,24},{20,28},{24,16},{28,20},{1,9},{5... | collective-permute-start | bytes 983048 | tf_op jit(solution)/shard_map/ppermute | solution.py:864
  332.9 13.1 %collective-permute-start.44 = (bf16[512,1024]{1,0:T(8,128)(2,1)}, bf16[512,1024]{1,0:T(8,128)(2,1)}, u32[]{:S(2)}, u32[]{:S(2)}) collective-permute-start(bf16[512,1024]{1,0:T(8,128)(2,1)} %get-tuple-element.300), channel_id=1, source_target_pairs={{0,1},{1,0},{2,3},{3,2},{4,5},{5,4},{6,7},{7,6},{8,9},{9,8},{10,11... | collective-permute-start | bytes 3145736 | tf_op jit(solution)/shard_map/ppermute | solution.py:864
  332.9 26.1 %collective-permute-start.45 = (bf16[512,1024]{1,0:T(8,128)(2,1)S(1)}, bf16[512,1024]{1,0:T(8,128)(2,1)}, u32[]{:S(2)}, u32[]{:S(2)}) collective-permute-start(bf16[512,1024]{1,0:T(8,128)(2,1)S(1)} %pad_maximum_fusion.refs_0_), channel_id=1, source_target_pairs={{0,4},{4,0},{8,12},{12,8},{16,20},{20,16},{24,28},{28,24},{1,5},{5... | collective-permute-start | bytes 3145736 | tf_op jit(solution)/shard_map/ppermute | solution.py:864
  333.1 36.0 %collective-permute-start.49 = (bf16[512,1024]{1,0:T(8,128)(2,1)S(1)}, bf16[512,1024]{1,0:T(8,128)(2,1)}, u32[]{:S(2)}, u32[]{:S(2)}) collective-permute-start(bf16[512,1024]{1,0:T(8,128)(2,1)S(1)} %pad_maximum_fusion.1.refs_0_), channel_id=1, source_target_pairs={{0,8},{4,12},{8,0},{12,4},{16,24},{20,28},{24,16},{28,20},{1,9},{5... | collective-permute-start | bytes 3145736 | tf_op jit(solution)/shard_map/ppermute | solution.py:864
  333.2 31.0 %collective-permute-start.46 = (bf16[128,640]{1,0:T(8,128)(2,1)}, bf16[128,640]{1,0:T(8,128)(2,1)}, u32[]{:S(2)}, u32[]{:S(2)}) collective-permute-start(bf16[128,640]{1,0:T(8,128)(2,1)} %get-tuple-element.373), channel_id=1, source_target_pairs={{0,16},{4,20},{8,24},{12,28},{16,0},{20,4},{24,8},{28,12},{1,17},{... | collective-permute-start | bytes 491528 | tf_op jit(solution)/shard_map/ppermute | solution.py:864
  335.0 32.0 %collective-permute-start.47 = (bf16[512,384]{1,0:T(8,128)(2,1)}, bf16[512,384]{1,0:T(8,128)(2,1)}, u32[]{:S(2)}, u32[]{:S(2)}) collective-permute-start(bf16[512,384]{1,0:T(8,128)(2,1)} %get-tuple-element.296), channel_id=1, source_target_pairs={{0,4},{4,0},{8,12},{12,8},{16,20},{20,16},{24,28},{28,24},{1,5},{5... | collective-permute-start | bytes 1179656 | tf_op jit(solution)/shard_map/ppermute | solution.py:864
  338.0 30.2 %all-to-all-start = ((f32[4,8,1024]{2,1,0:T(8,128)}), f32[4,8,1024]{2,1,0:T(8,128)S(1)}, u32[]{:S(2)}, u32[]{:S(2)}) async-start(f32[4,8,1024]{2,1,0:T(8,128)} %broadcast_in_dim.96), calls=%async_computation | async-start | bytes 262144 | tf_op jit(solution)/shard_map/all_to_all | solution.py:1213
  346.1 53.3 %collective-permute-start.54 = (bf16[512,1024]{1,0:T(8,128)(2,1)}, bf16[512,1024]{1,0:T(8,128)(2,1)}, u32[]{:S(2)}, u32[]{:S(2)}) collective-permute-start(bf16[512,1024]{1,0:T(8,128)(2,1)} %get-tuple-element.323), channel_id=1, source_target_pairs={{0,1},{1,0},{2,3},{3,2},{4,5},{5,4},{6,7},{7,6},{8,9},{9,8},{10,11... | collective-permute-start | bytes 3145736 | tf_op jit(solution)/shard_map/ppermute | solution.py:864
  359.0 40.3 %collective-permute-start.55 = (bf16[512,1024]{1,0:T(8,128)(2,1)}, bf16[512,1024]{1,0:T(8,128)(2,1)}, u32[]{:S(2)}, u32[]{:S(2)}) collective-permute-start(bf16[512,1024]{1,0:T(8,128)(2,1)} %add_convert_fusion.1), channel_id=1, source_target_pairs={{0,2},{1,3},{2,0},{3,1},{4,6},{5,7},{6,4},{7,5},{8,10},{9,11},{10,... | collective-permute-start | bytes 3145736 | tf_op jit(solution)/shard_map/ppermute | solution.py:864
  365.1 9.2 %collective-permute-start.48 = (bf16[128,640]{1,0:T(8,128)(2,1)S(1)}, bf16[128,640]{1,0:T(8,128)(2,1)S(1)}, u32[]{:S(2)}, u32[]{:S(2)}) collective-permute-start(bf16[128,640]{1,0:T(8,128)(2,1)S(1)} %add_convert_fusion.14), channel_id=1, source_target_pairs={{0,16},{4,20},{8,24},{12,28},{16,0},{20,4},{24,8},{28,12},{1,17},{... | collective-permute-start | bytes 491528 | tf_op jit(solution)/shard_map/ppermute | solution.py:864
  373.2 10.3 %collective-permute-start.51 = (bf16[128,384]{1,0:T(8,128)(2,1)S(1)}, bf16[128,384]{1,0:T(8,128)(2,1)S(1)}, u32[]{:S(2)}, u32[]{:S(2)}) collective-permute-start(bf16[128,384]{1,0:T(8,128)(2,1)S(1)} %get-tuple-element.367), channel_id=1, source_target_pairs={{0,16},{4,20},{8,24},{12,28},{16,0},{20,4},{24,8},{28,12},{1,17},{... | collective-permute-start | bytes 294920 | tf_op jit(solution)/shard_map/ppermute | solution.py:864
  374.3 9.2 %collective-permute-start.52 = (bf16[128,384]{1,0:T(8,128)(2,1)S(1)}, bf16[128,384]{1,0:T(8,128)(2,1)S(1)}, u32[]{:S(2)}, u32[]{:S(2)}) collective-permute-start(bf16[128,384]{1,0:T(8,128)(2,1)S(1)} %get-tuple-element.368), channel_id=1, source_target_pairs={{0,24},{4,28},{8,16},{12,20},{16,8},{20,12},{24,0},{28,4},{1,25},{... | collective-permute-start | bytes 294920 | tf_op jit(solution)/shard_map/ppermute | solution.py:864
  378.5 18.4 %collective-permute-start.56 = (bf16[256,640]{1,0:T(8,128)(2,1)S(1)}, bf16[256,640]{1,0:T(8,128)(2,1)S(1)}, u32[]{:S(2)}, u32[]{:S(2)}) collective-permute-start(bf16[256,640]{1,0:T(8,128)(2,1)S(1)} %pad_maximum_fusion.6), channel_id=1, source_target_pairs={{0,8},{4,12},{8,0},{12,4},{16,24},{20,28},{24,16},{28,20},{1,9},{5... | collective-permute-start | bytes 983048 | tf_op jit(solution)/shard_map/ppermute | solution.py:864
  378.6 28.5 %all-to-all-start.1 = ((f32[8,16,1024]{2,1,0:T(8,128)}), f32[8,16,1024]{2,1,0:T(8,128)}, u32[]{:S(2)}, u32[]{:S(2)}) async-start(f32[8,16,1024]{2,1,0:T(8,128)} %broadcast_in_dim.97), calls=%async_computation.1 | async-start | bytes 1048576 | tf_op jit(solution)/shard_map/all_to_all | solution.py:1230
  383.6 21.3 %collective-permute-start.58 = (bf16[128,384]{1,0:T(8,128)(2,1)S(1)}, bf16[128,384]{1,0:T(8,128)(2,1)S(1)}, u32[]{:S(2)}, u32[]{:S(2)}) collective-permute-start(bf16[128,384]{1,0:T(8,128)(2,1)S(1)} %add_convert_fusion.15), channel_id=1, source_target_pairs={{0,8},{4,12},{8,0},{12,4},{16,24},{20,28},{24,16},{28,20},{1,9},{5... | collective-permute-start | bytes 294920 | tf_op jit(solution)/shard_map/ppermute | solution.py:864
  385.2 19.6 %collective-permute-start.57 = (bf16[128,384]{1,0:T(8,128)(2,1)S(1)}, bf16[128,384]{1,0:T(8,128)(2,1)S(1)}, u32[]{:S(2)}, u32[]{:S(2)}) collective-permute-start(bf16[128,384]{1,0:T(8,128)(2,1)S(1)} %add_convert_fusion.15), channel_id=1, source_target_pairs={{0,16},{4,20},{8,24},{12,28},{16,0},{20,4},{24,8},{28,12},{1,17},{... | collective-permute-start | bytes 294920 | tf_op jit(solution)/shard_map/ppermute | solution.py:864
  396.9 7.9 %collective-permute-start.53 = (bf16[128,384]{1,0:T(8,128)(2,1)S(1)}, bf16[128,384]{1,0:T(8,128)(2,1)S(1)}, u32[]{:S(2)}, u32[]{:S(2)}) collective-permute-start(bf16[128,384]{1,0:T(8,128)(2,1)S(1)} %add_convert_fusion.15), channel_id=1, source_target_pairs={{0,24},{4,28},{8,16},{12,20},{16,8},{20,12},{24,0},{28,4},{1,25},{... | collective-permute-start | bytes 294920 | tf_op jit(solution)/shard_map/ppermute | solution.py:864
  399.4 18.0 %collective-permute-start.59 = (bf16[512,640]{1,0:T(8,128)(2,1)}, bf16[512,640]{1,0:T(8,128)(2,1)}, u32[]{:S(2)}, u32[]{:S(2)}) collective-permute-start(bf16[512,640]{1,0:T(8,128)(2,1)} %pad_maximum_fusion.2.refs_0_), channel_id=1, source_target_pairs={{0,4},{4,0},{8,12},{12,8},{16,20},{20,16},{24,28},{28,24},{1,5},{5... | collective-permute-start | bytes 1966088 | tf_op jit(solution)/shard_map/ppermute | solution.py:864
  405.0 17.0 %collective-permute-start.60 = (bf16[512,384]{1,0:T(8,128)(2,1)S(1)}, bf16[512,384]{1,0:T(8,128)(2,1)}, u32[]{:S(2)}, u32[]{:S(2)}) collective-permute-start(bf16[512,384]{1,0:T(8,128)(2,1)S(1)} %pad_maximum_fusion.5.refs_1_), channel_id=1, source_target_pairs={{0,4},{4,0},{8,12},{12,8},{16,20},{20,16},{24,28},{28,24},{1,5},{5... | collective-permute-start | bytes 1179656 | tf_op jit(solution)/shard_map/ppermute | solution.py:864
  (70 other events, 440.0 us)
where the time goes:
time: 431 us; the launch traced here: 426 us
  Pallas kernels  231 us (54%)
  waiting for transfers between devices  90.1 us (21%)
  starting transfers between devices  59.8 us (14%)
  other arithmetic  25.3 us (6%)
  local copies, waits for them, and re-layouts  18.1 us (4%)
    ppermute x61, waiting for transfers between devices, swap(): return lax.ppermute(value, axis, [(i, i ^ bit) for i in range(size)])  90.1 us
    pallas_call x4, Pallas kernels, attend_backward(): pl.pallas_call(functools.partial(backward_kernel, tok, turn), grid=(1,),...  56.5 us
    ppermute x61, starting transfers between devices, swap(): return lax.ppermute(value, axis, [(i, i ^ bit) for i in range(size)])  52 us
    pallas_call x4, Pallas kernels, gradient(): pl.pallas_call(functools.partial(gradient_kernel, steps, nl, nr, len(join...  32.3 us
    pallas_call x2, Pallas kernels, attend_forward(): pl.pallas_call(functools.partial(forward_kernel, tok), grid=(1,), out_sha...  28.3 us
    pallas_call x2, Pallas kernels, ffn_second(): pl.pallas_call(functools.partial(ffn_second_kernel, ndev, n, per), grid=(...  24 us
    pallas_call x2, Pallas kernels, ffn_first(): pl.pallas_call(functools.partial(ffn_first_kernel, xp, cp), grid=(rows //...  21.1 us
    pallas_call x3, Pallas kernels, products(): pl.pallas_call(functools.partial(products_kernel, len(xs), len(weights),...  18.1 us
  transfers between devices with their start and end apart: 63, of which 25 were waited for; matrix products, arithmetic and copies ran while one was open for 8% of the time, Pallas kernels for 43%

commit v1 on v0

--- a/solution.py
+++ b/solution.py
@@ -28,7 +28,7 @@
 
 
 def cost(us):
-    return pl.CostEstimate(flops=0, bytes_accessed=int(us * 1000), transcendentals=0)
+    return pl.CostEstimate(flops=int(us * 1e10), bytes_accessed=int(us * 3.6e7), transcendentals=0)
 
 
 def dot(a, b, ca=1, cb=0, precision=None):
@@ -185,16 +185,18 @@
     return last
 
 
-def backward_kernel(tok, turn, me_ref, len_ref, q_ref, k_ref, v_ref, att_ref, lse_ref, *refs):
+def backward_kernel(tok, turn, me_ref, len_ref, q_ref, k_ref, v_ref, lse_ref, *refs):
     nslot = ROW // tok
     width = q_ref.shape[1]
     heads = width // HEAD_DIM
+    if turn == 0:
+        att_ref, refs = refs[0], refs[1:]
     do_refs = refs[:nslot]
     if turn == 0:
-        dqkv_ref, sum_ref, dqt_ref = refs[nslot : nslot + 3]
+        dkv_ref, sum_ref, dqt_ref, delta_ref = refs[nslot : nslot + 4]
     else:
-        dqkv_in, sum_in, dqt_in, dqkv_ref, sum_ref, dqt_ref = refs[nslot : nslot + 6]
-    do_ref, q4_ref, do4_ref, delta_ref = refs[-4:]
+        dkv_in, sum_in, dqt_in, delta_ref, dqkv_ref, sum_ref, dqt_ref = refs[nslot : nslot + 7]
+    do_ref, q4_ref, do4_ref = refs[-3:]
     me = me_ref[0]
     ends = seq_ends(len_ref)
     for s in range(nslot):
@@ -214,11 +216,11 @@
         q4_ref[place] = spread_heads(q_ref[rows, :], heads)
         do = do_ref[place ^ me]
         do4_ref[place] = spread_heads(do, heads)
-        both = do.astype(F32) * att_ref[rows, :]
         if turn == 0:
+            both = do.astype(F32) * att_ref[rows, :]
             sum_ref[:, 3 * width :] += jnp.sum(both, 0, keepdims=True)
-        d = dot(pick, both, 1, 1, lax.Precision.HIGHEST)
-        delta_ref[place] = jnp.concatenate([d[h : h + 1] for h in range(heads)], axis=1)
+            d = dot(pick, both, 1, 1, lax.Precision.HIGHEST)
+            delta_ref[place] = jnp.concatenate([d[h : h + 1] for h in range(heads)], axis=1)
 
     @pl.loop(0, nslot // 2)
     def _(j):
@@ -259,8 +261,12 @@
         dk, dv = lax.fori_loop(whole, upto, lambda qi, st: tile(qi, st, True), state)
         dk = (dk * HEAD_DIM**-0.5).astype(BF16)
         dv = dv.astype(BF16)
-        dqkv_ref[rows, width : 2 * width] = dk
-        dqkv_ref[rows, 2 * width :] = dv
+        if turn == 0:
+            dkv_ref[j, :, :width] = dk
+            dkv_ref[j, :, width:] = dv
+        else:
+            dqkv_ref[rows, width : 2 * width] = dk
+            dqkv_ref[rows, 2 * width :] = dv
         sum_ref[:, width : 2 * width] += jnp.sum(dk.astype(F32), 0, keepdims=True)
         sum_ref[:, 2 * width : 3 * width] += jnp.sum(dv.astype(F32), 0, keepdims=True)
 
@@ -270,7 +276,7 @@
     @pl.loop(0, nslot // 2)
     def _(j):
         rows = slot_rows(4 * (j // 2) + 3 * (j % 2), me, tok)
-        dqkv_ref[rows, width:] = dqkv_in[rows, width:]
+        dqkv_ref[rows, width:] = dkv_in[j]
 
     @pl.loop(0, nslot)
     def _(place):
@@ -282,14 +288,20 @@
 def attend_backward(me, lengths, qkv, att, lse, grads, tok, pair, turn, held=()):
     nslot = ROW // tok
     lanes = PAIR // HEAD_DIM * tok
-    made = [((ROW, 3 * PAIR), BF16), ((1, 4 * PAIR), F32), ((nslot, HEAD_DIM, lanes), F32)]
+    made = [((1, 4 * PAIR), F32), ((nslot, HEAD_DIM, lanes), F32)]
+    if turn == 0:
+        made = [((nslot // 2, tok, 2 * PAIR), BF16), *made, ((nslot, 1, lanes), F32)]
+        first = [att]
+    else:
+        made = [((ROW, 3 * PAIR), BF16), *made]
+        first = []
     return pl.pallas_call(
         functools.partial(backward_kernel, tok, turn),
         grid=(1,),
         out_shape=[shape(*m) for m in made],
         in_specs=[SMEM_SPEC, SMEM_SPEC]
         + pair_blocks(qkv, pair)
-        + [whole_spec(att.shape), whole_spec(lse.shape)]
+        + [whole_spec(v.shape) for v in (lse, *first)]
         + [pl.BlockSpec((tok, PAIR), lambda t: (0, pair))] * nslot
         + [whole_spec(v.shape) for v in held],
         out_specs=[whole_spec(m[0]) for m in made],
@@ -297,12 +309,11 @@
             pltpu.VMEM((nslot, tok, PAIR), BF16),
             pltpu.VMEM((nslot, lanes, PAIR), BF16),
             pltpu.VMEM((nslot, lanes, PAIR), BF16),
-            pltpu.VMEM((nslot, 1, lanes), F32),
         ],
         compiler_params=PARAMS,
         cost_estimate=cost(8),
         name="attend_backward",
-    )(me, lengths, qkv, qkv, qkv, att, lse, *grads, *held)
+    )(me, lengths, qkv, qkv, qkv, lse, *first, *grads, *held)
 
 
 def centred(v):
@@ -412,7 +423,7 @@
     return pl.BlockSpec(array.shape, lambda *_: (0,) * array.ndim)
 
 
-def after_attention(mixed, weights, tokens, *vectors, tile=128):
+def after_attention(mixed, weights, tokens, *vectors, tile=256):
     rows, d = tokens.shape
     tile = min(tile, rows)
     n, pairs = len(mixed), len(mixed[0])
@@ -464,7 +475,7 @@
         pieces[s][...] = made.astype(BF16)
 
 
-def before_attention(came, residual, branch, cot, gain3, gain2, scale_slots, weights, tile=128):
+def before_attention(came, residual, branch, cot, gain3, gain2, scale_slots, weights, tile=256):
     rows, d = residual.shape
     width = weights[0].shape[0]
     tile = min(tile, rows)
@@ -498,7 +509,7 @@
     out_ref[...] = grad_ref[...] + norm_back(unit, inv, c * gain_ref[...])
 
 
-def last_norm(came, x, grad, gain, tile=128):
+def last_norm(came, x, grad, gain, tile=256):
     rows, d = x.shape
     tile = min(tile, rows)
     wide = row_tiles(rows, d, tile)
@@ -545,10 +556,30 @@
     ]
 
 
-def ffn_first_kernel(xp, cp, *refs):
-    n = len(xp) + len(cp)
-    w1_ref, b1_ref, gain_ref, w2_ref = refs[n : n + 4]
-    u_ref, hg_ref, stat_ref = refs[n + 4 :]
+def hidden_gradient_kernel(cp, *refs):
+    refs[-1][...] = dot(pick_piece(refs[: len(cp)], cp), refs[-2][...], 1, 1)
+
+
+def hidden_gradient(cots, w2, tile=256):
+    units, d = w2.shape
+    tile = min(tile, *(v.shape[0] for v in cots))
+    cp = places_of(cots, tile)
+    rows = sum(v.shape[0] for v in cots)
+    return pl.pallas_call(
+        functools.partial(hidden_gradient_kernel, cp),
+        grid=(rows // tile,),
+        in_specs=piece_tiles(cp, tile, d) + [fixed(w2)],
+        out_specs=row_tiles(rows, units, tile),
+        out_shape=shape((rows, units), F32),
+        compiler_params=PARAMS,
+        cost_estimate=cost(3),
+        name="hidden_gradient",
+    )(*map(array_of, cots), w2)
+
+
+def ffn_first_kernel(xp, *refs):
+    n = len(xp)
+    hg_ref, w1_ref, b1_ref, gain_ref, u_ref, stat_ref = refs[n:]
     units = u_ref.shape[1]
     u = dot(pick_piece(refs[: len(xp)], xp), w1_ref[...]) + b1_ref[...]
     u_ref[...] = u
@@ -556,9 +587,7 @@
     a = u * half
     total = jnp.sum(a, 1, keepdims=True)
     d = a - total * (1.0 / units)
-    hg = dot(pick_piece(refs[len(xp) : n], cp), w2_ref[...], 1, 1)
-    hg_ref[...] = hg
-    sg = hg * gain_ref[...]
+    sg = hg_ref[...] * gain_ref[...]
     cols = [
         total,
         jnp.sum(d * d, 1, keepdims=True),
@@ -572,27 +601,23 @@
     stat_ref[...] = wide.T[:8]
 
 
-def ffn_first(xs, cots, w1, b1, gain, w2, tile=256):
+def ffn_first(xs, hg, w1, b1, gain, tile=256):
     d, units = w1.shape
-    tile = min(tile, *(v.shape[0] for v in (*xs, *cots)))
-    xp, cp = places_of(xs, tile), places_of(cots, tile)
+    tile = min(tile, *(v.shape[0] for v in xs))
+    xp = places_of(xs, tile)
     rows = sum(v.shape[0] for v in xs)
     return pl.pallas_call(
-        functools.partial(ffn_first_kernel, xp, cp),
+        functools.partial(ffn_first_kernel, xp),
         grid=(rows // tile,),
         in_specs=piece_tiles(xp, tile, d)
-        + piece_tiles(cp, tile, d)
-        + [fixed(v) for v in (w1, b1, gain, w2)],
-        out_specs=(
-            row_tiles(rows, units, tile),
-            row_tiles(rows, units, tile),
-            pl.BlockSpec((8, tile), lambda t: (0, t)),
-        ),
-        out_shape=(shape((rows, units), F32), shape((rows, units), F32), shape((8, rows), F32)),
+        + [row_tiles(rows, units, tile)]
+        + [fixed(v) for v in (w1, b1, gain)],
+        out_specs=(row_tiles(rows, units, tile), pl.BlockSpec((8, tile), lambda t: (0, t))),
+        out_shape=(shape((rows, units), F32), shape((8, rows), F32)),
         compiler_params=PARAMS,
         cost_estimate=cost(5),
         name="ffn_first",
-    )(*xs, *map(array_of, cots), w1, b1, gain, w2)
+    )(*xs, hg, w1, b1, gain)
 
 
 def ffn_second_kernel(ndev, n, per, *refs):
@@ -692,7 +717,7 @@
             out[at * tok : (at + 1) * tok, :] = total.astype(BF16)
 
 
-def products(xs, weights, flip, tok, first, groups):
+def products(xs, weights, flip, tok, first, groups, us=2):
     n = sum(len(g) for g in groups)
     d = weights[0].shape[0 if flip else 1]
     out = pl.pallas_call(
@@ -703,7 +728,7 @@
         out_specs=[whole_spec((len(g) * tok, d)) for g in groups],
         out_shape=[shape((len(g) * tok, d), BF16) for g in groups],
         compiler_params=PARAMS,
-        cost_estimate=cost(2),
+        cost_estimate=cost(us),
         name="products",
     )(*xs, *weights)
     return list(out)
@@ -855,7 +880,7 @@
         in_specs=[SMEM_SPEC] + [VMEM_SPEC] * (2 * len(mine)),
         out_specs=[VMEM_SPEC] * len(out),
         compiler_params=PARAMS,
-        cost_estimate=cost(2),
+        cost_estimate=cost(0),
         name="assemble",
     )(side, *mine, *came)
 
@@ -1079,7 +1104,8 @@
     cot_near = spread_low({0: cot_low}, "mp", mp, lower)
     out_near = spread_low({0: output_weight}, "mp", mp, lower)
     both = jnp.concatenate([cot_low, output_weight])
-    normed_far = after(normed_far, qkv, both, cot_near[half - 1], out_near[half - 1])
+    hg_near = hidden_gradient([after(cot_near[s], qkv) for s in range(half)], fc2_weight)
+    normed_far = after(normed_far, hg_near, both, out_near[half - 1])
     both_far = wide_swap(after(both, normed_far))
     normed_far = spread_low({half: normed_far}, "mp", mp, lower)
     qkv = qkv_part([normed_far[half + s] for s in range(half)], qkv_weights, bias_qkv, 1, qkv)
@@ -1112,15 +1138,15 @@
     ffn_far = wide_swap(ffn_own)
     ffn_near = spread_low({0: ffn_own}, "mp", mp, lower)
     scale_slots = direct_slots(after(scale_lanes, ffn_own), "mp", mp)
-    ffn_args = (fc1_weight, row(fc1_bias), row(mid_gain), fc2_weight)
-    u_near, hg_near, st_near = ffn_first(
-        [ffn_near[s] for s in range(half)], [cot_near[s] for s in range(half)], *ffn_args
-    )
-    ffn_far = spread_low({half: after(ffn_far, st_near)}, "mp", mp, lower)
-    ffn_args = (fc1_weight, after(row(fc1_bias), *scale_slots[1:]), row(mid_gain), fc2_weight)
-    cots = listed(cot_near, cot_far)
-    ffn_in = listed(ffn_near, ffn_far)
-    u_far, hg_far, st_far = ffn_first(ffn_in[half:], cots[half:], *ffn_args)
+    cots, ffn_near = listed(cot_near, cot_far), [ffn_near[s] for s in range(half)]
+    ffn_args = (fc1_weight, row(fc1_bias), row(mid_gain))
+    u_near, st_near = ffn_first(ffn_near, hg_near, *ffn_args)
+    cot_ready = Window(after(cots[half].array, st_near), 0, tok)
+    hg_far = hidden_gradient([cot_ready, *cots[half + 1 :]], fc2_weight)
+    ffn_far = spread_low({half: after(ffn_far, hg_far)}, "mp", mp, lower)
+    ffn_in = ffn_near + [ffn_far[half + s] for s in range(half)]
+    ffn_args = (fc1_weight, after(row(fc1_bias), *scale_slots[1:]), row(mid_gain))
+    u_far, st_far = ffn_first(ffn_in[half:], hg_far, *ffn_args)
     stats = direct_slots(jnp.concatenate([st_near, st_far], axis=1), "mp", mp)
     ffn_args = (row(mid_gain), row(mid_shift), fc1_weight, stats, tok)
     hid, fg, mid_far, back_far = ffn_second(u_far, hg_far, *ffn_args, 1)
@@ -1135,44 +1161,44 @@
     fc2 = Stream(dp, plain, send, keep)
     send, keep = gradient(side_turned, ffn_in, [after(fg, send)])
     fc1 = Stream(dp, turned, send, keep)
-    hid = after(hid, send)
-    out_near_terms, out_far_terms = merged_terms(
-        products([hid], [fc2_weight], False, tok, 0, merged), tok
-    )
-    came = [after(v, *(t for t in out_far_terms if not isinstance(t, Window))) for v in (*back_near, back_far)]
+    came = [after(v, send) for v in (*back_near, back_far)]
     residual_grad, branch_low, sums, grads = before_attention(
         came, residual, branch, cot_low, row(norm3_gain), row(norm2_gain), scale_slots, out_rows
     )
 
     do = {s: swap(grads[s], "mp", mp, s) for s in far_first}
     do = [grads[0]] + [do[s] for s in range(1, mp)]
-    mark = fc1.advance(branch_low)
-    mark = fc2.advance(mark)
+    mark = fc2.advance(branch_low)
     low = after(branch_low, mark, *do[1:half])
     g_near_terms, g_far_terms = merged_terms(head_gradient(mixed, low, merged), d)
-    g_out_sum, g_out_top = scatter.across([plain_rows(v) for v in g_far_terms])
-    out_far_terms = [after(plain_rows(v), g_out_sum) for v in out_far_terms]
-    out_sum, out_top = scatter.across(out_far_terms)
-    mark = after(out_sum, *do[1:])
-    mark = fc2.advance(mark)
-    mark = fc1.advance(mark)
+    outs = products([after(hid, g_near_terms[0])], [fc2_weight], False, tok, half, one_by_one)
+    out_far_terms = scatter.within({half + j: v for j, v in enumerate(outs)})
+    mark = fc1.advance(outs[0])
+    do[half:] = [after(v, mark) for v in do[half:]]
+    mark = do[-1]
+    g_far_terms = [after(plain_rows(v), mark) for v in g_far_terms]
+    g_out_sum, g_out_top = scatter.across(g_far_terms)
+    mark = fc2.advance(g_out_sum)
 
     dqkvs, sums_att, rows, streams = [], [], [], []
 
     def between(call):
         nonlocal mark
+        nonlocal out_top
         if call == 0:
             mark = fc2.advance(mark)
+            mark = fc1.advance(mark)
+            out_sum, out_top = scatter.across([after(v, mark) for v in out_far_terms])
+            mark = out_sum
         elif call == 1:
-            mark = fc1.advance(after(mark, g_out_top))
-            mark = fc2.advance(mark)
+            mark = fc2.advance(after(mark, g_out_top))
         elif call == 2:
             mark = fc1.advance(mark)
             mark = fc2.advance(mark)
             for stream in streams:
                 mark = stream.advance(mark)
 
-    call = 0
+    call, out_top = 0, None
     for p in range(pairs):
         held = ()
         for turn in range(2):
@@ -1192,10 +1218,9 @@
             )
             rows.append(r)
             streams.append(Stream(dp, plain, send, keep))
-            mark = send
+            mark = fc1.advance(send)
 
     mark = after(mark, out_top)
-    mark = fc1.advance(mark)
     for stream in streams:
         mark = stream.advance(mark)
     joins = [*g_near_terms, g_out_top] if pairs == 1 else ()
@@ -1204,21 +1229,28 @@
     )
     rows.append(r)
     last = Direct(dp, send, keep)
-    far = products(
-        [after(v, send) for v in dqkvs], qkv_weights, True, tok, half, one_by_one
-    )
+    mark = send
+    for stream in streams:
+        mark = stream.advance(mark)
+    packed = jnp.concatenate([sums[:6], sum(rows)[:2]])
+    packed = jnp.broadcast_to(after(packed, mark)[None], (mp, *packed.shape))
+    sent = packed
+    packed = lax.all_to_all(packed, "mp", 0, 0)
+    far = products([after(v, sent) for v in dqkvs], qkv_weights, True, tok, half, one_by_one)
     far_terms = scatter.within({half + j: v for j, v in enumerate(far)})
-    packed = jnp.concatenate([sums[:6], sum(rows)[:2]])
-    packed = jnp.broadcast_to(after(packed, far[0])[None], (mp, *packed.shape))
-    packed = lax.all_to_all(packed, "mp", 0, 0)
-    near = products([after(v, far[0]) for v in dqkvs], qkv_weights, True, tok, 0, one_by_one)
+    mark = far[0]
+    for stream in streams:
+        mark = stream.advance(mark)
+    near = products([after(v, mark) for v in dqkvs], qkv_weights, True, tok, 0, one_by_one)
     far_terms[1:] = [after(v, near[0]) for v in far_terms[1:]]
     far_sum, far_top = scatter.across(far_terms)
     near_terms = scatter.within(dict(enumerate(near)))
-    fc2.done(far_sum)
-    [grad_fc2_weight] = assemble(side, [after(fc2.held, far_sum)], [fc2.came], fc2.held.shape[1])
+    mark = last.advance(far_sum)
+    fc2.done(mark)
+    [grad_fc2_weight] = assemble(side, [after(fc2.held, mark)], [fc2.came], fc2.held.shape[1])
+    mark = fc1.advance(grad_fc2_weight)
     for stream in streams:
-        mark = stream.advance(grad_fc2_weight)
+        mark = stream.advance(mark)
     mark = last.advance(mark)
     packed = after(packed, mark).sum(0)
     mids = jnp.pad(mid_near + mid_far, ((0, 0), (0, d - units)))[:4]
@@ -1228,29 +1260,26 @@
     packed = jnp.broadcast_to(packed[None], (dp, *packed.shape))
     sent = packed
     packed = lax.all_to_all(packed, "dp", 0, 0)
-    fc1.done(sent)
-    [grad_fc1_weight] = assemble(
-        side_turned, [after(fc1.held, sent)], [fc1.came], fc1.held.shape[1]
+    mark = last.advance(sent)
+    outs = products([after(hid, mark)], [fc2_weight], False, tok, 0, one_by_one, 0)
+    out_near_terms = scatter.within(dict(enumerate(outs)))
+    token_grad = last_norm(
+        [*near_terms, after(far_top, outs[0], *(v.came for v in streams))], tokens, residual_grad, row(norm1_gain)
     )
-    for stream in streams:
-        mark = stream.advance(grad_fc1_weight)
-    mark = last.advance(mark)
-    for stream in streams:
-        mark = stream.advance(mark)
-    token_grad = last_norm(
-        [*near_terms, after(far_top, mark)], tokens, residual_grad, row(norm1_gain)
-    )
-    mark = last.advance(token_grad)
     output = residual + row(fc2_bias)
     for t in (*out_near_terms, out_top):
-        output = output + after(plain_rows(t), mark).astype(F32)
+        output = output + after(t, token_grad).astype(F32)
     output = output.astype(BF16)
-    packed = after(packed, mark).sum(0)
+    packed = after(packed, output).sum(0)
+    fc1.done(output)
+    for stream in (*streams, last):
+        stream.done(output)
     streams.append(last)
-    for stream in streams:
-        stream.done(mark)
     grad_query_weight, grad_key_weight, grad_value_weight, grad_output_weight = assemble(
-        side, [v.held for v in streams], [v.came for v in streams], PAIR, width
+        side, [after(v.held, packed) for v in streams], [v.came for v in streams], PAIR, width
+    )
+    [grad_fc1_weight] = assemble(
+        side_turned, [after(fc1.held, grad_query_weight)], [fc1.came], fc1.held.shape[1]
     )
     shift1 = packed[7]
     gain1 = (packed[6] - norm1_shift * shift1) / norm1_gain

time: 431 us -> 397 us (0.921)
  waiting for transfers between devices: 90.1 us -> 58.9 us
  other arithmetic: 25.3 us -> 18.6 us
  Pallas kernels: 231 us -> 236 us
    ppermute x61 -> x62, waiting for transfers between devices: 90.1 us -> 58.9 us  [swap(): return lax.ppermute(value, axis, [(i, i ^ bit) for i in range(size)])]
    pallas_call x2 -> x4, Pallas kernels: 21.1 us -> 30.1 us  [the longest x2 16 us: ffn_first(): pl.pallas_call(functools.partial(ffn_first_kernel, xp), grid=(rows // til...]
    pallas_call x4, Pallas kernels: 56.5 us -> 52.2 us  [attend_backward(): pl.pallas_call(functools.partial(backward_kernel, tok, turn), grid=(1,),...]
    convert_element_type x10, other arithmetic: 6.03 us -> 1.7 us  [add_low(): return (left.astype(F32) + right.astype(F32)).astype(BF16)]
    ppermute x61 -> x62, starting transfers between devices: 52 us -> 55.9 us  [swap(): return lax.ppermute(value, axis, [(i, i ^ bit) for i in range(size)])]
    pallas_call x3 -> x4, Pallas kernels: 18.1 us -> 20.4 us  [products(): pl.pallas_call(functools.partial(products_kernel, len(xs), len(weights),...]
    unnamed x112 -> x120, local copies, waits for them, and re-layouts: 9.4 us -> 9.52 us
  transfers between devices with their start and end apart: 63 -> 64, of which waited for: 25 -> 21; matrix products, arithmetic and copies ran while one was open for 8% -> 6% of each run, Pallas kernels for 43% -> 52%
where the time goes in v1:
time: 397 us; the launch traced here: 393 us
  Pallas kernels  236 us (59%)
  starting transfers between devices  62.9 us (16%)
  waiting for transfers between devices  58.9 us (15%)
  other arithmetic  18.6 us (5%)
  local copies, waits for them, and re-layouts  15.2 us (4%)
    ppermute x62, waiting for transfers between devices, swap(): return lax.ppermute(value, axis, [(i, i ^ bit) for i in range(size)])  58.9 us
    ppermute x62, starting transfers between devices, swap(): return lax.ppermute(value, axis, [(i, i ^ bit) for i in range(size)])  55.9 us
    pallas_call x4, Pallas kernels, attend_backward(): pl.pallas_call(functools.partial(backward_kernel, tok, turn), grid=(1,),...  52.2 us
    pallas_call x4, Pallas kernels, gradient(): pl.pallas_call(functools.partial(gradient_kernel, steps, nl, nr, len(join...  32.4 us
    pallas_call x2, Pallas kernels, attend_forward(): pl.pallas_call(functools.partial(forward_kernel, tok), grid=(1,), out_sha...  28.1 us
    pallas_call x2, Pallas kernels, ffn_second(): pl.pallas_call(functools.partial(ffn_second_kernel, ndev, n, per), grid=(...  23.5 us
    pallas_call x4, Pallas kernels, products(): pl.pallas_call(functools.partial(products_kernel, len(xs), len(weights),...  20.4 us
    pallas_call x2, Pallas kernels, ffn_first(): pl.pallas_call(functools.partial(ffn_first_kernel, xp), grid=(rows // til...  16 us
  transfers between devices with their start and end apart: 64, of which 21 were waited for; matrix products, arithmetic and copies ran while one was open for 6% of the time, Pallas kernels for 52%

profile of v1, /device:TPU:0, one launch (start us, length us, event | category | flops | bytes accessed | tf_op | source)
XLA Modules:
  0.0 393.0 jit_solution(12901530195605347355)
XLA Ops:
  0.7 3.1 first_norm.1.refs_0_.refs_3_
  4.2 2.5 collective-permute-start
  9.8 4.9 %qkv_part.2.refs_6_ = bf16[2048,768]{1,0:T(8,128)(2,1)} custom-call(bf16[512,1024]{1,0:T(8,128)(2,1)} %first_norm.1.refs_0_.refs_3_, bf16[512,1024]{1,0:T(8,128)(2,1)} %copy-done.35, bf16[1024,256]{1,0:T(8,128)(2,1)} %refs_2_.11, bf16[1024,256]{1,0:T(8,128)(2,1)} %refs_3_.12, bf16[1024,256]{1,0:T(8,128)(2,1)} %refs_4_.11, f32[1,768]{1,0:T(1,128)} %broadcast_in_dim.84.refs_5_), custom_call_target="tpu_custom_call" | custom-call | flops 30000001024 | bytes 108000000 | tf_op jit(solution)/shard_map/qkv_part/pallas_call | solution.py:371
  17.8 6.9 %hidden_gradient.2.refs_2_.refs_1_ = f32[1024,1024]{1,0:T(8,128)} custom-call(bf16[512,1024]{1,0:T(8,128)(2,1)} %copy-done.1, bf16[512,1024]{1,0:T(8,128)(2,1)} %copy-done.38, bf16[1024,1024]{1,0:T(8,128)(2,1)} %refs_1_.3), custom_call_target="tpu_custom_call" | custom-call | flops 30000001024 | bytes 108000000 | tf_op jit(solution)/shard_map/hidden_gradient/pallas_call | solution.py:568
  24.7 6.0 %collective-permute-done.refs_0_.refs_5_.refs_2_ = bf16[512,1024]{1,0:T(8,128)(2,1)S(1)} collective-permute-done((bf16[512,1024]{1,0:T(8,128)(2,1)}, bf16[512,1024]{1,0:T(8,128)(2,1)S(1)}, u32[]{:S(2)}, u32[]{:S(2)}) %collective-permute-start) | collective-permute-done | bytes 1048608 | tf_op jit(solution)/shard_map/ppermute | solution.py:889
  35.2 4.9 %qkv_part.3.q_ref.k_ref.v_ref = bf16[2048,768]{1,0:T(8,128)(2,1)} custom-call(bf16[512,1024]{1,0:T(8,128)(2,1)} %copy-done.36, bf16[512,1024]{1,0:T(8,128)(2,1)} %copy-done.37, bf16[1024,256]{1,0:T(8,128)(2,1)} %refs_2_.11, bf16[1024,256]{1,0:T(8,128)(2,1)} %refs_3_.12, bf16[1024,256]{1,0:T(8,128)(2,1)} %refs_4_.11, ...), custom_call_target="tpu_custom_call", output_to_operand_aliasing={{}: (6, {})} | custom-call | flops 30000001024 | bytes 108000000 | tf_op jit(solution)/shard_map/qkv_part/pallas_call | solution.py:371
  40.2 14.0 %attend_forward.2 = (f32[2048,128]{1,0:T(8,128)}, f32[4,1,1024]{2,1,0:T(1,128)}, bf16[512,128]{1,0:T(8,128)(2,1)}, bf16[512,128]{1,0:T(8,128)(2,1)}, bf16[512,128]{1,0:T(8,128)(2,1)}, /*index=5*/bf16[512,128]{1,0:T(8,128)(2,1)}) custom-call(s32[1]{0:T(128)} %bitcast.me_ref, s32[1,8]{1,0:T(1,128)} %len_ref.11, bf16[2048,768]{1,0:T(8,128)(2,1)} %qkv_part.3.q_ref.k_ref.v_ref, ...), custom_call_target="tpu_custom_call" | custom-call | flops 80000000000 | bytes 288000000 | tf_op jit(solution)/shard_map/attend_forward/pallas_call | solution.py:162
  56.1 14.1 %attend_forward.3 = (f32[2048,128]{1,0:T(8,128)}, f32[4,1,1024]{2,1,0:T(1,128)}, bf16[512,128]{1,0:T(8,128)(2,1)}, bf16[512,128]{1,0:T(8,128)(2,1)}, bf16[512,128]{1,0:T(8,128)(2,1)}, /*index=5*/bf16[512,128]{1,0:T(8,128)(2,1)}) custom-call(s32[1]{0:T(128)} %bitcast.me_ref, s32[1,8]{1,0:T(1,128)} %len_ref.11, bf16[2048,768]{1,0:T(8,128)(2,1)} %qkv_part.3.q_ref.k_ref.v_ref, ...), custom_call_target="tpu_custom_call" | custom-call | flops 80000000000 | bytes 288000000 | tf_op jit(solution)/shard_map/attend_forward/pallas_call | solution.py:162
  76.7 3.8 collective-permute-done.10.refs_7_
  80.5 3.0 collective-permute-done.9.refs_5_
  84.8 6.1 %after_attention.1 = (f32[512,1024]{1,0:T(8,128)}, f32[512,1024]{1,0:T(8,128)}, bf16[512,1024]{1,0:T(8,128)(2,1)}) custom-call(bf16[512,128]{1,0:T(8,128)(2,1)} %get-tuple-element.197.refs_0_, bf16[512,128]{1,0:T(8,128)(2,1)} %get-tuple-element.203.refs_1_, bf16[512,128]{1,0:T(8,128)(2,1)} %copy-done.49, bf16[512,128]{1,0:T(8,128)(2,1)} %copy-done.54, ...), custom_call_target="tpu_custom_call" | custom-call | flops 30000001024 | bytes 108000000 | tf_op jit(solution)/shard_map/after_attention/pallas_call | solution.py:432
  94.9 8.0 %ffn_first.2 = (f32[1024,1024]{1,0:T(8,128)}, f32[8,1024]{1,0:T(8,128)}) custom-call(bf16[512,1024]{1,0:T(8,128)(2,1)} %get-tuple-element.213.refs_0_, bf16[512,1024]{1,0:T(8,128)(2,1)} %copy-done.39, f32[1024,1024]{1,0:T(8,128)} %hidden_gradient.2.refs_2_.refs_1_, bf16[1024,1024]{1,0:T(8,128)(2,1)} %refs_4_.9, f32[1,1024]{1,0:T(1,128)} %bitcast.50, ...), custom_call_target="tpu_custom_call" | custom-call | flops 49999998976 | bytes 180000000 | tf_op jit(solution)/shard_map/ffn_first/pallas_call | solution.py:609
  102.9 7.2 %hidden_gradient.3.refs_2_.refs_1_ = f32[1024,1024]{1,0:T(8,128)} custom-call(bf16[768,1024]{1,0:T(8,128)(2,1)} %collective-permute-done.11.refs_10_.refs_0_.refs_3_.refs_11_, bf16[768,1024]{1,0:T(8,128)(2,1)} %copy-done.34, bf16[1024,1024]{1,0:T(8,128)(2,1)} %refs_1_.3), custom_call_target="tpu_custom_call" | custom-call | flops 30000001024 | bytes 108000000 | tf_op jit(solution)/shard_map/hidden_gradient/pallas_call | solution.py:568
  110.0 6.7 %collective-permute-done.14.refs_0_.refs_2_ = bf16[512,1024]{1,0:T(8,128)(2,1)S(1)} collective-permute-done((bf16[512,1024]{1,0:T(8,128)(2,1)}, bf16[512,1024]{1,0:T(8,128)(2,1)S(1)}, u32[]{:S(2)}, u32[]{:S(2)}) %collective-permute-start.14) | collective-permute-done | bytes 1048608 | tf_op jit(solution)/shard_map/ppermute | solution.py:889
  123.1 8.0 %ffn_first.3 = (f32[1024,1024]{1,0:T(8,128)}, f32[8,1024]{1,0:T(8,128)}) custom-call(bf16[512,1024]{1,0:T(8,128)(2,1)} %copy-done.40, bf16[512,1024]{1,0:T(8,128)(2,1)} %copy-done.41, f32[1024,1024]{1,0:T(8,128)} %hidden_gradient.3.refs_2_.refs_1_, bf16[1024,1024]{1,0:T(8,128)(2,1)} %refs_4_.9, f32[1,1024]{1,0:T(1,128)} %bitcast.51, f32[1,1024]{1,0:T(1,128)} %bitcast.53), custom_call_target="tpu_custom_call" | custom-call | flops 49999998976 | bytes 180000000 | tf_op jit(solution)/shard_map/ffn_first/pallas_call | solution.py:609
  134.3 2.5 collective-permute-done.20.refs_7_
  137.9 11.7 %ffn_second.2 = (bf16[2048,1024]{1,0:T(8,128)(2,1)}, bf16[2048,1024]{1,0:T(8,128)(2,1)}, f32[8,1024]{1,0:T(8,128)}, bf16[512,1024]{1,0:T(8,128)(2,1)}, bf16[512,1024]{1,0:T(8,128)(2,1)}) custom-call(f32[1024,1024]{1,0:T(8,128)} %get-tuple-element.221.refs_0_, f32[1024,1024]{1,0:T(8,128)} %hidden_gradient.3.refs_2_.refs_1_, f32[1,1024]{1,0:T(1,128)} %bitcast.54, ...), custom_call_target="tpu_custom_call" | custom-call | flops 49999998976 | bytes 180000000 | tf_op jit(solution)/shard_map/ffn_second/pallas_call | solution.py:689
  150.0 11.8 %ffn_second.3 = (bf16[2048,1024]{1,0:T(8,128)(2,1)}, bf16[2048,1024]{1,0:T(8,128)(2,1)}, f32[8,1024]{1,0:T(8,128)}, bf16[512,1024]{1,0:T(8,128)(2,1)}, bf16[512,1024]{1,0:T(8,128)(2,1)}) custom-call(f32[1024,1024]{1,0:T(8,128)} %get-tuple-element.214.refs_0_, ...), custom_call_target="tpu_custom_call", output_to_operand_aliasing={{0}: (9, {}), {1}: (10, {})} | custom-call | flops 49999998976 | bytes 180000000 | tf_op jit(solution)/shard_map/ffn_second/pallas_call | solution.py:689
  164.7 8.9 %gradient.4 = (bf16[512,1024]{1,0:T(8,128)(2,1)}, bf16[512,1024]{1,0:T(8,128)(2,1)}) custom-call(s32[1]{0:T(128)} %bitcast.11.me_ref.side_ref, bf16[2048,1024]{1,0:T(8,128)(2,1)} %get-tuple-element.343.refs_0_, bf16[512,1024]{1,0:T(8,128)(2,1)} %copy-done.1, bf16[512,1024]{1,0:T(8,128)(2,1)} %copy-done.38, ...), custom_call_target="tpu_custom_call" | custom-call | flops 40000000000 | bytes 144000000 | tf_op jit(solution)/shard_map/gradient/pallas_call | solution.py:844
  175.2 9.1 %gradient.5 = (bf16[512,1024]{1,0:T(8,128)(2,1)}, bf16[512,1024]{1,0:T(8,128)(2,1)}) custom-call(s32[1]{0:T(128)} %bitcast.12.me_ref.side_ref, bf16[512,1024]{1,0:T(8,128)(2,1)} %get-tuple-element.213.refs_0_, bf16[512,1024]{1,0:T(8,128)(2,1)} %copy-done.39, bf16[512,1024]{1,0:T(8,128)(2,1)} %copy-done.40, bf16[512,1024]{1,0:T(8,128)(2,1)} %copy-done.41, ...), custom_call_target="tpu_custom_call" | custom-call | flops 40000000000 | bytes 144000000 | tf_op jit(solution)/shard_map/gradient/pallas_call | solution.py:844
  185.9 3.4 collective-permute-done.24.refs_2_
  190.3 9.6 %before_attention.1 = (f32[512,1024]{1,0:T(8,128)}, bf16[512,1024]{1,0:T(8,128)(2,1)}, f32[8,1024]{1,0:T(8,128)}, bf16[512,256]{1,0:T(8,128)(2,1)}, bf16[512,256...) custom-call(bf16[512,1024]{1,0:T(8,128)(2,1)} %get-tuple-element.235.refs_0_, ...), custom_call_target="tpu_custom_call" | custom-call | flops 30000001024 | bytes 108000000 | tf_op jit(solution)/shard_map/before_attention/pallas_call | solution.py:485
  203.9 4.0 %head_gradient.1 = (bf16[1024,256]{1,0:T(8,128)(2,1)}, bf16[1024,256]{1,0:T(8,128)(2,1)}, bf16[2048,256]{1,0:T(8,128)(2,1)}) custom-call(bf16[512,128]{1,0:T(8,128)(2,1)} %get-tuple-element.197.refs_0_, bf16[512,128]{1,0:T(8,128)(2,1)} %get-tuple-element.203.refs_1_, bf16[512,128]{1,0:T(8,128)(2,1)} %copy-done.49, bf16[512,128]{1,0:T(8,128)(2,1)} %copy-done.54, ...), custom_call_target="tpu_custom_call" | custom-call | flops 20000000000 | bytes 72000000 | tf_op jit(solution)/shard_map/head_gradient/pallas_call | solution.py:751
  208.1 5.6 %products.4 = (bf16[512,1024]{1,0:T(8,128)(2,1)}, bf16[512,1024]{1,0:T(8,128)(2,1)}) custom-call(bf16[2048,1024]{1,0:T(8,128)(2,1)} %get-tuple-element.343.refs_0_, bf16[1024,1024]{1,0:T(8,128)(2,1)} %refs_1_.3), custom_call_target="tpu_custom_call" | custom-call | flops 20000000000 | bytes 72000000 | tf_op jit(solution)/shard_map/products/pallas_call | solution.py:723
  217.2 3.2 collective-permute-done.31
  220.7 2.7 collective-permute-start.33
  224.8 12.8 %attend_backward.4 = (bf16[2,512,256]{2,1,0:T(8,128)(2,1)}, f32[1,512]{1,0:T(1,128)}, f32[4,64,1024]{2,1,0:T(8,128)}, f32[4,1,1024]{2,1,0:T(1,128)}) custom-call(s32[1]{0:T(128)} %bitcast.me_ref, s32[1,8]{1,0:T(1,128)} %len_ref.11, bf16[2048,768]{1,0:T(8,128)(2,1)} %qkv_part.3.q_ref.k_ref.v_ref, bf16[2048,768]{1,0:T(8,128)(2,1)} %qkv_part.3.q_ref.k_ref.v_ref, ...), custom_call_target="tpu_custom_call" | custom-call | flops 80000000000 | bytes 288000000 | tf_op jit(solution)/shard_map/attend_backward/pallas_call | solution.py:298
  238.0 3.0 collective-permute-start.38
  243.0 13.1 %attend_backward.5 = (bf16[2048,384]{1,0:T(8,128)(2,1)}, f32[1,512]{1,0:T(1,128)}, f32[4,64,1024]{2,1,0:T(8,128)}) custom-call(s32[1]{0:T(128)} %bitcast.me_ref, s32[1,8]{1,0:T(1,128)} %len_ref.11, bf16[2048,768]{1,0:T(8,128)(2,1)} %qkv_part.3.q_ref.k_ref.v_ref, bf16[2048,768]{1,0:T(8,128)(2,1)} %qkv_part.3.q_ref.k_ref.v_ref, ...), custom_call_target="tpu_custom_call" | custom-call | flops 80000000000 | bytes 288000000 | tf_op jit(solution)/shard_map/attend_backward/pallas_call | solution.py:298
  256.3 7.4 %gradient.6 = (bf16[512,640]{1,0:T(8,128)(2,1)}, bf16[512,640]{1,0:T(8,128)(2,1)}, f32[8,1024]{1,0:T(8,128)}) custom-call(s32[1]{0:T(128)} %bitcast.11.me_ref.side_ref, bf16[1024,256]{1,0:T(8,128)(2,1)} %get-tuple-element.246.refs_0_, bf16[2048,256]{1,0:T(8,128)(2,1)} %copy-done.17, bf16[1024,256]{1,0:T(8,128)(2,1)} %collective-permute-done.30.refs_2_, ...), custom_call_target="tpu_custom_call" | custom-call | flops 40000000000 | bytes 144000000 | tf_op jit(solution)/shard_map/gradient/pallas_call | solution.py:844
  265.9 12.8 %attend_backward.6 = (bf16[2,512,256]{2,1,0:T(8,128)(2,1)}, f32[1,512]{1,0:T(1,128)}, f32[4,64,1024]{2,1,0:T(8,128)}, f32[4,1,1024]{2,1,0:T(1,128)}) custom-call(s32[1]{0:T(128)} %bitcast.me_ref, s32[1,8]{1,0:T(1,128)} %len_ref.11, bf16[2048,768]{1,0:T(8,128)(2,1)} %qkv_part.3.q_ref.k_ref.v_ref, bf16[2048,768]{1,0:T(8,128)(2,1)} %qkv_part.3.q_ref.k_ref.v_ref, ...), custom_call_target="tpu_custom_call" | custom-call | flops 80000000000 | bytes 288000000 | tf_op jit(solution)/shard_map/attend_backward/pallas_call | solution.py:298
  279.6 3.8 collective-permute-done.37
  285.1 13.3 %attend_backward.7 = (bf16[2048,384]{1,0:T(8,128)(2,1)}, f32[1,512]{1,0:T(1,128)}, f32[4,64,1024]{2,1,0:T(8,128)}) custom-call(s32[1]{0:T(128)} %bitcast.me_ref, s32[1,8]{1,0:T(1,128)} %len_ref.11, bf16[2048,768]{1,0:T(8,128)(2,1)} %qkv_part.3.q_ref.k_ref.v_ref, bf16[2048,768]{1,0:T(8,128)(2,1)} %qkv_part.3.q_ref.k_ref.v_ref, ...), custom_call_target="tpu_custom_call" | custom-call | flops 80000000000 | bytes 288000000 | tf_op jit(solution)/shard_map/attend_backward/pallas_call | solution.py:298
  300.0 6.8 %gradient.7 = (bf16[512,384]{1,0:T(8,128)(2,1)}, bf16[512,384]{1,0:T(8,128)(2,1)}, f32[8,1024]{1,0:T(8,128)}) custom-call(s32[1]{0:T(128)} %bitcast.11.me_ref.side_ref, bf16[512,1024]{1,0:T(8,128)(2,1)} %first_norm.1.refs_0_.refs_3_, bf16[512,1024]{1,0:T(8,128)(2,1)} %copy-done.35, bf16[512,1024]{1,0:T(8,128)(2,1)} %copy-done.36, ...), custom_call_target="tpu_custom_call" | custom-call | flops 40000000000 | bytes 144000000 | tf_op jit(solution)/shard_map/gradient/pallas_call | solution.py:844
  310.8 3.3 all-to-all-start
  314.1 4.6 %products.5 = (bf16[512,1024]{1,0:T(8,128)(2,1)}, bf16[512,1024]{1,0:T(8,128)(2,1)}) custom-call(bf16[2048,384]{1,0:T(8,128)(2,1)} %get-tuple-element.322.refs_7_.refs_0_, bf16[2048,384]{1,0:T(8,128)(2,1)} %get-tuple-element.323.refs_4_.refs_1_, bf16[1024,256]{1,0:T(8,128)(2,1)} %refs_2_.11, bf16[1024,256]{1,0:T(8,128)(2,1)} %refs_3_.12, ...), custom_call_target="tpu_custom_call" | custom-call | flops 20000000000 | bytes 72000000 | tf_op jit(solution)/shard_map/products/pallas_call | solution.py:723
  321.2 4.6 %products.6 = (bf16[512,1024]{1,0:T(8,128)(2,1)}, bf16[512,1024]{1,0:T(8,128)(2,1)}) custom-call(bf16[2048,384]{1,0:T(8,128)(2,1)} %get-tuple-element.322.refs_7_.refs_0_, bf16[2048,384]{1,0:T(8,128)(2,1)} %get-tuple-element.323.refs_4_.refs_1_, bf16[1024,256]{1,0:T(8,128)(2,1)} %refs_2_.11, bf16[1024,256]{1,0:T(8,128)(2,1)} %refs_3_.12, ...), custom_call_target="tpu_custom_call" | custom-call | flops 20000000000 | bytes 72000000 | tf_op jit(solution)/shard_map/products/pallas_call | solution.py:723
  329.1 3.8 assemble.3
  334.8 2.5 collective-permute-start.51
  340.6 4.9 %collective-permute-done.51 = bf16[128,384]{1,0:T(8,128)(2,1)S(1)} collective-permute-done((bf16[128,384]{1,0:T(8,128)(2,1)S(1)}, bf16[128,384]{1,0:T(8,128)(2,1)S(1)}, u32[]{:S(2)}, u32[]{:S(2)}) %collective-permute-start.51) | collective-permute-done | bytes 98336 | tf_op jit(solution)/shard_map/ppermute | solution.py:889
  348.6 2.4 collective-permute-done.55
  353.5 3.7 all-to-all-start.1
  360.9 5.5 %products.7 = (bf16[512,1024]{1,0:T(8,128)(2,1)}, bf16[512,1024]{1,0:T(8,128)(2,1)}) custom-call(bf16[2048,1024]{1,0:T(8,128)(2,1)} %get-tuple-element.343.refs_0_, bf16[1024,1024]{1,0:T(8,128)(2,1)} %refs_1_.3), custom_call_target="tpu_custom_call" | custom-call | tf_op jit(solution)/shard_map/products/pallas_call | solution.py:723
  366.6 4.9 %last_norm.1 = f32[512,1024]{1,0:T(8,128)} custom-call(bf16[512,1024]{1,0:T(8,128)(2,1)} %get-tuple-element.324.refs_0_, bf16[512,1024]{1,0:T(8,128)(2,1)} %collective-permute-done.56.refs_1_, bf16[512,1024]{1,0:T(8,128)(2,1)} %collective-permute-done.57.refs_2_, bf16[512,1024]{1,0:T(8,128)(2,1)} %refs_3_.13, f32[512,1024]{1,0:T(8,128)} %get-tuple-element.347.refs_4_, ...), custom_call_target="tpu_custom_call" | custom-call | flops 20000000000 | bytes 72000000 | tf_op jit(solution)/shard_map/last_norm/pallas_call | solution.py:516
  371.6 3.0 add_convert_fusion
  374.6 3.8 assemble.4
  380.9 8.1 %collective-permute-done.61.refs_1_ = bf16[512,1024]{1,0:T(8,128)(2,1)} collective-permute-done((bf16[512,1024]{1,0:T(8,128)(2,1)S(1)}, bf16[512,1024]{1,0:T(8,128)(2,1)}, u32[]{:S(2)}, u32[]{:S(2)}) %collective-permute-start.61) | collective-permute-done | bytes 1048608 | tf_op jit(solution)/shard_map/ppermute | solution.py:889
  389.0 3.8 assemble.5
  (294 shorter events, 87.2 us)
Async XLA Ops:
  4.2 26.5 %collective-permute-start = (bf16[512,1024]{1,0:T(8,128)(2,1)}, bf16[512,1024]{1,0:T(8,128)(2,1)S(1)}, u32[]{:S(2)}, u32[]{:S(2)}) collective-permute-start(bf16[512,1024]{1,0:T(8,128)(2,1)} %first_norm.1.refs_0_.refs_3_), channel_id=1, source_target_pairs={{0,2},{1,3},{2,0},{3,1},{4,6},{5,7},{6,4},{7,5},{8,10},{9,11},{10,... | collective-permute-start | bytes 3145736 | tf_op jit(solution)/shard_map/ppermute | solution.py:889
  8.8 8.0 %collective-permute-start.2 = (bf16[512,1024]{1,0:T(8,128)(2,1)S(1)}, bf16[512,1024]{1,0:T(8,128)(2,1)S(1)}, u32[]{:S(2)}, u32[]{:S(2)}) collective-permute-start(bf16[512,1024]{1,0:T(8,128)(2,1)S(1)} %broadcast_select_fusion.refs_0_.refs_1_.refs_5_), channel_id=1, source_target_pairs={{0,1},{1,0},{2,3},{3,2},{4,5},{5,4},{6,7},{7,6},{8,9},{9,8},{10,11... | collective-permute-start | bytes 3145736 | tf_op jit(solution)/shard_map/ppermute | solution.py:889
  14.7 16.0 %collective-permute-start.3 = (bf16[256,1024]{1,0:T(8,128)(2,1)S(1)}, bf16[256,1024]{1,0:T(8,128)(2,1)S(1)}, u32[]{:S(2)}, u32[]{:S(2)}) collective-permute-start(bf16[256,1024]{1,0:T(8,128)(2,1)S(1)} %copy-done.15), channel_id=1, source_target_pairs={{0,1},{1,0},{2,3},{3,2},{4,5},{5,4},{6,7},{7,6},{8,9},{9,8},{10,11... | collective-permute-start | bytes 1572872 | tf_op jit(solution)/shard_map/ppermute | solution.py:889
  32.3 42.3 %collective-permute-start.11 = (bf16[768,1024]{1,0:T(8,128)(2,1)}, bf16[768,1024]{1,0:T(8,128)(2,1)}, u32[]{:S(2)}, u32[]{:S(2)}) collective-permute-start(bf16[768,1024]{1,0:T(8,128)(2,1)} %constant_dynamic-update-slice_fusion), channel_id=1, source_target_pairs={{0,2},{1,3},{2,0},{3,1},{4,6},{5,7},{6,4},{7,5},{8,10},{9,11},{10,... | collective-permute-start | bytes 4718600 | tf_op jit(solution)/shard_map/ppermute | solution.py:889
  54.2 16.0 %collective-permute-start.5 = (bf16[512,128]{1,0:T(8,128)(2,1)}, bf16[512,128]{1,0:T(8,128)(2,1)S(1)}, u32[]{:S(2)}, u32[]{:S(2)}) collective-permute-start(bf16[512,128]{1,0:T(8,128)(2,1)} %get-tuple-element.200), channel_id=1, source_target_pairs={{0,1},{1,0},{2,3},{3,2},{4,5},{5,4},{6,7},{7,6},{8,9},{9,8},{10,11... | collective-permute-start | bytes 393224 | tf_op jit(solution)/shard_map/ppermute | solution.py:889
  54.3 18.2 %collective-permute-start.6 = (bf16[512,128]{1,0:T(8,128)(2,1)}, bf16[512,128]{1,0:T(8,128)(2,1)S(1)}, u32[]{:S(2)}, u32[]{:S(2)}) collective-permute-start(bf16[512,128]{1,0:T(8,128)(2,1)} %get-tuple-element.201), channel_id=1, source_target_pairs={{0,2},{1,3},{2,0},{3,1},{4,6},{5,7},{6,4},{7,5},{8,10},{9,11},{10,... | collective-permute-start | bytes 393224 | tf_op jit(solution)/shard_map/ppermute | solution.py:889
  56.1 18.4 %collective-permute-start.7 = (bf16[512,128]{1,0:T(8,128)(2,1)}, bf16[512,128]{1,0:T(8,128)(2,1)S(1)}, u32[]{:S(2)}, u32[]{:S(2)}) collective-permute-start(bf16[512,128]{1,0:T(8,128)(2,1)} %get-tuple-element.202), channel_id=1, source_target_pairs={{0,3},{1,2},{2,1},{3,0},{4,7},{5,6},{6,5},{7,4},{8,11},{9,10},{10,... | collective-permute-start | bytes 393224 | tf_op jit(solution)/shard_map/ppermute | solution.py:889
  74.6 9.0 %collective-permute-start.12 = (bf16[768,1024]{1,0:T(8,128)(2,1)}, bf16[768,1024]{1,0:T(8,128)(2,1)S(1)}, u32[]{:S(2)}, u32[]{:S(2)}) collective-permute-start(bf16[768,1024]{1,0:T(8,128)(2,1)} %collective-permute-done.11.refs_10_.refs_0_.refs_3_.refs_11_), channel_id=1, source_target_pairs={{0,1},{1,0},{2,3},{3,2},{4,5},{5,4},{6,7},{7,6},{8,9},{9,8},{10,11... | collective-permute-start | bytes 4718600 | tf_op jit(solution)/shard_map/ppermute | solution.py:889
  76.4 7.2 %collective-permute-start.9 = (bf16[512,128]{1,0:T(8,128)(2,1)}, bf16[512,128]{1,0:T(8,128)(2,1)S(1)}, u32[]{:S(2)}, u32[]{:S(2)}) collective-permute-start(bf16[512,128]{1,0:T(8,128)(2,1)} %get-tuple-element.207), channel_id=1, source_target_pairs={{0,2},{1,3},{2,0},{3,1},{4,6},{5,7},{6,4},{7,5},{8,10},{9,11},{10,... | collective-permute-start | bytes 393224 | tf_op jit(solution)/shard_map/ppermute | solution.py:889
  91.0 25.8 %collective-permute-start.14 = (bf16[512,1024]{1,0:T(8,128)(2,1)}, bf16[512,1024]{1,0:T(8,128)(2,1)S(1)}, u32[]{:S(2)}, u32[]{:S(2)}) collective-permute-start(bf16[512,1024]{1,0:T(8,128)(2,1)} %get-tuple-element.213.refs_0_), channel_id=1, source_target_pairs={{0,2},{1,3},{2,0},{3,1},{4,6},{5,7},{6,4},{7,5},{8,10},{9,11},{10,... | collective-permute-start | bytes 3145736 | tf_op jit(solution)/shard_map/ppermute | solution.py:889
  149.6 13.9 %collective-permute-start.22 = (bf16[512,1024]{1,0:T(8,128)(2,1)}, bf16[512,1024]{1,0:T(8,128)(2,1)S(1)}, u32[]{:S(2)}, u32[]{:S(2)}) collective-permute-start(bf16[512,1024]{1,0:T(8,128)(2,1)} %get-tuple-element.228), channel_id=1, source_target_pairs={{0,1},{1,0},{2,3},{3,2},{4,5},{5,4},{6,7},{7,6},{8,9},{9,8},{10,11... | collective-permute-start | bytes 3145736 | tf_op jit(solution)/shard_map/ppermute | solution.py:889
  161.8 24.1 %collective-permute-start.23 = (bf16[512,1024]{1,0:T(8,128)(2,1)}, bf16[512,1024]{1,0:T(8,128)(2,1)S(1)}, u32[]{:S(2)}, u32[]{:S(2)}) collective-permute-start(bf16[512,1024]{1,0:T(8,128)(2,1)} %get-tuple-element.236), channel_id=1, source_target_pairs={{0,1},{1,0},{2,3},{3,2},{4,5},{5,4},{6,7},{7,6},{8,9},{9,8},{10,11... | collective-permute-start | bytes 3145736 | tf_op jit(solution)/shard_map/ppermute | solution.py:889
  163.9 25.4 %collective-permute-start.24 = (bf16[512,1024]{1,0:T(8,128)(2,1)S(1)}, bf16[512,1024]{1,0:T(8,128)(2,1)S(1)}, u32[]{:S(2)}, u32[]{:S(2)}) collective-permute-start(bf16[512,1024]{1,0:T(8,128)(2,1)S(1)} %add_convert_fusion.5), channel_id=1, source_target_pairs={{0,2},{1,3},{2,0},{3,1},{4,6},{5,7},{6,4},{7,5},{8,10},{9,11},{10,... | collective-permute-start | bytes 3145736 | tf_op jit(solution)/shard_map/ppermute | solution.py:889
  173.7 26.2 %collective-permute-start.25 = (bf16[512,1024]{1,0:T(8,128)(2,1)}, bf16[512,1024]{1,0:T(8,128)(2,1)S(1)}, u32[]{:S(2)}, u32[]{:S(2)}) collective-permute-start(bf16[512,1024]{1,0:T(8,128)(2,1)} %get-tuple-element.232), channel_id=1, source_target_pairs={{0,4},{4,0},{8,12},{12,8},{16,20},{20,16},{24,28},{28,24},{1,5},{5... | collective-permute-start | bytes 3145736 | tf_op jit(solution)/shard_map/ppermute | solution.py:889
  184.3 29.3 %collective-permute-start.29 = (bf16[512,1024]{1,0:T(8,128)(2,1)}, bf16[512,1024]{1,0:T(8,128)(2,1)S(1)}, u32[]{:S(2)}, u32[]{:S(2)}) collective-permute-start(bf16[512,1024]{1,0:T(8,128)(2,1)} %get-tuple-element.234), channel_id=1, source_target_pairs={{0,8},{4,12},{8,0},{12,4},{16,24},{20,28},{24,16},{28,20},{1,9},{5... | collective-permute-start | bytes 3145736 | tf_op jit(solution)/shard_map/ppermute | solution.py:889
  199.9 15.8 %collective-permute-start.32 = (bf16[512,256]{1,0:T(8,128)(2,1)}, bf16[512,256]{1,0:T(8,128)(2,1)S(1)}, u32[]{:S(2)}, u32[]{:S(2)}) collective-permute-start(bf16[512,256]{1,0:T(8,128)(2,1)} %get-tuple-element.264), channel_id=1, source_target_pairs={{0,2},{1,3},{2,0},{3,1},{4,6},{5,7},{6,4},{7,5},{8,10},{9,11},{10,... | collective-permute-start | bytes 786440 | tf_op jit(solution)/shard_map/ppermute | solution.py:889
  200.6 15.2 %collective-permute-start.28 = (bf16[512,256]{1,0:T(8,128)(2,1)}, bf16[512,256]{1,0:T(8,128)(2,1)S(1)}, u32[]{:S(2)}, u32[]{:S(2)}) collective-permute-start(bf16[512,256]{1,0:T(8,128)(2,1)} %get-tuple-element.249), channel_id=1, source_target_pairs={{0,3},{1,2},{2,1},{3,0},{4,7},{5,6},{6,5},{7,4},{8,11},{9,10},{10,... | collective-permute-start | bytes 786440 | tf_op jit(solution)/shard_map/ppermute | solution.py:889
  202.3 18.1 %collective-permute-start.31 = (bf16[256,1024]{1,0:T(8,128)(2,1)S(1)}, bf16[256,1024]{1,0:T(8,128)(2,1)S(1)}, u32[]{:S(2)}, u32[]{:S(2)}) collective-permute-start(bf16[256,1024]{1,0:T(8,128)(2,1)S(1)} %get-tuple-element.367), channel_id=1, source_target_pairs={{0,8},{4,12},{8,0},{12,4},{16,24},{20,28},{24,16},{28,20},{1,9},{5... | collective-permute-start | bytes 1572872 | tf_op jit(solution)/shard_map/ppermute | solution.py:889
  207.9 8.0 %collective-permute-start.27 = (bf16[2048,256]{1,0:T(8,128)(2,1)}, bf16[2048,256]{1,0:T(8,128)(2,1)S(1)}, u32[]{:S(2)}, u32[]{:S(2)}) collective-permute-start(bf16[2048,256]{1,0:T(8,128)(2,1)} %get-tuple-element.247), channel_id=1, source_target_pairs={{0,1},{1,0},{2,3},{3,2},{4,5},{5,4},{6,7},{7,6},{8,9},{9,8},{10,11... | collective-permute-start | bytes 3145736 | tf_op jit(solution)/shard_map/ppermute | solution.py:889
  214.2 23.6 %collective-permute-start.34 = (bf16[256,1024]{1,0:T(8,128)(2,1)S(1)}, bf16[256,1024]{1,0:T(8,128)(2,1)S(1)}, u32[]{:S(2)}, u32[]{:S(2)}) collective-permute-start(bf16[256,1024]{1,0:T(8,128)(2,1)S(1)} %get-tuple-element.365), channel_id=1, source_target_pairs={{0,4},{4,0},{8,12},{12,8},{16,20},{20,16},{24,28},{28,24},{1,5},{5... | collective-permute-start | bytes 1572872 | tf_op jit(solution)/shard_map/ppermute | solution.py:889
  215.8 25.2 %collective-permute-start.35 = (bf16[512,1024]{1,0:T(8,128)(2,1)S(1)}, bf16[512,1024]{1,0:T(8,128)(2,1)S(1)}, u32[]{:S(2)}, u32[]{:S(2)}) collective-permute-start(bf16[512,1024]{1,0:T(8,128)(2,1)S(1)} %copy-done.42), channel_id=1, source_target_pairs={{0,1},{1,0},{2,3},{3,2},{4,5},{5,4},{6,7},{7,6},{8,9},{9,8},{10,11... | collective-permute-start | bytes 3145736 | tf_op jit(solution)/shard_map/ppermute | solution.py:889
  220.7 16.9 %collective-permute-start.33 = (bf16[128,1024]{1,0:T(8,128)(2,1)S(1)}, bf16[128,1024]{1,0:T(8,128)(2,1)S(1)}, u32[]{:S(2)}, u32[]{:S(2)}) collective-permute-start(bf16[128,1024]{1,0:T(8,128)(2,1)S(1)} %get-tuple-element.379), channel_id=1, source_target_pairs={{0,16},{4,20},{8,24},{12,28},{16,0},{20,4},{24,8},{28,12},{1,17},{... | collective-permute-start | bytes 786440 | tf_op jit(solution)/shard_map/ppermute | solution.py:889
  223.3 32.8 %collective-permute-start.30 = (bf16[1024,256]{1,0:T(8,128)(2,1)}, bf16[1024,256]{1,0:T(8,128)(2,1)}, u32[]{:S(2)}, u32[]{:S(2)}) collective-permute-start(bf16[1024,256]{1,0:T(8,128)(2,1)} %add_convert_fusion.9), channel_id=1, source_target_pairs={{0,2},{1,3},{2,0},{3,1},{4,6},{5,7},{6,4},{7,5},{8,10},{9,11},{10,... | collective-permute-start | bytes 1572872 | tf_op jit(solution)/shard_map/ppermute | solution.py:889
  237.7 18.6 %collective-permute-start.36 = (bf16[128,1024]{1,0:T(8,128)(2,1)S(1)}, bf16[128,1024]{1,0:T(8,128)(2,1)S(1)}, u32[]{:S(2)}, u32[]{:S(2)}) collective-permute-start(bf16[128,1024]{1,0:T(8,128)(2,1)S(1)} %add_convert_fusion.13), channel_id=1, source_target_pairs={{0,16},{4,20},{8,24},{12,28},{16,0},{20,4},{24,8},{28,12},{1,17},{... | collective-permute-start | bytes 786440 | tf_op jit(solution)/shard_map/ppermute | solution.py:889
  238.0 25.8 %collective-permute-start.38 = (bf16[128,1024]{1,0:T(8,128)(2,1)S(1)}, bf16[128,1024]{1,0:T(8,128)(2,1)S(1)}, u32[]{:S(2)}, u32[]{:S(2)}) collective-permute-start(bf16[128,1024]{1,0:T(8,128)(2,1)S(1)} %get-tuple-element.375), channel_id=1, source_target_pairs={{0,16},{4,20},{8,24},{12,28},{16,0},{20,4},{24,8},{28,12},{1,17},{... | collective-permute-start | bytes 786440 | tf_op jit(solution)/shard_map/ppermute | solution.py:889
  242.4 56.1 %collective-permute-start.41 = (bf16[512,1024]{1,0:T(8,128)(2,1)}, bf16[512,1024]{1,0:T(8,128)(2,1)}, u32[]{:S(2)}, u32[]{:S(2)}) collective-permute-start(bf16[512,1024]{1,0:T(8,128)(2,1)} %add_convert_fusion.2), channel_id=1, source_target_pairs={{0,2},{1,3},{2,0},{3,1},{4,6},{5,7},{6,4},{7,5},{8,10},{9,11},{10,... | collective-permute-start | bytes 3145736 | tf_op jit(solution)/shard_map/ppermute | solution.py:889
  263.9 14.8 %collective-permute-start.39 = (bf16[128,1024]{1,0:T(8,128)(2,1)S(1)}, bf16[128,1024]{1,0:T(8,128)(2,1)S(1)}, u32[]{:S(2)}, u32[]{:S(2)}) collective-permute-start(bf16[128,1024]{1,0:T(8,128)(2,1)S(1)} %add_convert_fusion.12), channel_id=1, source_target_pairs={{0,16},{4,20},{8,24},{12,28},{16,0},{20,4},{24,8},{28,12},{1,17},{... | collective-permute-start | bytes 786440 | tf_op jit(solution)/shard_map/ppermute | solution.py:889
  263.9 19.4 %collective-permute-start.37 = (bf16[256,1024]{1,0:T(8,128)(2,1)S(1)}, bf16[256,1024]{1,0:T(8,128)(2,1)S(1)}, u32[]{:S(2)}, u32[]{:S(2)}) collective-permute-start(bf16[256,1024]{1,0:T(8,128)(2,1)S(1)} %pad_maximum_fusion.3), channel_id=1, source_target_pairs={{0,8},{4,12},{8,0},{12,4},{16,24},{20,28},{24,16},{28,20},{1,9},{5... | collective-permute-start | bytes 1572872 | tf_op jit(solution)/shard_map/ppermute | solution.py:889
  265.9 18.6 %collective-permute-start.40 = (bf16[512,640]{1,0:T(8,128)(2,1)}, bf16[512,640]{1,0:T(8,128)(2,1)S(1)}, u32[]{:S(2)}, u32[]{:S(2)}) collective-permute-start(bf16[512,640]{1,0:T(8,128)(2,1)} %get-tuple-element.285), channel_id=1, source_target_pairs={{0,4},{4,0},{8,12},{12,8},{16,20},{20,16},{24,28},{28,24},{1,5},{5... | collective-permute-start | bytes 1966088 | tf_op jit(solution)/shard_map/ppermute | solution.py:889
  279.6 53.3 %collective-permute-start.48 = (bf16[256,1024]{1,0:T(8,128)(2,1)}, bf16[256,1024]{1,0:T(8,128)(2,1)}, u32[]{:S(2)}, u32[]{:S(2)}) collective-permute-start(bf16[256,1024]{1,0:T(8,128)(2,1)} %pad_maximum_fusion.4), channel_id=1, source_target_pairs={{0,4},{4,0},{8,12},{12,8},{16,20},{20,16},{24,28},{28,24},{1,5},{5... | collective-permute-start | bytes 1572872 | tf_op jit(solution)/shard_map/ppermute | solution.py:889
  284.5 44.6 %collective-permute-start.49 = (bf16[512,1024]{1,0:T(8,128)(2,1)}, bf16[512,1024]{1,0:T(8,128)(2,1)}, u32[]{:S(2)}, u32[]{:S(2)}) collective-permute-start(bf16[512,1024]{1,0:T(8,128)(2,1)} %pad_maximum_fusion.refs_0_), channel_id=1, source_target_pairs={{0,4},{4,0},{8,12},{12,8},{16,20},{20,16},{24,28},{28,24},{1,5},{5... | collective-permute-start | bytes 3145736 | tf_op jit(solution)/shard_map/ppermute | solution.py:889
  284.8 13.7 %collective-permute-start.42 = (bf16[256,640]{1,0:T(8,128)(2,1)S(1)}, bf16[256,640]{1,0:T(8,128)(2,1)S(1)}, u32[]{:S(2)}, u32[]{:S(2)}) collective-permute-start(bf16[256,640]{1,0:T(8,128)(2,1)S(1)} %get-tuple-element.371), channel_id=1, source_target_pairs={{0,8},{4,12},{8,0},{12,4},{16,24},{20,28},{24,16},{28,20},{1,9},{5... | collective-permute-start | bytes 983048 | tf_op jit(solution)/shard_map/ppermute | solution.py:889
  298.6 11.2 %collective-permute-start.43 = (bf16[128,640]{1,0:T(8,128)(2,1)S(1)}, bf16[128,640]{1,0:T(8,128)(2,1)S(1)}, u32[]{:S(2)}, u32[]{:S(2)}) collective-permute-start(bf16[128,640]{1,0:T(8,128)(2,1)S(1)} %get-tuple-element.391), channel_id=1, source_target_pairs={{0,16},{4,20},{8,24},{12,28},{16,0},{20,4},{24,8},{28,12},{1,17},{... | collective-permute-start | bytes 491528 | tf_op jit(solution)/shard_map/ppermute | solution.py:889
  306.9 20.3 %collective-permute-start.46 = (bf16[512,384]{1,0:T(8,128)(2,1)}, bf16[512,384]{1,0:T(8,128)(2,1)S(1)}, u32[]{:S(2)}, u32[]{:S(2)}) collective-permute-start(bf16[512,384]{1,0:T(8,128)(2,1)} %get-tuple-element.312), channel_id=1, source_target_pairs={{0,4},{4,0},{8,12},{12,8},{16,20},{20,16},{24,28},{28,24},{1,5},{5... | collective-permute-start | bytes 1179656 | tf_op jit(solution)/shard_map/ppermute | solution.py:889
  310.5 8.8 %collective-permute-start.45 = (bf16[128,640]{1,0:T(8,128)(2,1)S(1)}, bf16[128,640]{1,0:T(8,128)(2,1)S(1)}, u32[]{:S(2)}, u32[]{:S(2)}) collective-permute-start(bf16[128,640]{1,0:T(8,128)(2,1)S(1)} %add_convert_fusion.14), channel_id=1, source_target_pairs={{0,16},{4,20},{8,24},{12,28},{16,0},{20,4},{24,8},{28,12},{1,17},{... | collective-permute-start | bytes 491528 | tf_op jit(solution)/shard_map/ppermute | solution.py:889
  310.8 37.8 %all-to-all-start = ((f32[4,8,1024]{2,1,0:T(8,128)}), f32[4,8,1024]{2,1,0:T(8,128)S(1)}, u32[]{:S(2)}, u32[]{:S(2)}) async-start(f32[4,8,1024]{2,1,0:T(8,128)} %broadcast_in_dim.96), calls=%async_computation | async-start | bytes 262144 | tf_op jit(solution)/shard_map/all_to_all | solution.py:1238
  318.8 7.0 %collective-permute-start.44 = (bf16[512,1024]{1,0:T(8,128)(2,1)}, bf16[512,1024]{1,0:T(8,128)(2,1)S(1)}, u32[]{:S(2)}, u32[]{:S(2)}) collective-permute-start(bf16[512,1024]{1,0:T(8,128)(2,1)} %get-tuple-element.319), channel_id=1, source_target_pairs={{0,1},{1,0},{2,3},{3,2},{4,5},{5,4},{6,7},{7,6},{8,9},{9,8},{10,11... | collective-permute-start | bytes 3145736 | tf_op jit(solution)/shard_map/ppermute | solution.py:889
  319.3 15.0 %collective-permute-start.47 = (bf16[256,640]{1,0:T(8,128)(2,1)S(1)}, bf16[256,640]{1,0:T(8,128)(2,1)S(1)}, u32[]{:S(2)}, u32[]{:S(2)}) collective-permute-start(bf16[256,640]{1,0:T(8,128)(2,1)S(1)} %pad_maximum_fusion.6), channel_id=1, source_target_pairs={{0,8},{4,12},{8,0},{12,4},{16,24},{20,28},{24,16},{28,20},{1,9},{5... | collective-permute-start | bytes 983048 | tf_op jit(solution)/shard_map/ppermute | solution.py:889
  325.8 40.8 %collective-permute-start.56 = (bf16[512,1024]{1,0:T(8,128)(2,1)}, bf16[512,1024]{1,0:T(8,128)(2,1)}, u32[]{:S(2)}, u32[]{:S(2)}) collective-permute-start(bf16[512,1024]{1,0:T(8,128)(2,1)} %get-tuple-element.345), channel_id=1, source_target_pairs={{0,1},{1,0},{2,3},{3,2},{4,5},{5,4},{6,7},{7,6},{8,9},{9,8},{10,11... | collective-permute-start | bytes 3145736 | tf_op jit(solution)/shard_map/ppermute | solution.py:889
  327.2 39.4 %collective-permute-start.57 = (bf16[512,1024]{1,0:T(8,128)(2,1)}, bf16[512,1024]{1,0:T(8,128)(2,1)}, u32[]{:S(2)}, u32[]{:S(2)}) collective-permute-start(bf16[512,1024]{1,0:T(8,128)(2,1)} %add_convert_fusion.1), channel_id=1, source_target_pairs={{0,2},{1,3},{2,0},{3,1},{4,6},{5,7},{6,4},{7,5},{8,10},{9,11},{10,... | collective-permute-start | bytes 3145736 | tf_op jit(solution)/shard_map/ppermute | solution.py:889
  334.8 10.8 %collective-permute-start.51 = (bf16[128,384]{1,0:T(8,128)(2,1)S(1)}, bf16[128,384]{1,0:T(8,128)(2,1)S(1)}, u32[]{:S(2)}, u32[]{:S(2)}) collective-permute-start(bf16[128,384]{1,0:T(8,128)(2,1)S(1)} %get-tuple-element.385), channel_id=1, source_target_pairs={{0,16},{4,20},{8,24},{12,28},{16,0},{20,4},{24,8},{28,12},{1,17},{... | collective-permute-start | bytes 294920 | tf_op jit(solution)/shard_map/ppermute | solution.py:889
  337.2 8.3 %collective-permute-start.52 = (bf16[128,384]{1,0:T(8,128)(2,1)S(1)}, bf16[128,384]{1,0:T(8,128)(2,1)S(1)}, u32[]{:S(2)}, u32[]{:S(2)}) collective-permute-start(bf16[128,384]{1,0:T(8,128)(2,1)S(1)} %get-tuple-element.386), channel_id=1, source_target_pairs={{0,24},{4,28},{8,16},{12,20},{16,8},{20,12},{24,0},{28,4},{1,25},{... | collective-permute-start | bytes 294920 | tf_op jit(solution)/shard_map/ppermute | solution.py:889
  340.6 25.9 %collective-permute-start.58 = (bf16[512,640]{1,0:T(8,128)(2,1)S(1)}, bf16[512,640]{1,0:T(8,128)(2,1)S(1)}, u32[]{:S(2)}, u32[]{:S(2)}) collective-permute-start(bf16[512,640]{1,0:T(8,128)(2,1)S(1)} %pad_maximum_fusion.2.refs_0_), channel_id=1, source_target_pairs={{0,4},{4,0},{8,12},{12,8},{16,20},{20,16},{24,28},{28,24},{1,5},{5... | collective-permute-start | bytes 1966088 | tf_op jit(solution)/shard_map/ppermute | solution.py:889
  347.3 9.9 %collective-permute-start.54 = (bf16[128,384]{1,0:T(8,128)(2,1)S(1)}, bf16[128,384]{1,0:T(8,128)(2,1)S(1)}, u32[]{:S(2)}, u32[]{:S(2)}) collective-permute-start(bf16[128,384]{1,0:T(8,128)(2,1)S(1)} %add_convert_fusion.15), channel_id=1, source_target_pairs={{0,16},{4,20},{8,24},{12,28},{16,0},{20,4},{24,8},{28,12},{1,17},{... | collective-permute-start | bytes 294920 | tf_op jit(solution)/shard_map/ppermute | solution.py:889
  351.0 8.3 %collective-permute-start.53 = (bf16[128,384]{1,0:T(8,128)(2,1)S(1)}, bf16[128,384]{1,0:T(8,128)(2,1)S(1)}, u32[]{:S(2)}, u32[]{:S(2)}) collective-permute-start(bf16[128,384]{1,0:T(8,128)(2,1)S(1)} %add_convert_fusion.15), channel_id=1, source_target_pairs={{0,24},{4,28},{8,16},{12,20},{16,8},{20,12},{24,0},{28,4},{1,25},{... | collective-permute-start | bytes 294920 | tf_op jit(solution)/shard_map/ppermute | solution.py:889
  353.5 21.1 %all-to-all-start.1 = ((f32[8,16,1024]{2,1,0:T(8,128)}), f32[8,16,1024]{2,1,0:T(8,128)S(1)}, u32[]{:S(2)}, u32[]{:S(2)}) async-start(f32[8,16,1024]{2,1,0:T(8,128)} %broadcast_in_dim.97), calls=%async_computation.1 | async-start | bytes 1048576 | tf_op jit(solution)/shard_map/all_to_all | solution.py:1262
  357.2 31.8 %collective-permute-start.61 = (bf16[512,1024]{1,0:T(8,128)(2,1)S(1)}, bf16[512,1024]{1,0:T(8,128)(2,1)}, u32[]{:S(2)}, u32[]{:S(2)}) collective-permute-start(bf16[512,1024]{1,0:T(8,128)(2,1)S(1)} %pad_maximum_fusion.1.refs_0_), channel_id=1, source_target_pairs={{0,8},{4,12},{8,0},{12,4},{16,24},{20,28},{24,16},{28,20},{1,9},{5... | collective-permute-start | bytes 3145736 | tf_op jit(solution)/shard_map/ppermute | solution.py:889
  359.4 15.2 %collective-permute-start.60 = (bf16[512,384]{1,0:T(8,128)(2,1)S(1)}, bf16[512,384]{1,0:T(8,128)(2,1)}, u32[]{:S(2)}, u32[]{:S(2)}) collective-permute-start(bf16[512,384]{1,0:T(8,128)(2,1)S(1)} %pad_maximum_fusion.5.refs_1_), channel_id=1, source_target_pairs={{0,4},{4,0},{8,12},{12,8},{16,20},{20,16},{24,28},{28,24},{1,5},{5... | collective-permute-start | bytes 1179656 | tf_op jit(solution)/shard_map/ppermute | solution.py:889
  (75 other events, 470.9 us)

commit v2 on v1

--- a/solution.py
+++ b/solution.py
@@ -883,6 +883,35 @@
         cost_estimate=cost(0),
         name="assemble",
     )(side, *mine, *came)
+
+
+def place_half_kernel(side_ref, v_ref, *refs):
+    del side_ref
+    refs[-1][...] = v_ref[...].astype(F32)
+
+
+def place_half(side, v, earlier=None, steps=2):
+    size, n = v.shape
+    tile = size // steps
+    args, specs, aliases = [side, v], [pl.BlockSpec((tile, n), lambda t, side: (t, 0))], {}
+    if earlier is not None:
+        args.append(earlier)
+        specs.append(pl.BlockSpec(memory_space=pl.ANY))
+        aliases = {2: 0}
+    return pl.pallas_call(
+        place_half_kernel,
+        grid_spec=pltpu.PrefetchScalarGridSpec(
+            num_scalar_prefetch=1,
+            grid=(steps,),
+            in_specs=specs,
+            out_specs=pl.BlockSpec((tile, n), lambda t, side: (side[0] * steps + t, 0)),
+        ),
+        out_shape=shape((2 * size, n), F32),
+        input_output_aliases=aliases,
+        compiler_params=PARAMS,
+        cost_estimate=cost(0),
+        name="place_half",
+    )(*args)
 
 
 def swap(value, axis, size, bit):
@@ -1223,6 +1252,7 @@
     mark = after(mark, out_top)
     for stream in streams:
         mark = stream.advance(mark)
+    mark = fc1.advance(mark)
     joins = [*g_near_terms, g_out_top] if pairs == 1 else ()
     send, keep, r = gradient(
         side, normed, [after(dqkvs[-1], mark)], qkv_weights, pairs - 1, sums_att[-1], joins
@@ -1248,7 +1278,7 @@
     mark = last.advance(far_sum)
     fc2.done(mark)
     [grad_fc2_weight] = assemble(side, [after(fc2.held, mark)], [fc2.came], fc2.held.shape[1])
-    mark = fc1.advance(grad_fc2_weight)
+    mark = grad_fc2_weight
     for stream in streams:
         mark = stream.advance(mark)
     mark = last.advance(mark)
@@ -1278,9 +1308,9 @@
     grad_query_weight, grad_key_weight, grad_value_weight, grad_output_weight = assemble(
         side, [after(v.held, packed) for v in streams], [v.came for v in streams], PAIR, width
     )
-    [grad_fc1_weight] = assemble(
-        side_turned, [after(fc1.held, grad_query_weight)], [fc1.came], fc1.held.shape[1]
-    )
+    own_half = place_half(side_turned, after(fc1.held, grad_query_weight))
+    came = after(fc1.came, own_half)
+    grad_fc1_weight = place_half(1 - side_turned, came, own_half)
     shift1 = packed[7]
     gain1 = (packed[6] - norm1_shift * shift1) / norm1_gain
     per_head = packed[12, : 4 * width].reshape(pairs, 4, PAIR)

time: 397 us -> 397 us (level)
    pallas_call x0 -> x2, Pallas kernels: none -> 4.89 us  [place_half(): pl.pallas_call(place_half_kernel, grid_spec=pltpu.PrefetchScalarGridSpec(...]
    pallas_call x3 -> x2, Pallas kernels: 11.4 us -> 7.59 us  [assemble(): pl.pallas_call(functools.partial(assemble_kernel, len(mine), cols, turned...]
  transfers between devices with their start and end apart: 64 -> 64, of which waited for: 21 -> 20; matrix products, arithmetic and copies ran while one was open for 6% -> 5% of each run, Pallas kernels for 52% -> 52%
where the time goes in v2:
time: 397 us; the launch traced here: 392 us
  Pallas kernels  237 us (60%)
  starting transfers between devices  63 us (16%)
  waiting for transfers between devices  59 us (15%)
  other arithmetic  16.6 us (4%)
  local copies, waits for them, and re-layouts  15.2 us (4%)
    ppermute x62, waiting for transfers between devices, swap(): return lax.ppermute(value, axis, [(i, i ^ bit) for i in range(size)])  59 us
    ppermute x62, starting transfers between devices, swap(): return lax.ppermute(value, axis, [(i, i ^ bit) for i in range(size)])  56 us
    pallas_call x4, Pallas kernels, attend_backward(): pl.pallas_call(functools.partial(backward_kernel, tok, turn), grid=(1,),...  52.2 us
    pallas_call x4, Pallas kernels, gradient(): pl.pallas_call(functools.partial(gradient_kernel, steps, nl, nr, len(join...  32.6 us
    pallas_call x2, Pallas kernels, attend_forward(): pl.pallas_call(functools.partial(forward_kernel, tok), grid=(1,), out_sha...  28.1 us
    pallas_call x2, Pallas kernels, ffn_second(): pl.pallas_call(functools.partial(ffn_second_kernel, ndev, n, per), grid=(...  23.5 us
    pallas_call x4, Pallas kernels, products(): pl.pallas_call(functools.partial(products_kernel, len(xs), len(weights),...  20.4 us
    pallas_call x2, Pallas kernels, ffn_first(): pl.pallas_call(functools.partial(ffn_first_kernel, xp), grid=(rows // til...  16 us
  transfers between devices with their start and end apart: 64, of which 20 were waited for; matrix products, arithmetic and copies ran while one was open for 5% of the time, Pallas kernels for 52%

profile of v2, /device:TPU:0, one launch (start us, length us, event | category | flops | bytes accessed | tf_op | source)
XLA Modules:
  0.0 392.5 jit_solution(16510578923971955081)
XLA Ops:
  0.7 3.1 first_norm.1.refs_0_.refs_3_
  4.2 2.5 collective-permute-start
  9.8 4.9 %qkv_part.2.refs_6_ = bf16[2048,768]{1,0:T(8,128)(2,1)} custom-call(bf16[512,1024]{1,0:T(8,128)(2,1)} %first_norm.1.refs_0_.refs_3_, bf16[512,1024]{1,0:T(8,128)(2,1)} %copy-done.35, bf16[1024,256]{1,0:T(8,128)(2,1)} %refs_2_.11, bf16[1024,256]{1,0:T(8,128)(2,1)} %refs_3_.12, bf16[1024,256]{1,0:T(8,128)(2,1)} %refs_4_.11, f32[1,768]{1,0:T(1,128)} %broadcast_in_dim.84.refs_5_), custom_call_target="tpu_custom_call" | custom-call | flops 30000001024 | bytes 108000000 | tf_op jit(solution)/shard_map/qkv_part/pallas_call | solution.py:371
  17.8 6.9 %hidden_gradient.2.refs_2_.refs_1_ = f32[1024,1024]{1,0:T(8,128)} custom-call(bf16[512,1024]{1,0:T(8,128)(2,1)} %copy-done, bf16[512,1024]{1,0:T(8,128)(2,1)} %copy-done.38, bf16[1024,1024]{1,0:T(8,128)(2,1)} %refs_1_.3), custom_call_target="tpu_custom_call" | custom-call | flops 30000001024 | bytes 108000000 | tf_op jit(solution)/shard_map/hidden_gradient/pallas_call | solution.py:568
  24.7 6.0 %collective-permute-done.refs_0_.refs_5_.refs_2_ = bf16[512,1024]{1,0:T(8,128)(2,1)S(1)} collective-permute-done((bf16[512,1024]{1,0:T(8,128)(2,1)}, bf16[512,1024]{1,0:T(8,128)(2,1)S(1)}, u32[]{:S(2)}, u32[]{:S(2)}) %collective-permute-start) | collective-permute-done | bytes 1048608 | tf_op jit(solution)/shard_map/ppermute | solution.py:918
  35.2 4.9 %qkv_part.3.q_ref.k_ref.v_ref = bf16[2048,768]{1,0:T(8,128)(2,1)} custom-call(bf16[512,1024]{1,0:T(8,128)(2,1)} %copy-done.36, bf16[512,1024]{1,0:T(8,128)(2,1)} %copy-done.37, bf16[1024,256]{1,0:T(8,128)(2,1)} %refs_2_.11, bf16[1024,256]{1,0:T(8,128)(2,1)} %refs_3_.12, bf16[1024,256]{1,0:T(8,128)(2,1)} %refs_4_.11, ...), custom_call_target="tpu_custom_call", output_to_operand_aliasing={{}: (6, {})} | custom-call | flops 30000001024 | bytes 108000000 | tf_op jit(solution)/shard_map/qkv_part/pallas_call | solution.py:371
  40.2 14.0 %attend_forward.2 = (f32[2048,128]{1,0:T(8,128)}, f32[4,1,1024]{2,1,0:T(1,128)}, bf16[512,128]{1,0:T(8,128)(2,1)}, bf16[512,128]{1,0:T(8,128)(2,1)}, bf16[512,128]{1,0:T(8,128)(2,1)}, /*index=5*/bf16[512,128]{1,0:T(8,128)(2,1)}) custom-call(s32[1]{0:T(128)} %bitcast.me_ref, s32[1,8]{1,0:T(1,128)} %len_ref.11, bf16[2048,768]{1,0:T(8,128)(2,1)} %qkv_part.3.q_ref.k_ref.v_ref, ...), custom_call_target="tpu_custom_call" | custom-call | flops 80000000000 | bytes 288000000 | tf_op jit(solution)/shard_map/attend_forward/pallas_call | solution.py:162
  56.1 14.1 %attend_forward.3 = (f32[2048,128]{1,0:T(8,128)}, f32[4,1,1024]{2,1,0:T(1,128)}, bf16[512,128]{1,0:T(8,128)(2,1)}, bf16[512,128]{1,0:T(8,128)(2,1)}, bf16[512,128]{1,0:T(8,128)(2,1)}, /*index=5*/bf16[512,128]{1,0:T(8,128)(2,1)}) custom-call(s32[1]{0:T(128)} %bitcast.me_ref, s32[1,8]{1,0:T(1,128)} %len_ref.11, bf16[2048,768]{1,0:T(8,128)(2,1)} %qkv_part.3.q_ref.k_ref.v_ref, ...), custom_call_target="tpu_custom_call" | custom-call | flops 80000000000 | bytes 288000000 | tf_op jit(solution)/shard_map/attend_forward/pallas_call | solution.py:162
  76.7 3.8 collective-permute-done.10.refs_7_
  80.5 3.0 collective-permute-done.9.refs_5_
  84.8 6.1 %after_attention.1 = (f32[512,1024]{1,0:T(8,128)}, f32[512,1024]{1,0:T(8,128)}, bf16[512,1024]{1,0:T(8,128)(2,1)}) custom-call(bf16[512,128]{1,0:T(8,128)(2,1)} %get-tuple-element.198.refs_0_, bf16[512,128]{1,0:T(8,128)(2,1)} %get-tuple-element.204.refs_1_, bf16[512,128]{1,0:T(8,128)(2,1)} %copy-done.49, bf16[512,128]{1,0:T(8,128)(2,1)} %copy-done.54, ...), custom_call_target="tpu_custom_call" | custom-call | flops 30000001024 | bytes 108000000 | tf_op jit(solution)/shard_map/after_attention/pallas_call | solution.py:432
  94.9 8.0 %ffn_first.2 = (f32[1024,1024]{1,0:T(8,128)}, f32[8,1024]{1,0:T(8,128)}) custom-call(bf16[512,1024]{1,0:T(8,128)(2,1)} %get-tuple-element.214.refs_0_, bf16[512,1024]{1,0:T(8,128)(2,1)} %copy-done.39, f32[1024,1024]{1,0:T(8,128)} %hidden_gradient.2.refs_2_.refs_1_, bf16[1024,1024]{1,0:T(8,128)(2,1)} %refs_4_.9, f32[1,1024]{1,0:T(1,128)} %bitcast.50, ...), custom_call_target="tpu_custom_call" | custom-call | flops 49999998976 | bytes 180000000 | tf_op jit(solution)/shard_map/ffn_first/pallas_call | solution.py:609
  102.9 7.2 %hidden_gradient.3.refs_2_.refs_1_ = f32[1024,1024]{1,0:T(8,128)} custom-call(bf16[768,1024]{1,0:T(8,128)(2,1)} %collective-permute-done.11.refs_10_.refs_0_.refs_3_.refs_11_, bf16[768,1024]{1,0:T(8,128)(2,1)} %copy-done.34, bf16[1024,1024]{1,0:T(8,128)(2,1)} %refs_1_.3), custom_call_target="tpu_custom_call" | custom-call | flops 30000001024 | bytes 108000000 | tf_op jit(solution)/shard_map/hidden_gradient/pallas_call | solution.py:568
  110.0 6.7 %collective-permute-done.14.refs_0_.refs_2_ = bf16[512,1024]{1,0:T(8,128)(2,1)S(1)} collective-permute-done((bf16[512,1024]{1,0:T(8,128)(2,1)}, bf16[512,1024]{1,0:T(8,128)(2,1)S(1)}, u32[]{:S(2)}, u32[]{:S(2)}) %collective-permute-start.14) | collective-permute-done | bytes 1048608 | tf_op jit(solution)/shard_map/ppermute | solution.py:918
  123.1 8.0 %ffn_first.3 = (f32[1024,1024]{1,0:T(8,128)}, f32[8,1024]{1,0:T(8,128)}) custom-call(bf16[512,1024]{1,0:T(8,128)(2,1)} %copy-done.40, bf16[512,1024]{1,0:T(8,128)(2,1)} %copy-done.41, f32[1024,1024]{1,0:T(8,128)} %hidden_gradient.3.refs_2_.refs_1_, bf16[1024,1024]{1,0:T(8,128)(2,1)} %refs_4_.9, f32[1,1024]{1,0:T(1,128)} %bitcast.51, f32[1,1024]{1,0:T(1,128)} %bitcast.53), custom_call_target="tpu_custom_call" | custom-call | flops 49999998976 | bytes 180000000 | tf_op jit(solution)/shard_map/ffn_first/pallas_call | solution.py:609
  134.3 2.5 collective-permute-done.20.refs_7_
  137.9 11.7 %ffn_second.2 = (bf16[2048,1024]{1,0:T(8,128)(2,1)}, bf16[2048,1024]{1,0:T(8,128)(2,1)}, f32[8,1024]{1,0:T(8,128)}, bf16[512,1024]{1,0:T(8,128)(2,1)}, bf16[512,1024]{1,0:T(8,128)(2,1)}) custom-call(f32[1024,1024]{1,0:T(8,128)} %get-tuple-element.222.refs_0_, f32[1024,1024]{1,0:T(8,128)} %hidden_gradient.3.refs_2_.refs_1_, f32[1,1024]{1,0:T(1,128)} %bitcast.54, ...), custom_call_target="tpu_custom_call" | custom-call | flops 49999998976 | bytes 180000000 | tf_op jit(solution)/shard_map/ffn_second/pallas_call | solution.py:689
  150.0 11.8 %ffn_second.3 = (bf16[2048,1024]{1,0:T(8,128)(2,1)}, bf16[2048,1024]{1,0:T(8,128)(2,1)}, f32[8,1024]{1,0:T(8,128)}, bf16[512,1024]{1,0:T(8,128)(2,1)}, bf16[512,1024]{1,0:T(8,128)(2,1)}) custom-call(f32[1024,1024]{1,0:T(8,128)} %get-tuple-element.215.refs_0_, ...), custom_call_target="tpu_custom_call", output_to_operand_aliasing={{0}: (9, {}), {1}: (10, {})} | custom-call | flops 49999998976 | bytes 180000000 | tf_op jit(solution)/shard_map/ffn_second/pallas_call | solution.py:689
  164.7 8.9 %gradient.4 = (bf16[512,1024]{1,0:T(8,128)(2,1)}, bf16[512,1024]{1,0:T(8,128)(2,1)}) custom-call(s32[1]{0:T(128)} %bitcast.11.me_ref.side_ref, bf16[2048,1024]{1,0:T(8,128)(2,1)} %get-tuple-element.344.refs_0_, bf16[512,1024]{1,0:T(8,128)(2,1)} %copy-done, bf16[512,1024]{1,0:T(8,128)(2,1)} %copy-done.38, ...), custom_call_target="tpu_custom_call" | custom-call | flops 40000000000 | bytes 144000000 | tf_op jit(solution)/shard_map/gradient/pallas_call | solution.py:844
  175.2 9.1 %gradient.5 = (bf16[512,1024]{1,0:T(8,128)(2,1)}, bf16[512,1024]{1,0:T(8,128)(2,1)}) custom-call(s32[1]{0:T(128)} %bitcast.12.me_ref.side_ref, bf16[512,1024]{1,0:T(8,128)(2,1)} %get-tuple-element.214.refs_0_, bf16[512,1024]{1,0:T(8,128)(2,1)} %copy-done.39, bf16[512,1024]{1,0:T(8,128)(2,1)} %copy-done.40, bf16[512,1024]{1,0:T(8,128)(2,1)} %copy-done.41, ...), custom_call_target="tpu_custom_call" | custom-call | flops 40000000000 | bytes 144000000 | tf_op jit(solution)/shard_map/gradient/pallas_call | solution.py:844
  185.9 3.4 collective-permute-done.24.refs_2_
  190.3 9.6 %before_attention.1 = (f32[512,1024]{1,0:T(8,128)}, bf16[512,1024]{1,0:T(8,128)(2,1)}, f32[8,1024]{1,0:T(8,128)}, bf16[512,256]{1,0:T(8,128)(2,1)}, bf16[512,256...) custom-call(bf16[512,1024]{1,0:T(8,128)(2,1)} %get-tuple-element.236.refs_0_, ...), custom_call_target="tpu_custom_call" | custom-call | flops 30000001024 | bytes 108000000 | tf_op jit(solution)/shard_map/before_attention/pallas_call | solution.py:485
  203.9 4.0 %head_gradient.1 = (bf16[1024,256]{1,0:T(8,128)(2,1)}, bf16[1024,256]{1,0:T(8,128)(2,1)}, bf16[2048,256]{1,0:T(8,128)(2,1)}) custom-call(bf16[512,128]{1,0:T(8,128)(2,1)} %get-tuple-element.198.refs_0_, bf16[512,128]{1,0:T(8,128)(2,1)} %get-tuple-element.204.refs_1_, bf16[512,128]{1,0:T(8,128)(2,1)} %copy-done.49, bf16[512,128]{1,0:T(8,128)(2,1)} %copy-done.54, ...), custom_call_target="tpu_custom_call" | custom-call | flops 20000000000 | bytes 72000000 | tf_op jit(solution)/shard_map/head_gradient/pallas_call | solution.py:751
  208.1 5.6 %products.4 = (bf16[512,1024]{1,0:T(8,128)(2,1)}, bf16[512,1024]{1,0:T(8,128)(2,1)}) custom-call(bf16[2048,1024]{1,0:T(8,128)(2,1)} %get-tuple-element.344.refs_0_, bf16[1024,1024]{1,0:T(8,128)(2,1)} %refs_1_.3), custom_call_target="tpu_custom_call" | custom-call | flops 20000000000 | bytes 72000000 | tf_op jit(solution)/shard_map/products/pallas_call | solution.py:723
  217.2 3.2 collective-permute-done.31
  220.7 2.7 collective-permute-start.33
  224.8 12.8 %attend_backward.4 = (bf16[2,512,256]{2,1,0:T(8,128)(2,1)}, f32[1,512]{1,0:T(1,128)}, f32[4,64,1024]{2,1,0:T(8,128)}, f32[4,1,1024]{2,1,0:T(1,128)}) custom-call(s32[1]{0:T(128)} %bitcast.me_ref, s32[1,8]{1,0:T(1,128)} %len_ref.11, bf16[2048,768]{1,0:T(8,128)(2,1)} %qkv_part.3.q_ref.k_ref.v_ref, bf16[2048,768]{1,0:T(8,128)(2,1)} %qkv_part.3.q_ref.k_ref.v_ref, ...), custom_call_target="tpu_custom_call" | custom-call | flops 80000000000 | bytes 288000000 | tf_op jit(solution)/shard_map/attend_backward/pallas_call | solution.py:298
  238.0 3.0 collective-permute-start.38
  243.0 13.1 %attend_backward.5 = (bf16[2048,384]{1,0:T(8,128)(2,1)}, f32[1,512]{1,0:T(1,128)}, f32[4,64,1024]{2,1,0:T(8,128)}) custom-call(s32[1]{0:T(128)} %bitcast.me_ref, s32[1,8]{1,0:T(1,128)} %len_ref.11, bf16[2048,768]{1,0:T(8,128)(2,1)} %qkv_part.3.q_ref.k_ref.v_ref, bf16[2048,768]{1,0:T(8,128)(2,1)} %qkv_part.3.q_ref.k_ref.v_ref, ...), custom_call_target="tpu_custom_call" | custom-call | flops 80000000000 | bytes 288000000 | tf_op jit(solution)/shard_map/attend_backward/pallas_call | solution.py:298
  256.2 7.4 %gradient.6 = (bf16[512,640]{1,0:T(8,128)(2,1)}, bf16[512,640]{1,0:T(8,128)(2,1)}, f32[8,1024]{1,0:T(8,128)}) custom-call(s32[1]{0:T(128)} %bitcast.11.me_ref.side_ref, bf16[1024,256]{1,0:T(8,128)(2,1)} %get-tuple-element.247.refs_0_, bf16[2048,256]{1,0:T(8,128)(2,1)} %copy-done.17, bf16[1024,256]{1,0:T(8,128)(2,1)} %collective-permute-done.30.refs_2_, ...), custom_call_target="tpu_custom_call" | custom-call | flops 40000000000 | bytes 144000000 | tf_op jit(solution)/shard_map/gradient/pallas_call | solution.py:844
  265.9 12.8 %attend_backward.6 = (bf16[2,512,256]{2,1,0:T(8,128)(2,1)}, f32[1,512]{1,0:T(1,128)}, f32[4,64,1024]{2,1,0:T(8,128)}, f32[4,1,1024]{2,1,0:T(1,128)}) custom-call(s32[1]{0:T(128)} %bitcast.me_ref, s32[1,8]{1,0:T(1,128)} %len_ref.11, bf16[2048,768]{1,0:T(8,128)(2,1)} %qkv_part.3.q_ref.k_ref.v_ref, bf16[2048,768]{1,0:T(8,128)(2,1)} %qkv_part.3.q_ref.k_ref.v_ref, ...), custom_call_target="tpu_custom_call" | custom-call | flops 80000000000 | bytes 288000000 | tf_op jit(solution)/shard_map/attend_backward/pallas_call | solution.py:298
  278.9 4.3 %collective-permute-done.37 = bf16[256,1024]{1,0:T(8,128)(2,1)S(1)} collective-permute-done((bf16[256,1024]{1,0:T(8,128)(2,1)S(1)}, bf16[256,1024]{1,0:T(8,128)(2,1)S(1)}, u32[]{:S(2)}, u32[]{:S(2)}) %collective-permute-start.37) | collective-permute-done | bytes 524320 | tf_op jit(solution)/shard_map/ppermute | solution.py:918
  284.7 13.4 %attend_backward.7 = (bf16[2048,384]{1,0:T(8,128)(2,1)}, f32[1,512]{1,0:T(1,128)}, f32[4,64,1024]{2,1,0:T(8,128)}) custom-call(s32[1]{0:T(128)} %bitcast.me_ref, s32[1,8]{1,0:T(1,128)} %len_ref.11, bf16[2048,768]{1,0:T(8,128)(2,1)} %qkv_part.3.q_ref.k_ref.v_ref, bf16[2048,768]{1,0:T(8,128)(2,1)} %qkv_part.3.q_ref.k_ref.v_ref, ...), custom_call_target="tpu_custom_call" | custom-call | flops 80000000000 | bytes 288000000 | tf_op jit(solution)/shard_map/attend_backward/pallas_call | solution.py:298
  299.5 7.1 %gradient.7 = (bf16[512,384]{1,0:T(8,128)(2,1)}, bf16[512,384]{1,0:T(8,128)(2,1)}, f32[8,1024]{1,0:T(8,128)}) custom-call(s32[1]{0:T(128)} %bitcast.11.me_ref.side_ref, bf16[512,1024]{1,0:T(8,128)(2,1)} %first_norm.1.refs_0_.refs_3_, bf16[512,1024]{1,0:T(8,128)(2,1)} %copy-done.35, bf16[512,1024]{1,0:T(8,128)(2,1)} %copy-done.36, ...), custom_call_target="tpu_custom_call" | custom-call | flops 40000000000 | bytes 144000000 | tf_op jit(solution)/shard_map/gradient/pallas_call | solution.py:844
  310.8 3.3 all-to-all-start
  314.2 4.6 %products.5 = (bf16[512,1024]{1,0:T(8,128)(2,1)}, bf16[512,1024]{1,0:T(8,128)(2,1)}) custom-call(bf16[2048,384]{1,0:T(8,128)(2,1)} %get-tuple-element.325.refs_7_.refs_0_, bf16[2048,384]{1,0:T(8,128)(2,1)} %get-tuple-element.326.refs_4_.refs_1_, bf16[1024,256]{1,0:T(8,128)(2,1)} %refs_2_.11, bf16[1024,256]{1,0:T(8,128)(2,1)} %refs_3_.12, ...), custom_call_target="tpu_custom_call" | custom-call | flops 20000000000 | bytes 72000000 | tf_op jit(solution)/shard_map/products/pallas_call | solution.py:723
  321.4 4.6 %products.6 = (bf16[512,1024]{1,0:T(8,128)(2,1)}, bf16[512,1024]{1,0:T(8,128)(2,1)}) custom-call(bf16[2048,384]{1,0:T(8,128)(2,1)} %get-tuple-element.325.refs_7_.refs_0_, bf16[2048,384]{1,0:T(8,128)(2,1)} %get-tuple-element.326.refs_4_.refs_1_, bf16[1024,256]{1,0:T(8,128)(2,1)} %refs_2_.11, bf16[1024,256]{1,0:T(8,128)(2,1)} %refs_3_.12, ...), custom_call_target="tpu_custom_call" | custom-call | flops 20000000000 | bytes 72000000 | tf_op jit(solution)/shard_map/products/pallas_call | solution.py:723
  329.4 3.8 assemble.2
  339.3 5.2 %collective-permute-done.51 = bf16[128,384]{1,0:T(8,128)(2,1)S(1)} collective-permute-done((bf16[128,384]{1,0:T(8,128)(2,1)S(1)}, bf16[128,384]{1,0:T(8,128)(2,1)S(1)}, u32[]{:S(2)}, u32[]{:S(2)}) %collective-permute-start.51) | collective-permute-done | bytes 98336 | tf_op jit(solution)/shard_map/ppermute | solution.py:918
  347.0 2.4 collective-permute-done.55
  352.3 3.7 all-to-all-start.1
  359.7 5.5 %products.7 = (bf16[512,1024]{1,0:T(8,128)(2,1)}, bf16[512,1024]{1,0:T(8,128)(2,1)}) custom-call(bf16[2048,1024]{1,0:T(8,128)(2,1)} %get-tuple-element.344.refs_0_, bf16[1024,1024]{1,0:T(8,128)(2,1)} %refs_1_.3), custom_call_target="tpu_custom_call" | custom-call | tf_op jit(solution)/shard_map/products/pallas_call | solution.py:723
  365.4 4.9 %last_norm.1 = f32[512,1024]{1,0:T(8,128)} custom-call(bf16[512,1024]{1,0:T(8,128)(2,1)} %get-tuple-element.327.refs_0_, bf16[512,1024]{1,0:T(8,128)(2,1)} %collective-permute-done.56.refs_1_, bf16[512,1024]{1,0:T(8,128)(2,1)} %collective-permute-done.57.refs_2_, bf16[512,1024]{1,0:T(8,128)(2,1)} %refs_3_.13, f32[512,1024]{1,0:T(8,128)} %get-tuple-element.348.refs_4_, ...), custom_call_target="tpu_custom_call" | custom-call | flops 20000000000 | bytes 72000000 | tf_op jit(solution)/shard_map/last_norm/pallas_call | solution.py:516
  370.4 3.0 add_convert_fusion
  373.4 3.8 assemble.3
  377.2 2.4 place_half.2.refs_0_
  380.2 7.7 %collective-permute-done.61.v_ref = bf16[512,1024]{1,0:T(8,128)(2,1)} collective-permute-done((bf16[512,1024]{1,0:T(8,128)(2,1)S(1)}, bf16[512,1024]{1,0:T(8,128)(2,1)}, u32[]{:S(2)}, u32[]{:S(2)}) %collective-permute-start.61) | collective-permute-done | bytes 1048608 | tf_op jit(solution)/shard_map/ppermute | solution.py:918
  389.2 2.5 place_half.3
  (295 shorter events, 87.4 us)
Async XLA Ops:
  4.2 26.5 %collective-permute-start = (bf16[512,1024]{1,0:T(8,128)(2,1)}, bf16[512,1024]{1,0:T(8,128)(2,1)S(1)}, u32[]{:S(2)}, u32[]{:S(2)}) collective-permute-start(bf16[512,1024]{1,0:T(8,128)(2,1)} %first_norm.1.refs_0_.refs_3_), channel_id=1, source_target_pairs={{0,2},{1,3},{2,0},{3,1},{4,6},{5,7},{6,4},{7,5},{8,10},{9,11},{10,... | collective-permute-start | bytes 3145736 | tf_op jit(solution)/shard_map/ppermute | solution.py:918
  8.8 8.0 %collective-permute-start.2 = (bf16[512,1024]{1,0:T(8,128)(2,1)S(1)}, bf16[512,1024]{1,0:T(8,128)(2,1)S(1)}, u32[]{:S(2)}, u32[]{:S(2)}) collective-permute-start(bf16[512,1024]{1,0:T(8,128)(2,1)S(1)} %broadcast_select_fusion.refs_0_.refs_1_.refs_5_), channel_id=1, source_target_pairs={{0,1},{1,0},{2,3},{3,2},{4,5},{5,4},{6,7},{7,6},{8,9},{9,8},{10,11... | collective-permute-start | bytes 3145736 | tf_op jit(solution)/shard_map/ppermute | solution.py:918
  14.7 16.0 %collective-permute-start.3 = (bf16[256,1024]{1,0:T(8,128)(2,1)S(1)}, bf16[256,1024]{1,0:T(8,128)(2,1)S(1)}, u32[]{:S(2)}, u32[]{:S(2)}) collective-permute-start(bf16[256,1024]{1,0:T(8,128)(2,1)S(1)} %copy-done.15), channel_id=1, source_target_pairs={{0,1},{1,0},{2,3},{3,2},{4,5},{5,4},{6,7},{7,6},{8,9},{9,8},{10,11... | collective-permute-start | bytes 1572872 | tf_op jit(solution)/shard_map/ppermute | solution.py:918
  32.3 42.3 %collective-permute-start.11 = (bf16[768,1024]{1,0:T(8,128)(2,1)}, bf16[768,1024]{1,0:T(8,128)(2,1)}, u32[]{:S(2)}, u32[]{:S(2)}) collective-permute-start(bf16[768,1024]{1,0:T(8,128)(2,1)} %constant_dynamic-update-slice_fusion), channel_id=1, source_target_pairs={{0,2},{1,3},{2,0},{3,1},{4,6},{5,7},{6,4},{7,5},{8,10},{9,11},{10,... | collective-permute-start | bytes 4718600 | tf_op jit(solution)/shard_map/ppermute | solution.py:918
  54.2 16.0 %collective-permute-start.5 = (bf16[512,128]{1,0:T(8,128)(2,1)}, bf16[512,128]{1,0:T(8,128)(2,1)S(1)}, u32[]{:S(2)}, u32[]{:S(2)}) collective-permute-start(bf16[512,128]{1,0:T(8,128)(2,1)} %get-tuple-element.201), channel_id=1, source_target_pairs={{0,1},{1,0},{2,3},{3,2},{4,5},{5,4},{6,7},{7,6},{8,9},{9,8},{10,11... | collective-permute-start | bytes 393224 | tf_op jit(solution)/shard_map/ppermute | solution.py:918
  54.3 18.2 %collective-permute-start.6 = (bf16[512,128]{1,0:T(8,128)(2,1)}, bf16[512,128]{1,0:T(8,128)(2,1)S(1)}, u32[]{:S(2)}, u32[]{:S(2)}) collective-permute-start(bf16[512,128]{1,0:T(8,128)(2,1)} %get-tuple-element.202), channel_id=1, source_target_pairs={{0,2},{1,3},{2,0},{3,1},{4,6},{5,7},{6,4},{7,5},{8,10},{9,11},{10,... | collective-permute-start | bytes 393224 | tf_op jit(solution)/shard_map/ppermute | solution.py:918
  56.1 18.4 %collective-permute-start.7 = (bf16[512,128]{1,0:T(8,128)(2,1)}, bf16[512,128]{1,0:T(8,128)(2,1)S(1)}, u32[]{:S(2)}, u32[]{:S(2)}) collective-permute-start(bf16[512,128]{1,0:T(8,128)(2,1)} %get-tuple-element.203), channel_id=1, source_target_pairs={{0,3},{1,2},{2,1},{3,0},{4,7},{5,6},{6,5},{7,4},{8,11},{9,10},{10,... | collective-permute-start | bytes 393224 | tf_op jit(solution)/shard_map/ppermute | solution.py:918
  74.6 9.0 %collective-permute-start.12 = (bf16[768,1024]{1,0:T(8,128)(2,1)}, bf16[768,1024]{1,0:T(8,128)(2,1)S(1)}, u32[]{:S(2)}, u32[]{:S(2)}) collective-permute-start(bf16[768,1024]{1,0:T(8,128)(2,1)} %collective-permute-done.11.refs_10_.refs_0_.refs_3_.refs_11_), channel_id=1, source_target_pairs={{0,1},{1,0},{2,3},{3,2},{4,5},{5,4},{6,7},{7,6},{8,9},{9,8},{10,11... | collective-permute-start | bytes 4718600 | tf_op jit(solution)/shard_map/ppermute | solution.py:918
  76.4 7.2 %collective-permute-start.9 = (bf16[512,128]{1,0:T(8,128)(2,1)}, bf16[512,128]{1,0:T(8,128)(2,1)S(1)}, u32[]{:S(2)}, u32[]{:S(2)}) collective-permute-start(bf16[512,128]{1,0:T(8,128)(2,1)} %get-tuple-element.208), channel_id=1, source_target_pairs={{0,2},{1,3},{2,0},{3,1},{4,6},{5,7},{6,4},{7,5},{8,10},{9,11},{10,... | collective-permute-start | bytes 393224 | tf_op jit(solution)/shard_map/ppermute | solution.py:918
  91.0 25.8 %collective-permute-start.14 = (bf16[512,1024]{1,0:T(8,128)(2,1)}, bf16[512,1024]{1,0:T(8,128)(2,1)S(1)}, u32[]{:S(2)}, u32[]{:S(2)}) collective-permute-start(bf16[512,1024]{1,0:T(8,128)(2,1)} %get-tuple-element.214.refs_0_), channel_id=1, source_target_pairs={{0,2},{1,3},{2,0},{3,1},{4,6},{5,7},{6,4},{7,5},{8,10},{9,11},{10,... | collective-permute-start | bytes 3145736 | tf_op jit(solution)/shard_map/ppermute | solution.py:918
  149.6 13.9 %collective-permute-start.22 = (bf16[512,1024]{1,0:T(8,128)(2,1)}, bf16[512,1024]{1,0:T(8,128)(2,1)S(1)}, u32[]{:S(2)}, u32[]{:S(2)}) collective-permute-start(bf16[512,1024]{1,0:T(8,128)(2,1)} %get-tuple-element.229), channel_id=1, source_target_pairs={{0,1},{1,0},{2,3},{3,2},{4,5},{5,4},{6,7},{7,6},{8,9},{9,8},{10,11... | collective-permute-start | bytes 3145736 | tf_op jit(solution)/shard_map/ppermute | solution.py:918
  161.8 24.1 %collective-permute-start.23 = (bf16[512,1024]{1,0:T(8,128)(2,1)}, bf16[512,1024]{1,0:T(8,128)(2,1)S(1)}, u32[]{:S(2)}, u32[]{:S(2)}) collective-permute-start(bf16[512,1024]{1,0:T(8,128)(2,1)} %get-tuple-element.237), channel_id=1, source_target_pairs={{0,1},{1,0},{2,3},{3,2},{4,5},{5,4},{6,7},{7,6},{8,9},{9,8},{10,11... | collective-permute-start | bytes 3145736 | tf_op jit(solution)/shard_map/ppermute | solution.py:918
  163.9 25.4 %collective-permute-start.24 = (bf16[512,1024]{1,0:T(8,128)(2,1)S(1)}, bf16[512,1024]{1,0:T(8,128)(2,1)S(1)}, u32[]{:S(2)}, u32[]{:S(2)}) collective-permute-start(bf16[512,1024]{1,0:T(8,128)(2,1)S(1)} %add_convert_fusion.5), channel_id=1, source_target_pairs={{0,2},{1,3},{2,0},{3,1},{4,6},{5,7},{6,4},{7,5},{8,10},{9,11},{10,... | collective-permute-start | bytes 3145736 | tf_op jit(solution)/shard_map/ppermute | solution.py:918
  173.7 26.2 %collective-permute-start.25 = (bf16[512,1024]{1,0:T(8,128)(2,1)}, bf16[512,1024]{1,0:T(8,128)(2,1)S(1)}, u32[]{:S(2)}, u32[]{:S(2)}) collective-permute-start(bf16[512,1024]{1,0:T(8,128)(2,1)} %get-tuple-element.233), channel_id=1, source_target_pairs={{0,4},{4,0},{8,12},{12,8},{16,20},{20,16},{24,28},{28,24},{1,5},{5... | collective-permute-start | bytes 3145736 | tf_op jit(solution)/shard_map/ppermute | solution.py:918
  184.3 29.3 %collective-permute-start.29 = (bf16[512,1024]{1,0:T(8,128)(2,1)}, bf16[512,1024]{1,0:T(8,128)(2,1)S(1)}, u32[]{:S(2)}, u32[]{:S(2)}) collective-permute-start(bf16[512,1024]{1,0:T(8,128)(2,1)} %get-tuple-element.235), channel_id=1, source_target_pairs={{0,8},{4,12},{8,0},{12,4},{16,24},{20,28},{24,16},{28,20},{1,9},{5... | collective-permute-start | bytes 3145736 | tf_op jit(solution)/shard_map/ppermute | solution.py:918
  199.9 15.8 %collective-permute-start.32 = (bf16[512,256]{1,0:T(8,128)(2,1)}, bf16[512,256]{1,0:T(8,128)(2,1)S(1)}, u32[]{:S(2)}, u32[]{:S(2)}) collective-permute-start(bf16[512,256]{1,0:T(8,128)(2,1)} %get-tuple-element.265), channel_id=1, source_target_pairs={{0,2},{1,3},{2,0},{3,1},{4,6},{5,7},{6,4},{7,5},{8,10},{9,11},{10,... | collective-permute-start | bytes 786440 | tf_op jit(solution)/shard_map/ppermute | solution.py:918
  200.6 15.2 %collective-permute-start.28 = (bf16[512,256]{1,0:T(8,128)(2,1)}, bf16[512,256]{1,0:T(8,128)(2,1)S(1)}, u32[]{:S(2)}, u32[]{:S(2)}) collective-permute-start(bf16[512,256]{1,0:T(8,128)(2,1)} %get-tuple-element.250), channel_id=1, source_target_pairs={{0,3},{1,2},{2,1},{3,0},{4,7},{5,6},{6,5},{7,4},{8,11},{9,10},{10,... | collective-permute-start | bytes 786440 | tf_op jit(solution)/shard_map/ppermute | solution.py:918
  202.3 18.1 %collective-permute-start.31 = (bf16[256,1024]{1,0:T(8,128)(2,1)S(1)}, bf16[256,1024]{1,0:T(8,128)(2,1)S(1)}, u32[]{:S(2)}, u32[]{:S(2)}) collective-permute-start(bf16[256,1024]{1,0:T(8,128)(2,1)S(1)} %get-tuple-element.369), channel_id=1, source_target_pairs={{0,8},{4,12},{8,0},{12,4},{16,24},{20,28},{24,16},{28,20},{1,9},{5... | collective-permute-start | bytes 1572872 | tf_op jit(solution)/shard_map/ppermute | solution.py:918
  207.9 8.0 %collective-permute-start.27 = (bf16[2048,256]{1,0:T(8,128)(2,1)}, bf16[2048,256]{1,0:T(8,128)(2,1)S(1)}, u32[]{:S(2)}, u32[]{:S(2)}) collective-permute-start(bf16[2048,256]{1,0:T(8,128)(2,1)} %get-tuple-element.248), channel_id=1, source_target_pairs={{0,1},{1,0},{2,3},{3,2},{4,5},{5,4},{6,7},{7,6},{8,9},{9,8},{10,11... | collective-permute-start | bytes 3145736 | tf_op jit(solution)/shard_map/ppermute | solution.py:918
  214.2 23.6 %collective-permute-start.34 = (bf16[256,1024]{1,0:T(8,128)(2,1)S(1)}, bf16[256,1024]{1,0:T(8,128)(2,1)S(1)}, u32[]{:S(2)}, u32[]{:S(2)}) collective-permute-start(bf16[256,1024]{1,0:T(8,128)(2,1)S(1)} %get-tuple-element.367), channel_id=1, source_target_pairs={{0,4},{4,0},{8,12},{12,8},{16,20},{20,16},{24,28},{28,24},{1,5},{5... | collective-permute-start | bytes 1572872 | tf_op jit(solution)/shard_map/ppermute | solution.py:918
  215.8 25.2 %collective-permute-start.35 = (bf16[512,1024]{1,0:T(8,128)(2,1)S(1)}, bf16[512,1024]{1,0:T(8,128)(2,1)S(1)}, u32[]{:S(2)}, u32[]{:S(2)}) collective-permute-start(bf16[512,1024]{1,0:T(8,128)(2,1)S(1)} %copy-done.42), channel_id=1, source_target_pairs={{0,1},{1,0},{2,3},{3,2},{4,5},{5,4},{6,7},{7,6},{8,9},{9,8},{10,11... | collective-permute-start | bytes 3145736 | tf_op jit(solution)/shard_map/ppermute | solution.py:918
  220.7 16.9 %collective-permute-start.33 = (bf16[128,1024]{1,0:T(8,128)(2,1)S(1)}, bf16[128,1024]{1,0:T(8,128)(2,1)S(1)}, u32[]{:S(2)}, u32[]{:S(2)}) collective-permute-start(bf16[128,1024]{1,0:T(8,128)(2,1)S(1)} %get-tuple-element.381), channel_id=1, source_target_pairs={{0,16},{4,20},{8,24},{12,28},{16,0},{20,4},{24,8},{28,12},{1,17},{... | collective-permute-start | bytes 786440 | tf_op jit(solution)/shard_map/ppermute | solution.py:918
  223.3 32.8 %collective-permute-start.30 = (bf16[1024,256]{1,0:T(8,128)(2,1)}, bf16[1024,256]{1,0:T(8,128)(2,1)}, u32[]{:S(2)}, u32[]{:S(2)}) collective-permute-start(bf16[1024,256]{1,0:T(8,128)(2,1)} %add_convert_fusion.9), channel_id=1, source_target_pairs={{0,2},{1,3},{2,0},{3,1},{4,6},{5,7},{6,4},{7,5},{8,10},{9,11},{10,... | collective-permute-start | bytes 1572872 | tf_op jit(solution)/shard_map/ppermute | solution.py:918
  237.7 18.4 %collective-permute-start.36 = (bf16[128,1024]{1,0:T(8,128)(2,1)S(1)}, bf16[128,1024]{1,0:T(8,128)(2,1)S(1)}, u32[]{:S(2)}, u32[]{:S(2)}) collective-permute-start(bf16[128,1024]{1,0:T(8,128)(2,1)S(1)} %add_convert_fusion.13), channel_id=1, source_target_pairs={{0,16},{4,20},{8,24},{12,28},{16,0},{20,4},{24,8},{28,12},{1,17},{... | collective-permute-start | bytes 786440 | tf_op jit(solution)/shard_map/ppermute | solution.py:918
  238.0 25.6 %collective-permute-start.38 = (bf16[128,1024]{1,0:T(8,128)(2,1)S(1)}, bf16[128,1024]{1,0:T(8,128)(2,1)S(1)}, u32[]{:S(2)}, u32[]{:S(2)}) collective-permute-start(bf16[128,1024]{1,0:T(8,128)(2,1)S(1)} %get-tuple-element.377), channel_id=1, source_target_pairs={{0,16},{4,20},{8,24},{12,28},{16,0},{20,4},{24,8},{28,12},{1,17},{... | collective-permute-start | bytes 786440 | tf_op jit(solution)/shard_map/ppermute | solution.py:918
  242.4 55.7 %collective-permute-start.42 = (bf16[512,1024]{1,0:T(8,128)(2,1)}, bf16[512,1024]{1,0:T(8,128)(2,1)}, u32[]{:S(2)}, u32[]{:S(2)}) collective-permute-start(bf16[512,1024]{1,0:T(8,128)(2,1)} %add_convert_fusion.2), channel_id=1, source_target_pairs={{0,2},{1,3},{2,0},{3,1},{4,6},{5,7},{6,4},{7,5},{8,10},{9,11},{10,... | collective-permute-start | bytes 3145736 | tf_op jit(solution)/shard_map/ppermute | solution.py:918
  263.7 15.0 %collective-permute-start.39 = (bf16[128,1024]{1,0:T(8,128)(2,1)S(1)}, bf16[128,1024]{1,0:T(8,128)(2,1)S(1)}, u32[]{:S(2)}, u32[]{:S(2)}) collective-permute-start(bf16[128,1024]{1,0:T(8,128)(2,1)S(1)} %add_convert_fusion.12), channel_id=1, source_target_pairs={{0,16},{4,20},{8,24},{12,28},{16,0},{20,4},{24,8},{28,12},{1,17},{... | collective-permute-start | bytes 786440 | tf_op jit(solution)/shard_map/ppermute | solution.py:918
  263.8 19.4 %collective-permute-start.37 = (bf16[256,1024]{1,0:T(8,128)(2,1)S(1)}, bf16[256,1024]{1,0:T(8,128)(2,1)S(1)}, u32[]{:S(2)}, u32[]{:S(2)}) collective-permute-start(bf16[256,1024]{1,0:T(8,128)(2,1)S(1)} %pad_maximum_fusion.3), channel_id=1, source_target_pairs={{0,8},{4,12},{8,0},{12,4},{16,24},{20,28},{24,16},{28,20},{1,9},{5... | collective-permute-start | bytes 1572872 | tf_op jit(solution)/shard_map/ppermute | solution.py:918
  265.9 18.5 %collective-permute-start.40 = (bf16[512,640]{1,0:T(8,128)(2,1)}, bf16[512,640]{1,0:T(8,128)(2,1)S(1)}, u32[]{:S(2)}, u32[]{:S(2)}) collective-permute-start(bf16[512,640]{1,0:T(8,128)(2,1)} %get-tuple-element.286), channel_id=1, source_target_pairs={{0,4},{4,0},{8,12},{12,8},{16,20},{20,16},{24,28},{28,24},{1,5},{5... | collective-permute-start | bytes 1966088 | tf_op jit(solution)/shard_map/ppermute | solution.py:918
  278.8 20.6 %collective-permute-start.41 = (bf16[256,1024]{1,0:T(8,128)(2,1)S(1)}, bf16[256,1024]{1,0:T(8,128)(2,1)S(1)}, u32[]{:S(2)}, u32[]{:S(2)}) collective-permute-start(bf16[256,1024]{1,0:T(8,128)(2,1)S(1)} %pad_maximum_fusion.4), channel_id=1, source_target_pairs={{0,4},{4,0},{8,12},{12,8},{16,20},{20,16},{24,28},{28,24},{1,5},{5... | collective-permute-start | bytes 1572872 | tf_op jit(solution)/shard_map/ppermute | solution.py:918
  284.3 45.0 %collective-permute-start.49 = (bf16[512,1024]{1,0:T(8,128)(2,1)}, bf16[512,1024]{1,0:T(8,128)(2,1)}, u32[]{:S(2)}, u32[]{:S(2)}) collective-permute-start(bf16[512,1024]{1,0:T(8,128)(2,1)} %pad_maximum_fusion.refs_0_), channel_id=1, source_target_pairs={{0,4},{4,0},{8,12},{12,8},{16,20},{20,16},{24,28},{28,24},{1,5},{5... | collective-permute-start | bytes 3145736 | tf_op jit(solution)/shard_map/ppermute | solution.py:918
  284.6 13.4 %collective-permute-start.43 = (bf16[256,640]{1,0:T(8,128)(2,1)S(1)}, bf16[256,640]{1,0:T(8,128)(2,1)S(1)}, u32[]{:S(2)}, u32[]{:S(2)}) collective-permute-start(bf16[256,640]{1,0:T(8,128)(2,1)S(1)} %get-tuple-element.373), channel_id=1, source_target_pairs={{0,8},{4,12},{8,0},{12,4},{16,24},{20,28},{24,16},{28,20},{1,9},{5... | collective-permute-start | bytes 983048 | tf_op jit(solution)/shard_map/ppermute | solution.py:918
  298.2 11.3 %collective-permute-start.44 = (bf16[128,640]{1,0:T(8,128)(2,1)S(1)}, bf16[128,640]{1,0:T(8,128)(2,1)S(1)}, u32[]{:S(2)}, u32[]{:S(2)}) collective-permute-start(bf16[128,640]{1,0:T(8,128)(2,1)S(1)} %get-tuple-element.393), channel_id=1, source_target_pairs={{0,16},{4,20},{8,24},{12,28},{16,0},{20,4},{24,8},{28,12},{1,17},{... | collective-permute-start | bytes 491528 | tf_op jit(solution)/shard_map/ppermute | solution.py:918
  306.6 22.6 %collective-permute-start.47 = (bf16[512,384]{1,0:T(8,128)(2,1)}, bf16[512,384]{1,0:T(8,128)(2,1)S(1)}, u32[]{:S(2)}, u32[]{:S(2)}) collective-permute-start(bf16[512,384]{1,0:T(8,128)(2,1)} %get-tuple-element.315), channel_id=1, source_target_pairs={{0,4},{4,0},{8,12},{12,8},{16,20},{20,16},{24,28},{28,24},{1,5},{5... | collective-permute-start | bytes 1179656 | tf_op jit(solution)/shard_map/ppermute | solution.py:918
  310.2 9.0 %collective-permute-start.46 = (bf16[128,640]{1,0:T(8,128)(2,1)S(1)}, bf16[128,640]{1,0:T(8,128)(2,1)S(1)}, u32[]{:S(2)}, u32[]{:S(2)}) collective-permute-start(bf16[128,640]{1,0:T(8,128)(2,1)S(1)} %add_convert_fusion.14), channel_id=1, source_target_pairs={{0,16},{4,20},{8,24},{12,28},{16,0},{20,4},{24,8},{28,12},{1,17},{... | collective-permute-start | bytes 491528 | tf_op jit(solution)/shard_map/ppermute | solution.py:918
  310.8 36.2 %all-to-all-start = ((f32[4,8,1024]{2,1,0:T(8,128)}), f32[4,8,1024]{2,1,0:T(8,128)S(1)}, u32[]{:S(2)}, u32[]{:S(2)}) async-start(f32[4,8,1024]{2,1,0:T(8,128)} %broadcast_in_dim.96), calls=%async_computation | async-start | bytes 262144 | tf_op jit(solution)/shard_map/all_to_all | solution.py:1268
  318.8 7.3 %collective-permute-start.45 = (bf16[512,1024]{1,0:T(8,128)(2,1)}, bf16[512,1024]{1,0:T(8,128)(2,1)S(1)}, u32[]{:S(2)}, u32[]{:S(2)}) collective-permute-start(bf16[512,1024]{1,0:T(8,128)(2,1)} %get-tuple-element.322), channel_id=1, source_target_pairs={{0,1},{1,0},{2,3},{3,2},{4,5},{5,4},{6,7},{7,6},{8,9},{9,8},{10,11... | collective-permute-start | bytes 3145736 | tf_op jit(solution)/shard_map/ppermute | solution.py:918
  319.4 13.9 %collective-permute-start.48 = (bf16[256,640]{1,0:T(8,128)(2,1)S(1)}, bf16[256,640]{1,0:T(8,128)(2,1)S(1)}, u32[]{:S(2)}, u32[]{:S(2)}) collective-permute-start(bf16[256,640]{1,0:T(8,128)(2,1)S(1)} %pad_maximum_fusion.6), channel_id=1, source_target_pairs={{0,8},{4,12},{8,0},{12,4},{16,24},{20,28},{24,16},{28,20},{1,9},{5... | collective-permute-start | bytes 983048 | tf_op jit(solution)/shard_map/ppermute | solution.py:918
  326.1 39.3 %collective-permute-start.56 = (bf16[512,1024]{1,0:T(8,128)(2,1)}, bf16[512,1024]{1,0:T(8,128)(2,1)}, u32[]{:S(2)}, u32[]{:S(2)}) collective-permute-start(bf16[512,1024]{1,0:T(8,128)(2,1)} %get-tuple-element.346), channel_id=1, source_target_pairs={{0,1},{1,0},{2,3},{3,2},{4,5},{5,4},{6,7},{7,6},{8,9},{9,8},{10,11... | collective-permute-start | bytes 3145736 | tf_op jit(solution)/shard_map/ppermute | solution.py:918
  327.4 37.9 %collective-permute-start.57 = (bf16[512,1024]{1,0:T(8,128)(2,1)}, bf16[512,1024]{1,0:T(8,128)(2,1)}, u32[]{:S(2)}, u32[]{:S(2)}) collective-permute-start(bf16[512,1024]{1,0:T(8,128)(2,1)} %add_convert_fusion.1), channel_id=1, source_target_pairs={{0,2},{1,3},{2,0},{3,1},{4,6},{5,7},{6,4},{7,5},{8,10},{9,11},{10,... | collective-permute-start | bytes 3145736 | tf_op jit(solution)/shard_map/ppermute | solution.py:918
  333.7 10.8 %collective-permute-start.51 = (bf16[128,384]{1,0:T(8,128)(2,1)S(1)}, bf16[128,384]{1,0:T(8,128)(2,1)S(1)}, u32[]{:S(2)}, u32[]{:S(2)}) collective-permute-start(bf16[128,384]{1,0:T(8,128)(2,1)S(1)} %get-tuple-element.387), channel_id=1, source_target_pairs={{0,16},{4,20},{8,24},{12,28},{16,0},{20,4},{24,8},{28,12},{1,17},{... | collective-permute-start | bytes 294920 | tf_op jit(solution)/shard_map/ppermute | solution.py:918
  335.6 8.8 %collective-permute-start.52 = (bf16[128,384]{1,0:T(8,128)(2,1)S(1)}, bf16[128,384]{1,0:T(8,128)(2,1)S(1)}, u32[]{:S(2)}, u32[]{:S(2)}) collective-permute-start(bf16[128,384]{1,0:T(8,128)(2,1)S(1)} %get-tuple-element.388), channel_id=1, source_target_pairs={{0,24},{4,28},{8,16},{12,20},{16,8},{20,12},{24,0},{28,4},{1,25},{... | collective-permute-start | bytes 294920 | tf_op jit(solution)/shard_map/ppermute | solution.py:918
  339.3 26.0 %collective-permute-start.58 = (bf16[512,640]{1,0:T(8,128)(2,1)S(1)}, bf16[512,640]{1,0:T(8,128)(2,1)S(1)}, u32[]{:S(2)}, u32[]{:S(2)}) collective-permute-start(bf16[512,640]{1,0:T(8,128)(2,1)S(1)} %pad_maximum_fusion.2.refs_0_), channel_id=1, source_target_pairs={{0,4},{4,0},{8,12},{12,8},{16,20},{20,16},{24,28},{28,24},{1,5},{5... | collective-permute-start | bytes 1966088 | tf_op jit(solution)/shard_map/ppermute | solution.py:918
  346.2 9.8 %collective-permute-start.54 = (bf16[128,384]{1,0:T(8,128)(2,1)S(1)}, bf16[128,384]{1,0:T(8,128)(2,1)S(1)}, u32[]{:S(2)}, u32[]{:S(2)}) collective-permute-start(bf16[128,384]{1,0:T(8,128)(2,1)S(1)} %add_convert_fusion.15), channel_id=1, source_target_pairs={{0,16},{4,20},{8,24},{12,28},{16,0},{20,4},{24,8},{28,12},{1,17},{... | collective-permute-start | bytes 294920 | tf_op jit(solution)/shard_map/ppermute | solution.py:918
  349.4 8.7 %collective-permute-start.53 = (bf16[128,384]{1,0:T(8,128)(2,1)S(1)}, bf16[128,384]{1,0:T(8,128)(2,1)S(1)}, u32[]{:S(2)}, u32[]{:S(2)}) collective-permute-start(bf16[128,384]{1,0:T(8,128)(2,1)S(1)} %add_convert_fusion.15), channel_id=1, source_target_pairs={{0,24},{4,28},{8,16},{12,20},{16,8},{20,12},{24,0},{28,4},{1,25},{... | collective-permute-start | bytes 294920 | tf_op jit(solution)/shard_map/ppermute | solution.py:918
  352.3 21.1 %all-to-all-start.1 = ((f32[8,16,1024]{2,1,0:T(8,128)}), f32[8,16,1024]{2,1,0:T(8,128)S(1)}, u32[]{:S(2)}, u32[]{:S(2)}) async-start(f32[8,16,1024]{2,1,0:T(8,128)} %broadcast_in_dim.97), calls=%async_computation.1 | async-start | bytes 1048576 | tf_op jit(solution)/shard_map/all_to_all | solution.py:1292
  356.0 32.0 %collective-permute-start.61 = (bf16[512,1024]{1,0:T(8,128)(2,1)S(1)}, bf16[512,1024]{1,0:T(8,128)(2,1)}, u32[]{:S(2)}, u32[]{:S(2)}) collective-permute-start(bf16[512,1024]{1,0:T(8,128)(2,1)S(1)} %pad_maximum_fusion.1.v_ref), channel_id=1, source_target_pairs={{0,8},{4,12},{8,0},{12,4},{16,24},{20,28},{24,16},{28,20},{1,9},{5... | collective-permute-start | bytes 3145736 | tf_op jit(solution)/shard_map/ppermute | solution.py:918
  358.2 15.2 %collective-permute-start.60 = (bf16[512,384]{1,0:T(8,128)(2,1)S(1)}, bf16[512,384]{1,0:T(8,128)(2,1)}, u32[]{:S(2)}, u32[]{:S(2)}) collective-permute-start(bf16[512,384]{1,0:T(8,128)(2,1)S(1)} %pad_maximum_fusion.5.refs_1_), channel_id=1, source_target_pairs={{0,4},{4,0},{8,12},{12,8},{16,20},{20,16},{24,28},{28,24},{1,5},{5... | collective-permute-start | bytes 1179656 | tf_op jit(solution)/shard_map/ppermute | solution.py:918
  (75 other events, 501.8 us)
